TPU v7x, 128 devices: a whole 4x4x4 slice. The times are simulated.
128 devices in a mesh: ctx: 8 (over x, core), tp: 16 (over y, z).
Axes of the slice: x: 4, y: 4, z: 4, core: 2. Of those that a mesh axis runs over, the one named last changes fastest.
Arguments:
- mamba_in: bfloat16 [8192, 16384], P(('ctx', 'tp')), may hold values from -6 to 6
- state_in_b: float32 [8192, 16], P('ctx'), may hold values from -6 to 6
- state_out_c: float32 [8192, 16], P('ctx'), may hold values from -1.5 to 1.5
- step_decay: float32 [8192, 256], P('ctx', 'tp'), may hold values from -1 to 0, as said below
- skip_gain: float32 [256], P('tp'), may hold values from 0.5 to 1.5
- queries: bfloat16 [8192, 8192], P(('ctx', 'tp')), may hold values from -6 to 6
- keys: bfloat16 [8192, 1024], P(('ctx', 'tp')), may hold values from -6 to 6
- values: bfloat16 [8192, 1024], P(('ctx', 'tp')), may hold values from -6 to 6
- doc_ids: int32 [64], replicated, may hold values from 0 to 3, never falling along the last dimension, each value on 1 to 40 neighbouring positions
Outputs:
- mamba_out: bfloat16 [8192, 16384], P(('ctx', 'tp'))
- attn_out: bfloat16 [8192, 8192], P(('ctx', 'tp'))
Inputs may be any that keep to these rules, and one draw needn't show every extreme that they name: `step_decay`: strictly negative.
All inputs are finite; a program needn't handle non-finite values.
Results may differ from a plain program's by a relative error of at most 0.008.
Values may be sent and summed in bfloat16 or wider, within the bound.
No kernel may reach another device: no remote copies, remote signals or barrier semaphores. Data moves between devices by JAX's collectives and lax.ppermute only.
A program may use at most 128 MiB of HBM per device.

v0:
```python
import jax
import jax.numpy as jnp
from jax import lax
from jax.sharding import PartitionSpec as P

NS = 16
QH = 64
KVH = 8
HD = 128
P_SIZE = 64
SPAN = 128
BLK = 128


NEG_FILL = -1e30
HIGHEST = lax.Precision.HIGHEST


def carried_in(array, axis, combine, identity):
    devices, place = (lax.axis_size(axis), lax.axis_index(axis))
    everything = jax.tree.map(
        lambda part, kind: lax.all_gather(part.astype(kind), axis),
        array,
        (jnp.bfloat16, jnp.bfloat16),
    )
    start = jax.tree.map(
        lambda part, zero: jnp.broadcast_to(jnp.asarray(zero, part.dtype), part.shape),
        array,
        identity,
    )

    def turn(k, before):
        reached = k < place
        new = combine(
            before, jax.tree.map(lambda part, own: part[k].astype(own.dtype), everything, array)
        )
        return jax.tree.map(lambda a, b: jnp.where(reached, a, b), new, before)

    return lax.fori_loop(0, devices, turn, start)


def ssd_blocks(inputs, decay, state_in_b, state_out_c, initial, span_len):
    row_count, head_count, head_width = inputs.shape
    span_count = row_count // span_len
    inject = jnp.sqrt(-jnp.expm1(2.0 * decay))
    driven = (inputs * inject[:, :, None]).reshape(span_count, span_len, head_count, head_width)
    running = jnp.cumsum(decay.reshape(span_count, span_len, head_count), axis=1)
    b_blocks = state_in_b.reshape(span_count, span_len, -1)
    c_blocks = state_out_c.reshape(span_count, span_len, -1)
    causal_tri = jnp.tril(jnp.ones((span_len, span_len), dtype=bool))

    def advance(state_now, members):
        driven_c, running_c, b_span, c_span = members
        spread = running_c[:, None, :] - running_c[None, :, :]
        within = jnp.exp(jnp.where(causal_tri[:, :, None], spread, NEG_FILL))
        intersection = jnp.dot(c_span, b_span.T, precision=HIGHEST)
        inside = jnp.einsum(
            "tsh,shp->thp", within * intersection[:, :, None], driven_c, precision=HIGHEST
        )
        entering = (
            jnp.einsum("tn,hpn->thp", c_span, state_now, precision=HIGHEST)
            * jnp.exp(running_c)[:, :, None]
        )
        remain = jnp.exp(running_c[-1][None, :] - running_c)
        state_next = state_now * jnp.exp(running_c[-1])[:, None, None] + jnp.einsum(
            "shp,sn->hpn", driven_c * remain[:, :, None], b_span, precision=HIGHEST
        )
        return (state_next, inside + entering)

    final_state, outputs = lax.scan(advance, initial, (driven, running, b_blocks, c_blocks))
    return (outputs.reshape(row_count, head_count, head_width), final_state)


def attend_block(states, key_block, value_block, key_pos, key_doc, query_sets, score_scale):
    updated = []
    for state_now, query_set in zip(states, query_sets):
        query_rows, query_pos, query_doc = query_set
        visible = (query_doc[:, None] == key_doc[None, :]) & (
            query_pos[:, None] >= key_pos[None, :]
        )

        def update(state_in):
            row_max, row_sum, accum = state_in
            scores = (
                jnp.einsum("rhd,kd->hrk", query_rows, key_block, preferred_element_type=jnp.float32)
                * score_scale
            )
            scores = jnp.where(visible[None], scores, NEG_FILL)
            new_max = jnp.maximum(row_max, jnp.max(scores, axis=-1))
            terms = jnp.where(visible[None], jnp.exp(scores - new_max[:, :, None]), 0.0)
            fade = jnp.exp(row_max - new_max)
            new_sum = row_sum * fade + jnp.sum(terms, axis=-1)
            weights = terms.astype(jnp.bfloat16)
            added = jnp.einsum(
                "hrk,kd->rhd", weights, value_block, preferred_element_type=jnp.float32
            )
            return (new_max, new_sum, accum * fade.T[:, :, None] + added)

        updated.append(lax.cond(jnp.any(visible), update, lambda state_in: state_in, state_now))
    return tuple(updated)


def per_device(
    mamba_in, state_in_b, state_out_c, step_decay, skip_gain, queries, keys, values, doc_ids
):
    ctx_rank = lax.axis_index("ctx")
    tp_rank = lax.axis_index("tp")
    mixed, query_cols = (
        lax.all_to_all(mamba_in, "tp", split_axis=1, concat_axis=0, tiled=True),
        lax.all_to_all(queries, "tp", split_axis=1, concat_axis=0, tiled=True),
    )
    row_count = mixed.shape[0]
    heads_here = query_cols.shape[1] // HD
    group_size = QH // KVH
    full_keys, full_values = (
        lax.all_gather(keys, "tp", axis=0, tiled=True),
        lax.all_gather(values, "tp", axis=0, tiled=True),
    )
    first_col = tp_rank * heads_here // group_size * HD
    key_head = lax.dynamic_slice_in_dim(full_keys, first_col, HD, 1)
    value_head = lax.dynamic_slice_in_dim(full_values, first_col, HD, 1)
    groups_here = step_decay.shape[1]
    inputs = mixed.astype(jnp.float32).reshape(row_count, groups_here, P_SIZE)
    zero_state = jnp.zeros((groups_here, P_SIZE, NS), jnp.float32)
    outputs, local_end = ssd_blocks(inputs, step_decay, state_in_b, state_out_c, zero_state, SPAN)
    through = jnp.cumsum(step_decay, axis=0)
    totals = through[-1]

    def combine(earlier, later):
        return (earlier[0] * jnp.exp(later[1])[:, None, None] + later[0], earlier[1] + later[1])

    incoming, _ = carried_in(
        (local_end, totals), "ctx", combine, (zero_state, jnp.zeros_like(totals))
    )
    carried = (
        jnp.einsum("tn,hpn->thp", state_out_c, incoming, precision=HIGHEST)
        * jnp.exp(through)[:, :, None]
    )
    mamba_rows = (
        (outputs + carried + skip_gain[None, :, None] * inputs)
        .reshape(row_count, -1)
        .astype(jnp.bfloat16)
    )
    score_scale = HD ** (-0.5)
    half_rows = row_count // 2
    query_heads = query_cols.reshape(row_count, heads_here, HD)
    lead_rows = query_heads[:half_rows]
    tail_rows = query_heads[half_rows:]
    own_first = ctx_rank * row_count
    tail_first = own_first + half_rows
    lead_pos = own_first + jnp.arange(half_rows, dtype=jnp.int32)
    tail_pos = tail_first + jnp.arange(half_rows, dtype=jnp.int32)
    query_sets = (
        (lead_rows, lead_pos, doc_ids[lead_pos // BLK]),
        (tail_rows, tail_pos, doc_ids[tail_pos // BLK]),
    )
    blank = (
        jnp.full((heads_here, half_rows), NEG_FILL, jnp.float32),
        jnp.zeros((heads_here, half_rows), jnp.float32),
        jnp.zeros((half_rows, heads_here, HD), jnp.float32),
    )
    key_part = lax.all_gather(key_head, "ctx", axis=0, tiled=True)
    value_part = lax.all_gather(value_head, "ctx", axis=0, tiled=True)
    key_rows = key_part.shape[0]
    block_len = 512
    block_total = key_rows // block_len
    key_blocks = key_part.reshape(block_total, block_len, HD)
    value_blocks = value_part.reshape(block_total, block_len, HD)

    def visit(state_in, members):
        key_block, value_block, block_index = members
        key_pos = block_index * block_len + jnp.arange(block_len, dtype=jnp.int32)
        key_doc = doc_ids[key_pos // BLK]
        return (
            attend_block(
                state_in, key_block, value_block, key_pos, key_doc, query_sets, score_scale
            ),
            None,
        )

    result, _ = lax.scan(
        visit, (blank, blank), (key_blocks, value_blocks, jnp.arange(block_total, dtype=jnp.int32))
    )
    lead_state, tail_state = result

    def finish(state_in):
        return (state_in[2] / state_in[1].T[:, :, None]).reshape(half_rows, -1).astype(jnp.bfloat16)

    lead_out = finish(lead_state)
    tail_out = finish(tail_state)
    attn_rows = jnp.concatenate([lead_out, tail_out], axis=0)
    mamba_out, attn_out = (
        lax.all_to_all(mamba_rows, "tp", split_axis=0, concat_axis=1, tiled=True),
        lax.all_to_all(attn_rows, "tp", split_axis=0, concat_axis=1, tiled=True),
    )
    return (mamba_out, attn_out)


def solution(mesh):
    in_specs = (
        P(("ctx", "tp"), None),
        P("ctx", None),
        P("ctx", None),
        P("ctx", "tp"),
        P("tp"),
        P(("ctx", "tp"), None),
        P(("ctx", "tp"), None),
        P(("ctx", "tp"), None),
        P(),
    )
    out_specs = (P(("ctx", "tp"), None), P(("ctx", "tp"), None))
    return jax.shard_map(
        per_device, mesh=mesh, in_specs=in_specs, out_specs=out_specs, check_vma=False
    )
```

profile of v0, /device:TPU:4, one launch (start us, length us, event | category | flops | bytes accessed | tf_op | source)
XLA Modules:
  0.0 1361.8 jit_solution(5781053253116142585)
XLA Ops:
  11.0 8.0 all-to-all-start.2
  19.1 43.3 %all-gather.7.cloned.1.call-done = bf16[1024,1024]{1,0:T(8,128)(2,1)} async-done(((bf16[64,1024]{1,0:T(8,128)(2,1)}), bf16[1024,1024]{1,0:T(8,128)(2,1)}) %all-gather.7.cloned.1.call-update) | async-done | bytes 2097168 | tf_op jit(solution)/shard_map/all_gather | solution.py:116
  64.1 4.5 reduce-window.6
  69.3 8.3 all-gather.1
  80.7 5.1 all-to-all-start
  86.5 23.3 %fusion.85 = f32[8,128,16]{2,0,1:T(8,128)S(1)} fusion(f32[8,128,16]{2,0,1:T(8,128)S(1)} %copy.68), kind=kOutput, calls=%fused_computation.321 | output fusion | flops 2080768 | bytes 131072 | tf_op jit(solution)/shard_map/jit(cumsum)/reduce_window_sum | solution.py:47
  113.9 4.5 compare_select_fusion.12
  118.4 4.5 compare_select_fusion.18
  124.3 35.7 %select_select_fusion.1 = s32[512]{0:T(512)S(1)} fusion(pred[512]{0:T(512)(128)(4,1)S(1)} %get-tuple-element.923, pred[512]{0:T(512)(128)(4,1)S(1)} %get-tuple-element.924, pred[512]{0:T(512)(128)(4,1)S(1)} %get-tuple-element.925, pred[512]{0:T(512)(128)(4,1)S(1)} %get-tuple-element.926, pred[512]{0:T(512)(128)(4,1)S(1)} %get-tuple-element.927, ...), kind=kLoop, calls=%fused_computation.303 | loop fusion | flops 29184 | bytes 33508 | tf_op jit(solution)/shard_map/gather | solution.py:155
  160.0 35.7 %select_select_fusion.2 = s32[512]{0:T(512)S(1)} fusion(pred[512]{0:T(512)(128)(4,1)S(1)} %get-tuple-element.867, pred[512]{0:T(512)(128)(4,1)S(1)} %get-tuple-element.868, pred[512]{0:T(512)(128)(4,1)S(1)} %get-tuple-element.869, pred[512]{0:T(512)(128)(4,1)S(1)} %get-tuple-element.870, pred[512]{0:T(512)(128)(4,1)S(1)} %get-tuple-element.871, ...), kind=kLoop, calls=%fused_computation.304 | loop fusion | flops 29184 | bytes 33508 | tf_op jit(solution)/shard_map/gather | solution.py:154
  200.3 7.2 reshape.328
  207.5 8.0 broadcast_multiply_fusion
  215.5 7.1 copy.72
  224.3 172.1 %while.51 = (s32[]{:T(128)}, f32[16,64,16]{1,2,0:T(8,128)S(1)}, f32[8,128,16,64]{1,0,3,2:T(8,128)}, f32[8,128,16]{1,2,0:T(8,128)S(1)}, f32[8,128,16,64]{1,3,2,0:...) while((s32[]{:T(128)}, f32[16,64,16]{1,2,0:T(8,128)S(1)}, ...), condition=%wide.region_2.3_spmd.clone, body=%wide.region_1.2_spmd.clone.sunk | while | flops 256067584 | bytes 4171280 | solution.py:70
  229.0 14.3 %dynamic_update_slice.6 = f32[8,128,16,64]{1,0,3,2:T(8,128)} dynamic-update-slice(f32[8,128,16,64]{1,0,3,2:T(8,128)} %get-tuple-element.1456, f32[1,128,16,64]{1,0,3,2:T(1,128)S(1)} %bitcast.469, s32[]{:T(128)} %get-tuple-element.1454, s32[]{:T(128)} %constant.166.clone.1..sunk, s32[]{:T(128)} %constant.166.clone.1..sunk, s32[]{:T(128)} %constant.166.clone.1..sunk) | dynamic-update-slice | bytes 1048580 | tf_op jit(solution)/shard_map/while/body/jit(dynamic_update_index_in_dim)/dynamic_update_slice | solution.py:70
  250.5 14.2 %dynamic_update_slice.6 = f32[8,128,16,64]{1,0,3,2:T(8,128)} dynamic-update-slice(f32[8,128,16,64]{1,0,3,2:T(8,128)} %get-tuple-element.1456, f32[1,128,16,64]{1,0,3,2:T(1,128)S(1)} %bitcast.469, s32[]{:T(128)} %get-tuple-element.1454, s32[]{:T(128)} %constant.166.clone.1..sunk, s32[]{:T(128)} %constant.166.clone.1..sunk, s32[]{:T(128)} %constant.166.clone.1..sunk) | dynamic-update-slice | bytes 1048580 | tf_op jit(solution)/shard_map/while/body/jit(dynamic_update_index_in_dim)/dynamic_update_slice | solution.py:70
  272.0 14.2 %dynamic_update_slice.6 = f32[8,128,16,64]{1,0,3,2:T(8,128)} dynamic-update-slice(f32[8,128,16,64]{1,0,3,2:T(8,128)} %get-tuple-element.1456, f32[1,128,16,64]{1,0,3,2:T(1,128)S(1)} %bitcast.469, s32[]{:T(128)} %get-tuple-element.1454, s32[]{:T(128)} %constant.166.clone.1..sunk, s32[]{:T(128)} %constant.166.clone.1..sunk, s32[]{:T(128)} %constant.166.clone.1..sunk) | dynamic-update-slice | bytes 1048580 | tf_op jit(solution)/shard_map/while/body/jit(dynamic_update_index_in_dim)/dynamic_update_slice | solution.py:70
  293.5 14.2 %dynamic_update_slice.6 = f32[8,128,16,64]{1,0,3,2:T(8,128)} dynamic-update-slice(f32[8,128,16,64]{1,0,3,2:T(8,128)} %get-tuple-element.1456, f32[1,128,16,64]{1,0,3,2:T(1,128)S(1)} %bitcast.469, s32[]{:T(128)} %get-tuple-element.1454, s32[]{:T(128)} %constant.166.clone.1..sunk, s32[]{:T(128)} %constant.166.clone.1..sunk, s32[]{:T(128)} %constant.166.clone.1..sunk) | dynamic-update-slice | bytes 1048580 | tf_op jit(solution)/shard_map/while/body/jit(dynamic_update_index_in_dim)/dynamic_update_slice | solution.py:70
  315.0 14.2 %dynamic_update_slice.6 = f32[8,128,16,64]{1,0,3,2:T(8,128)} dynamic-update-slice(f32[8,128,16,64]{1,0,3,2:T(8,128)} %get-tuple-element.1456, f32[1,128,16,64]{1,0,3,2:T(1,128)S(1)} %bitcast.469, s32[]{:T(128)} %get-tuple-element.1454, s32[]{:T(128)} %constant.166.clone.1..sunk, s32[]{:T(128)} %constant.166.clone.1..sunk, s32[]{:T(128)} %constant.166.clone.1..sunk) | dynamic-update-slice | bytes 1048580 | tf_op jit(solution)/shard_map/while/body/jit(dynamic_update_index_in_dim)/dynamic_update_slice | solution.py:70
  336.5 14.2 %dynamic_update_slice.6 = f32[8,128,16,64]{1,0,3,2:T(8,128)} dynamic-update-slice(f32[8,128,16,64]{1,0,3,2:T(8,128)} %get-tuple-element.1456, f32[1,128,16,64]{1,0,3,2:T(1,128)S(1)} %bitcast.469, s32[]{:T(128)} %get-tuple-element.1454, s32[]{:T(128)} %constant.166.clone.1..sunk, s32[]{:T(128)} %constant.166.clone.1..sunk, s32[]{:T(128)} %constant.166.clone.1..sunk) | dynamic-update-slice | bytes 1048580 | tf_op jit(solution)/shard_map/while/body/jit(dynamic_update_index_in_dim)/dynamic_update_slice | solution.py:70
  358.0 14.2 %dynamic_update_slice.6 = f32[8,128,16,64]{1,0,3,2:T(8,128)} dynamic-update-slice(f32[8,128,16,64]{1,0,3,2:T(8,128)} %get-tuple-element.1456, f32[1,128,16,64]{1,0,3,2:T(1,128)S(1)} %bitcast.469, s32[]{:T(128)} %get-tuple-element.1454, s32[]{:T(128)} %constant.166.clone.1..sunk, s32[]{:T(128)} %constant.166.clone.1..sunk, s32[]{:T(128)} %constant.166.clone.1..sunk) | dynamic-update-slice | bytes 1048580 | tf_op jit(solution)/shard_map/while/body/jit(dynamic_update_index_in_dim)/dynamic_update_slice | solution.py:70
  379.5 14.2 %dynamic_update_slice.6 = f32[8,128,16,64]{1,0,3,2:T(8,128)} dynamic-update-slice(f32[8,128,16,64]{1,0,3,2:T(8,128)} %get-tuple-element.1456, f32[1,128,16,64]{1,0,3,2:T(1,128)S(1)} %bitcast.469, s32[]{:T(128)} %get-tuple-element.1454, s32[]{:T(128)} %constant.166.clone.1..sunk, s32[]{:T(128)} %constant.166.clone.1..sunk, s32[]{:T(128)} %constant.166.clone.1..sunk) | dynamic-update-slice | bytes 1048580 | tf_op jit(solution)/shard_map/while/body/jit(dynamic_update_index_in_dim)/dynamic_update_slice | solution.py:70
  396.4 7.2 reshape.329
  403.7 4.9 reshape.322
  408.6 6.8 copy.79
  415.4 13.7 %all-gather = bf16[128,64,16]{1,2,0:T(8,128)(2,1)S(1)} all-gather(bf16[16,64,16]{1,2,0:T(8,128)(2,1)S(1)} %convert_element_type.84), channel_id=2, replica_groups=mesh['ctx'=8,'tp'=16] {'ctx'}, dimensions={0}, use_global_device_ids=true | all-gather | bytes 294912 | tf_op jit(solution)/shard_map/all_gather | solution.py:22
  430.2 7.3 fusion.70
  437.5 6.4 reshape.1101
  443.9 5.4 copy.93
  449.3 7.2 all-to-all-start.1
  457.7 870.6 %while.50 = (s32[]{:T(128)}, f32[4,512]{1,0:T(4,128)S(1)}, f32[4,512]{1,0:T(4,128)S(1)}, f32[512,4,128]{2,0,1:T(8,128)S(1)}, f32[4,512]{1,0:T(4,128)S(1)}, /*ind...) while((s32[]{:T(128)}, f32[4,512]{1,0:T(4,128)S(1)}, ...), condition=%wide.region_18.19_spmd.clone, body=%wide.region_7.18_spmd.clone.sunk | while | flops 1104520704 | bytes 33900856 | solution.py:181
  460.3 4.4 compare_select_fusion.31
  467.3 35.8 %select_select_fusion.4 = s32[512]{0:T(512)S(1)} fusion(pred[512]{0:T(512)(128)(4,1)S(1)} %get-tuple-element.1283, pred[512]{0:T(512)(128)(4,1)S(1)} %get-tuple-element.1284, pred[512]{0:T(512)(128)(4,1)S(1)} %get-tuple-element.1285, pred[512]{0:T(512)(128)(4,1)S(1)} %get-tuple-element.1286, pred[512]{0:T(512)(128)(4,1)S(1)} %get-tuple-element.1287, ...), kind=kLoop, calls=%fused_computation.116.clone.1 | loop fusion | flops 29184 | bytes 33508 | tf_op jit(solution)/shard_map/while/body/eval_jaxpr/gather | solution.py:173
  505.8 5.7 conditional.7
  518.4 4.4 compare_select_fusion.31
  525.4 35.8 %select_select_fusion.4 = s32[512]{0:T(512)S(1)} fusion(pred[512]{0:T(512)(128)(4,1)S(1)} %get-tuple-element.1283, pred[512]{0:T(512)(128)(4,1)S(1)} %get-tuple-element.1284, pred[512]{0:T(512)(128)(4,1)S(1)} %get-tuple-element.1285, pred[512]{0:T(512)(128)(4,1)S(1)} %get-tuple-element.1286, pred[512]{0:T(512)(128)(4,1)S(1)} %get-tuple-element.1287, ...), kind=kLoop, calls=%fused_computation.116.clone.1 | loop fusion | flops 29184 | bytes 33508 | tf_op jit(solution)/shard_map/while/body/eval_jaxpr/gather | solution.py:173
  564.0 5.7 conditional.7
  576.5 4.4 compare_select_fusion.31
  583.6 35.8 %select_select_fusion.4 = s32[512]{0:T(512)S(1)} fusion(pred[512]{0:T(512)(128)(4,1)S(1)} %get-tuple-element.1283, pred[512]{0:T(512)(128)(4,1)S(1)} %get-tuple-element.1284, pred[512]{0:T(512)(128)(4,1)S(1)} %get-tuple-element.1285, pred[512]{0:T(512)(128)(4,1)S(1)} %get-tuple-element.1286, pred[512]{0:T(512)(128)(4,1)S(1)} %get-tuple-element.1287, ...), kind=kLoop, calls=%fused_computation.116.clone.1 | loop fusion | flops 29184 | bytes 33508 | tf_op jit(solution)/shard_map/while/body/eval_jaxpr/gather | solution.py:173
  622.1 5.7 conditional.7
  634.7 4.4 compare_select_fusion.31
  641.7 35.8 %select_select_fusion.4 = s32[512]{0:T(512)S(1)} fusion(pred[512]{0:T(512)(128)(4,1)S(1)} %get-tuple-element.1283, pred[512]{0:T(512)(128)(4,1)S(1)} %get-tuple-element.1284, pred[512]{0:T(512)(128)(4,1)S(1)} %get-tuple-element.1285, pred[512]{0:T(512)(128)(4,1)S(1)} %get-tuple-element.1286, pred[512]{0:T(512)(128)(4,1)S(1)} %get-tuple-element.1287, ...), kind=kLoop, calls=%fused_computation.116.clone.1 | loop fusion | flops 29184 | bytes 33508 | tf_op jit(solution)/shard_map/while/body/eval_jaxpr/gather | solution.py:173
  680.2 5.7 conditional.7
  692.8 4.4 compare_select_fusion.31
  699.8 35.8 %select_select_fusion.4 = s32[512]{0:T(512)S(1)} fusion(pred[512]{0:T(512)(128)(4,1)S(1)} %get-tuple-element.1283, pred[512]{0:T(512)(128)(4,1)S(1)} %get-tuple-element.1284, pred[512]{0:T(512)(128)(4,1)S(1)} %get-tuple-element.1285, pred[512]{0:T(512)(128)(4,1)S(1)} %get-tuple-element.1286, pred[512]{0:T(512)(128)(4,1)S(1)} %get-tuple-element.1287, ...), kind=kLoop, calls=%fused_computation.116.clone.1 | loop fusion | flops 29184 | bytes 33508 | tf_op jit(solution)/shard_map/while/body/eval_jaxpr/gather | solution.py:173
  738.4 5.7 conditional.7
  758.0 35.8 %select_select_fusion.4 = s32[512]{0:T(512)S(1)} fusion(pred[512]{0:T(512)(128)(4,1)S(1)} %get-tuple-element.1283, pred[512]{0:T(512)(128)(4,1)S(1)} %get-tuple-element.1284, pred[512]{0:T(512)(128)(4,1)S(1)} %get-tuple-element.1285, pred[512]{0:T(512)(128)(4,1)S(1)} %get-tuple-element.1286, pred[512]{0:T(512)(128)(4,1)S(1)} %get-tuple-element.1287, ...), kind=kLoop, calls=%fused_computation.116.clone.1 | loop fusion | flops 29184 | bytes 33508 | tf_op jit(solution)/shard_map/while/body/eval_jaxpr/gather | solution.py:173
  796.5 5.7 conditional.7
  816.1 35.8 %select_select_fusion.4 = s32[512]{0:T(512)S(1)} fusion(pred[512]{0:T(512)(128)(4,1)S(1)} %get-tuple-element.1283, pred[512]{0:T(512)(128)(4,1)S(1)} %get-tuple-element.1284, pred[512]{0:T(512)(128)(4,1)S(1)} %get-tuple-element.1285, pred[512]{0:T(512)(128)(4,1)S(1)} %get-tuple-element.1286, pred[512]{0:T(512)(128)(4,1)S(1)} %get-tuple-element.1287, ...), kind=kLoop, calls=%fused_computation.116.clone.1 | loop fusion | flops 29184 | bytes 33508 | tf_op jit(solution)/shard_map/while/body/eval_jaxpr/gather | solution.py:173
  854.6 5.7 conditional.7
  874.2 35.8 %select_select_fusion.4 = s32[512]{0:T(512)S(1)} fusion(pred[512]{0:T(512)(128)(4,1)S(1)} %get-tuple-element.1283, pred[512]{0:T(512)(128)(4,1)S(1)} %get-tuple-element.1284, pred[512]{0:T(512)(128)(4,1)S(1)} %get-tuple-element.1285, pred[512]{0:T(512)(128)(4,1)S(1)} %get-tuple-element.1286, pred[512]{0:T(512)(128)(4,1)S(1)} %get-tuple-element.1287, ...), kind=kLoop, calls=%fused_computation.116.clone.1 | loop fusion | flops 29184 | bytes 33508 | tf_op jit(solution)/shard_map/while/body/eval_jaxpr/gather | solution.py:173
  912.8 5.7 conditional.7
  932.4 35.8 %select_select_fusion.4 = s32[512]{0:T(512)S(1)} fusion(pred[512]{0:T(512)(128)(4,1)S(1)} %get-tuple-element.1283, pred[512]{0:T(512)(128)(4,1)S(1)} %get-tuple-element.1284, pred[512]{0:T(512)(128)(4,1)S(1)} %get-tuple-element.1285, pred[512]{0:T(512)(128)(4,1)S(1)} %get-tuple-element.1286, pred[512]{0:T(512)(128)(4,1)S(1)} %get-tuple-element.1287, ...), kind=kLoop, calls=%fused_computation.116.clone.1 | loop fusion | flops 29184 | bytes 33508 | tf_op jit(solution)/shard_map/while/body/eval_jaxpr/gather | solution.py:173
  970.9 5.7 conditional.7
  990.5 35.8 %select_select_fusion.4 = s32[512]{0:T(512)S(1)} fusion(pred[512]{0:T(512)(128)(4,1)S(1)} %get-tuple-element.1283, pred[512]{0:T(512)(128)(4,1)S(1)} %get-tuple-element.1284, pred[512]{0:T(512)(128)(4,1)S(1)} %get-tuple-element.1285, pred[512]{0:T(512)(128)(4,1)S(1)} %get-tuple-element.1286, pred[512]{0:T(512)(128)(4,1)S(1)} %get-tuple-element.1287, ...), kind=kLoop, calls=%fused_computation.116.clone.1 | loop fusion | flops 29184 | bytes 33508 | tf_op jit(solution)/shard_map/while/body/eval_jaxpr/gather | solution.py:173
  1029.0 5.7 conditional.7
  1045.0 35.8 %select_select_fusion.4 = s32[512]{0:T(512)S(1)} fusion(pred[512]{0:T(512)(128)(4,1)S(1)} %get-tuple-element.1283, pred[512]{0:T(512)(128)(4,1)S(1)} %get-tuple-element.1284, pred[512]{0:T(512)(128)(4,1)S(1)} %get-tuple-element.1285, pred[512]{0:T(512)(128)(4,1)S(1)} %get-tuple-element.1286, pred[512]{0:T(512)(128)(4,1)S(1)} %get-tuple-element.1287, ...), kind=kLoop, calls=%fused_computation.116.clone.1 | loop fusion | flops 29184 | bytes 33508 | tf_op jit(solution)/shard_map/while/body/eval_jaxpr/gather | solution.py:173
  1093.8 35.8 %select_select_fusion.4 = s32[512]{0:T(512)S(1)} fusion(pred[512]{0:T(512)(128)(4,1)S(1)} %get-tuple-element.1283, pred[512]{0:T(512)(128)(4,1)S(1)} %get-tuple-element.1284, pred[512]{0:T(512)(128)(4,1)S(1)} %get-tuple-element.1285, pred[512]{0:T(512)(128)(4,1)S(1)} %get-tuple-element.1286, pred[512]{0:T(512)(128)(4,1)S(1)} %get-tuple-element.1287, ...), kind=kLoop, calls=%fused_computation.116.clone.1 | loop fusion | flops 29184 | bytes 33508 | tf_op jit(solution)/shard_map/while/body/eval_jaxpr/gather | solution.py:173
  1142.6 35.8 %select_select_fusion.4 = s32[512]{0:T(512)S(1)} fusion(pred[512]{0:T(512)(128)(4,1)S(1)} %get-tuple-element.1283, pred[512]{0:T(512)(128)(4,1)S(1)} %get-tuple-element.1284, pred[512]{0:T(512)(128)(4,1)S(1)} %get-tuple-element.1285, pred[512]{0:T(512)(128)(4,1)S(1)} %get-tuple-element.1286, pred[512]{0:T(512)(128)(4,1)S(1)} %get-tuple-element.1287, ...), kind=kLoop, calls=%fused_computation.116.clone.1 | loop fusion | flops 29184 | bytes 33508 | tf_op jit(solution)/shard_map/while/body/eval_jaxpr/gather | solution.py:173
  1191.4 35.8 %select_select_fusion.4 = s32[512]{0:T(512)S(1)} fusion(pred[512]{0:T(512)(128)(4,1)S(1)} %get-tuple-element.1283, pred[512]{0:T(512)(128)(4,1)S(1)} %get-tuple-element.1284, pred[512]{0:T(512)(128)(4,1)S(1)} %get-tuple-element.1285, pred[512]{0:T(512)(128)(4,1)S(1)} %get-tuple-element.1286, pred[512]{0:T(512)(128)(4,1)S(1)} %get-tuple-element.1287, ...), kind=kLoop, calls=%fused_computation.116.clone.1 | loop fusion | flops 29184 | bytes 33508 | tf_op jit(solution)/shard_map/while/body/eval_jaxpr/gather | solution.py:173
  1240.3 35.8 %select_select_fusion.4 = s32[512]{0:T(512)S(1)} fusion(pred[512]{0:T(512)(128)(4,1)S(1)} %get-tuple-element.1283, pred[512]{0:T(512)(128)(4,1)S(1)} %get-tuple-element.1284, pred[512]{0:T(512)(128)(4,1)S(1)} %get-tuple-element.1285, pred[512]{0:T(512)(128)(4,1)S(1)} %get-tuple-element.1286, pred[512]{0:T(512)(128)(4,1)S(1)} %get-tuple-element.1287, ...), kind=kLoop, calls=%fused_computation.116.clone.1 | loop fusion | flops 29184 | bytes 33508 | tf_op jit(solution)/shard_map/while/body/eval_jaxpr/gather | solution.py:173
  1289.1 35.8 %select_select_fusion.4 = s32[512]{0:T(512)S(1)} fusion(pred[512]{0:T(512)(128)(4,1)S(1)} %get-tuple-element.1283, pred[512]{0:T(512)(128)(4,1)S(1)} %get-tuple-element.1284, pred[512]{0:T(512)(128)(4,1)S(1)} %get-tuple-element.1285, pred[512]{0:T(512)(128)(4,1)S(1)} %get-tuple-element.1286, pred[512]{0:T(512)(128)(4,1)S(1)} %get-tuple-element.1287, ...), kind=kLoop, calls=%fused_computation.116.clone.1 | loop fusion | flops 29184 | bytes 33508 | tf_op jit(solution)/shard_map/while/body/eval_jaxpr/gather | solution.py:173
  1334.1 7.2 all-to-all-start.3
  1344.5 9.8 all-to-all-done.3
  (984 shorter events, 369.9 us)
Async XLA Ops:
  7.2 56.9 %copy-start.2 = (f32[1024,16]{0,1:T(8,128)S(1)}, f32[1024,16]{0,1:T(8,128)}, u32[]{:S(2)}) copy-start(f32[1024,16]{0,1:T(8,128)} %param.22) | copy-start | bytes 196612
  7.2 55.2 %all-gather.7.cloned.1.call-start = ((), (), s32[]{:S(2)}) async-start(), calls=%async_computation.4 | async-start | bytes 2228224 | tf_op jit(solution)/shard_map/all_gather | solution.py:116
  7.9 214.7 %all-gather.11.cloned.1.call-start = ((), (), s32[]{:S(2)}) async-start(), calls=%async_computation.6 | async-start | bytes 2228224 | tf_op jit(solution)/shard_map/all_gather | solution.py:117
  11.0 69.8 %all-to-all-start.2 = ((bf16[64,16,512]{2,0,1:T(8,128)(2,1)}), bf16[64,16,512]{2,0,1:T(8,128)(2,1)S(1)}, u32[]{:S(2)}, u32[]{:S(2)}) async-start(bf16[64,16,512]{2,0,1:T(8,128)(2,1)} %bitcast.303), calls=%async_computation.2 | async-start | bytes 2097152 | tf_op jit(solution)/shard_map/all_to_all | solution.py:110
  19.0 437.5 %all-gather.9.cloned.1.call-start = ((), (), s32[]{:S(2)}) async-start(), calls=%async_computation.5 | async-start | bytes 2359296 | tf_op jit(solution)/shard_map/all_gather | solution.py:162
  80.7 29.2 %copy-start.3 = (f32[1024,16]{0,1:T(8,128)S(1)}, f32[1024,16]{0,1:T(8,128)}, u32[]{:S(2)}) copy-start(f32[1024,16]{0,1:T(8,128)} %param.20) | copy-start | bytes 196612
  80.7 29.3 %copy-start.1 = (f32[1024,16]{0,1:T(8,128)S(1)}, f32[1024,16]{0,1:T(8,128)}, u32[]{:S(2)}) copy-start(f32[1024,16]{0,1:T(8,128)} %param.21) | copy-start | bytes 196612
  80.7 31.7 %copy-start = (s32[64]{0:T(128)S(1)}, s32[64]{0:T(128)}, u32[]{:S(2)}) copy-start(s32[64]{0:T(128)} %param.27) | copy-start | bytes 772
  80.7 115.5 %all-to-all-start = ((bf16[64,16,1024]{2,0,1:T(8,128)(2,1)}), bf16[64,16,1024]{2,0,1:T(8,128)(2,1)}, u32[]{:S(2)}, u32[]{:S(2)}) async-start(bf16[64,16,1024]{2,0,1:T(8,128)(2,1)} %bitcast.302), calls=%async_computation | async-start | bytes 4194304 | tf_op jit(solution)/shard_map/all_to_all | solution.py:109
  85.9 370.6 %all-gather.13.cloned.1.call-start = ((), (), s32[]{:S(2)}) async-start(), calls=%async_computation.7 | async-start | bytes 2359296 | tf_op jit(solution)/shard_map/all_gather | solution.py:163
  408.6 21.6 %copy-start.4 = (f32[16]{0:T(128)S(1)}, f32[16]{0:T(128)}, u32[]{:S(2)}) copy-start(f32[16]{0:T(128)} %param.23) | copy-start | bytes 196
  449.3 884.8 %all-to-all-start.1 = ((bf16[16,64,1024]{2,1,0:T(8,128)(2,1)}), bf16[16,64,1024]{2,1,0:T(8,128)(2,1)}, u32[]{:S(2)}, u32[]{:S(2)}) async-start(bf16[16,64,1024]{2,1,0:T(8,128)(2,1)} %copy.93), calls=%async_computation.1 | async-start | bytes 4194304 | tf_op jit(solution)/shard_map/all_to_all | solution.py:193
  1334.1 20.1 %all-to-all-start.3 = ((bf16[16,64,512]{2,1,0:T(8,128)(2,1)}), bf16[16,64,512]{2,1,0:T(8,128)(2,1)S(1)}, u32[]{:S(2)}, u32[]{:S(2)}) async-start(bf16[16,64,512]{2,1,0:T(8,128)(2,1)} %bitcast.95), calls=%async_computation.3 | async-start | bytes 2097152 | tf_op jit(solution)/shard_map/all_to_all | solution.py:194
Sparse Core Ops, SparseCore 0:
  10.1 52.1 all-gather.6
  64.5 59.4 all-gather.10
  125.7 23.9 all-gather.8
  224.5 25.6 all-gather.12
where the time goes:
time: 1380 us; the launch traced here: 1360 us
  other arithmetic  825 us (60%)
  local copies, waits for them, and re-layouts  255 us (18%)
  matrix products  131 us (9%)
  waiting for transfers between devices  54.5 us (4%)
  loops' own time  32.6 us (2%)
  starting transfers between devices  27.7 us (2%)
  blocking collectives  22 us (2%)
  between operations  14.3 us (1%)
    gather x496, other arithmetic, visit(): key_doc = doc_ids[key_pos // BLK]  660 us
    dynamic_update_slice x8, local copies, waits for them, and re-layouts, ssd_blocks(): lax.scan(advance, initial, (driven, running, b_blocks, c_blocks))  114 us
    dot_general x19, matrix products, update(): jnp.einsum('hrk,kd->rhd', weights, value_block, preferred_element_type=jn...  51.7 us
    gather x64, local copies, waits for them, and re-layouts, visit(): key_doc = doc_ids[key_pos // BLK]  45.7 us
    all_gather x1, waiting for transfers between devices, per_device(): lax.all_gather(keys, 'tp', axis=0, tiled=True)  43.3 us
    gather x31, other arithmetic, per_device(): doc_ids[lead_pos // BLK]  41.3 us
    gather x31, other arithmetic, per_device(): doc_ids[tail_pos // BLK]  41.3 us
    another operation x1, loops' own time, per_device(): lax.scan(visit, (blank, blank), (key_blocks, value_blocks, jnp.arange(blo...  30.8 us
  transfers between devices with their start and end apart: 8, of which 2 were waited for; matrix products, arithmetic and copies ran while one was open for 89% of the time, Pallas kernels for 0%

commit v1 on v0

v1 whole, which is shorter than its diff:
```python
import math

import jax
import jax.numpy as jnp
from jax import lax
from jax.experimental import pallas as pl
from jax.experimental.pallas import tpu as pltpu
from jax.sharding import Mesh, PartitionSpec as P

NS = 16
KVH = 8
HD = 128
HM = 256
CHUNK = 64
NEG = -1e30
SCORE_EXP2 = HD**-0.5 * math.log2(math.e)
HIGHEST = lax.Precision.HIGHEST
F32 = jnp.float32
BF16 = jnp.bfloat16
ALL = ("x", "core", "y", "zh", "zl")
CTX = ("x", "core")
TP = ("y", "zh", "zl")
HEADS = ("x", "zh")
SHARE = ("core", "y", "zl")
VMEM = pl.BlockSpec(memory_space=pltpu.VMEM)
SMEM = pl.BlockSpec(memory_space=pltpu.SMEM)
TK = 1024
NG = 2
RG = 512 // NG


def dot(a, b, dims=((1,), (0,)), precision=None):
    return lax.dot_general(
        a, b, (dims, ((), ())), precision=precision, preferred_element_type=F32
    )


def params(mib):
    return pltpu.CompilerParams(vmem_limit_bytes=mib * 1024 * 1024)


def attn_kernel(meta_ref, q_ref, kv_ref, o_ref, m_ref, acc_ref, s_ref, vt_ref):
    def key_tile(j, low):
        x, core = j // 2, j % 2
        parts = [
            kv_ref[core, y, zl, x, zh, :, low : low + HD]
            for y in range(4)
            for zh in range(2)
            for zl in range(2)
        ]
        return jnp.concatenate(parts, axis=0)

    @pl.loop(0, vt_ref.shape[0])
    def _(j):
        vt_ref[j, :HD, :] = key_tile(j, HD).T
        vt_ref[j, HD:, :] = jnp.ones((16, TK), BF16)

    def scores(i, j, slot):
        k = key_tile(j, 0)
        for g in range(NG):
            s_ref[slot, g] = dot(k, q_ref[i, g * RG : (g + 1) * RG, :], ((1,), (1,)))

    def absorb(i, j, slot, masked):
        v = vt_ref[j]
        if masked:
            kpos = j * TK + lax.broadcasted_iota(jnp.int32, (TK, RG), 0)
            qpos = meta_ref[0, i] + lax.broadcasted_iota(jnp.int32, (TK, RG), 1) % CHUNK
            visible = (kpos <= qpos) & (kpos >= meta_ref[1, i])
        for g in range(NG):
            s = s_ref[slot, g]
            if masked:
                s = jnp.where(visible, s, NEG)
            before = m_ref[g]
            top = jnp.maximum(before, jnp.max(s, axis=0, keepdims=True))
            p = jnp.exp2((s - top) * SCORE_EXP2)
            fade = jnp.exp2((before - top) * SCORE_EXP2)
            m_ref[g] = top
            acc_ref[g] = acc_ref[g] * fade + dot(v, p.astype(BF16))

    def reset():
        m_ref[...] = jnp.full_like(m_ref, NEG)
        acc_ref[...] = jnp.zeros_like(acc_ref)

    def body(carry):
        i, j, slot = carry
        first = meta_ref[1, i]
        last = j == meta_ref[0, i] // TK
        i_next = jnp.where(last, i + 1, i)
        i_read = jnp.minimum(i_next, 7)
        j_next = jnp.where(last, meta_ref[1, i_read] // TK, j + 1)
        edge = last | (j * TK < first)

        @pl.when(edge)
        def _():
            scores(i_read, j_next, 1 - slot)
            absorb(i, j, slot, True)

        @pl.when(jnp.logical_not(edge))
        def _():
            scores(i_read, j_next, 1 - slot)
            absorb(i, j, slot, False)

        @pl.when(last)
        def _():
            for g in range(NG):
                out = (acc_ref[g, :HD] * (1.0 / acc_ref[g, HD : HD + 1])).T
                o_ref[i, g * RG : (g + 1) * RG] = out.astype(BF16)
            reset()

        return (i_next, j_next, 1 - slot)

    reset()
    scores(0, meta_ref[1, 0] // TK, 0)
    lax.while_loop(
        lambda carry: carry[0] < 8, body, (jnp.int32(0), meta_ref[1, 0] // TK, jnp.int32(0))
    )


def attend(meta, q, kv):
    return pl.pallas_call(
        attn_kernel,
        out_shape=jax.ShapeDtypeStruct((8, 512, HD), BF16),
        in_specs=[SMEM, VMEM, VMEM],
        out_specs=VMEM,
        scratch_shapes=[
            pltpu.VMEM((NG, 1, RG), F32),
            pltpu.VMEM((NG, HD + 16, RG), F32),
            pltpu.VMEM((2, NG, TK, RG), F32),
            pltpu.VMEM((8192 // TK, HD + 16, TK), BF16),
        ],
        compiler_params=params(40),
        cost_estimate=pl.CostEstimate(
            flops=4 * 512 * HD * 20000, bytes_accessed=6 << 20, transcendentals=10_000_000
        ),
    )(meta, q, kv)


def one_minus_exp(u):
    small = -u * (
        1
        + u / 2 * (1 + u / 3 * (1 + u / 4 * (1 + u / 5 * (1 + u / 6 * (1 + u / 7 * (1 + u / 8))))))
    )
    return jnp.where(u > -0.5, small, 1 - jnp.exp(u))


def spread(columns, heads, lanes=CHUNK):
    rows = columns.shape[0]
    left = lax.broadcasted_iota(jnp.int32, (rows, 2 * lanes), 1) < lanes
    parts = []
    for h in range(0, heads, 2):
        a = jnp.broadcast_to(columns[:, h : h + 1], (rows, 2 * lanes))
        b = jnp.broadcast_to(columns[:, h + 1 : h + 2], (rows, 2 * lanes))
        parts.append(jnp.where(left, a, b))
    return jnp.concatenate(parts, axis=1)


def running_decay(decay):
    row = lax.broadcasted_iota(jnp.int32, (CHUNK, CHUNK), 0)
    col = lax.broadcasted_iota(jnp.int32, (CHUNK, CHUNK), 1)
    tri = jnp.where(row >= col, 1.0, 0.0).astype(F32)
    return dot(tri, decay, precision=HIGHEST)


def state_kernel(x_ref, dec_ref, b_ref, s_ref, f_ref, e_ref):
    decay = dec_ref[...].T[:CHUNK]
    run = running_decay(decay)
    drive = jnp.exp(-run) * jnp.sqrt(one_minus_exp(2.0 * decay))
    end = jnp.exp(run[CHUNK - 1 :])
    for k in range(16):
        f_ref[k, :, :16] = drive[:, 16 * k : 16 * k + 16]
        e_ref[k, :, :16] = jnp.broadcast_to(end[:, 16 * k : 16 * k + 16], (16, 16))
    b = b_ref[...]
    b_high = b.astype(BF16)
    b_low = (b - b_high.astype(F32)).astype(BF16)
    b_two = jnp.concatenate([b_high, b_low], axis=1)

    @pl.loop(0, 16)
    def _(k):
        cols = pl.ds(pl.multiple_of(k * 1024, 1024), 1024)
        z = (x_ref[:, cols].astype(F32) * spread(f_ref[k], 16)).astype(BF16)
        two = dot(b_two, z, ((0,), (0,)))
        s_ref[k] = ((two[:NS] + two[NS:]) * spread(e_ref[k], 16)).astype(BF16)


def chunk_states(x, dec, b):
    return pl.pallas_call(
        state_kernel,
        out_shape=jax.ShapeDtypeStruct((16, NS, 1024), BF16),
        in_specs=[VMEM] * 3,
        out_specs=VMEM,
        scratch_shapes=[pltpu.VMEM((16, CHUNK, 128), F32), pltpu.VMEM((16, 16, 128), F32)],
        compiler_params=params(16),
        cost_estimate=pl.CostEstimate(
            flops=2 * 32 * CHUNK * 16384, bytes_accessed=3 << 20, transcendentals=50_000
        ),
    )(x, dec, b)


def output_kernel(x_ref, dec_ref, b_ref, c_ref, e_ref, y_ref, f_ref, r_ref, g_ref):
    both = dec_ref[...].T
    decay = both[:CHUNK]
    run = running_decay(decay)
    drive = jnp.exp(-run) * jnp.sqrt(one_minus_exp(2.0 * decay))
    reach = jnp.exp(run)
    gain = jnp.broadcast_to(both[CHUNK : CHUNK + 1], (8, HM))
    for k in range(16):
        f_ref[k, :, :16] = drive[:, 16 * k : 16 * k + 16]
        r_ref[k, :, :16] = reach[:, 16 * k : 16 * k + 16]
        g_ref[k, :, :16] = gain[:, 16 * k : 16 * k + 16]
    row = lax.broadcasted_iota(jnp.int32, (CHUNK, CHUNK), 0)
    col = lax.broadcasted_iota(jnp.int32, (CHUNK, CHUNK), 1)
    inner = jnp.where(row >= col, dot(c_ref[...], b_ref[...], ((1,), (1,)), HIGHEST), 0.0)
    weights = jnp.concatenate([inner, c_ref[...]], axis=1).astype(BF16)

    @pl.loop(0, 16)
    def _(k):
        cols = pl.ds(pl.multiple_of(k * 1024, 1024), 1024)
        x = x_ref[:, cols].astype(F32)
        z = (x * spread(f_ref[k], 16)).astype(BF16)
        y = dot(weights, jnp.concatenate([z, e_ref[k]], axis=0))
        y = y * spread(r_ref[k], 16) + spread(g_ref[k], 16)[:1] * x
        y_ref[:, cols] = y.astype(BF16)


def chunk_outputs(x, dec, b, c, entering):
    return pl.pallas_call(
        output_kernel,
        out_shape=jax.ShapeDtypeStruct((CHUNK, 16384), BF16),
        in_specs=[VMEM] * 5,
        out_specs=VMEM,
        scratch_shapes=[
            pltpu.VMEM((16, CHUNK, 128), F32),
            pltpu.VMEM((16, CHUNK, 128), F32),
            pltpu.VMEM((16, 8, 128), F32),
        ],
        compiler_params=params(24),
        cost_estimate=pl.CostEstimate(
            flops=2 * 80 * CHUNK * 16384, bytes_accessed=5 << 20, transcendentals=50_000
        ),
    )(x, dec, b, c, entering)


def chunk_decays(own_ref, d_ref):
    token = lax.broadcasted_iota(jnp.int32, (1024, 16), 0)
    chunk = lax.broadcasted_iota(jnp.int32, (1024, 16), 1)
    pick = jnp.where(token // CHUNK == chunk, 1.0, 0.0).astype(F32)
    total = dot(pick, own_ref[...], ((0,), (1,)), HIGHEST)
    d_ref[...] = spread(jnp.exp(total), 16)
    return spread(jnp.exp(jnp.sum(total, axis=0, keepdims=True)), 16)


def ends_kernel(s_ref, own_ref, end_ref, d_ref):
    through = chunk_decays(own_ref, d_ref)
    state = jnp.zeros((NS, 1024), F32)
    for k in range(16):
        state = state * d_ref[k : k + 1] + s_ref[k].astype(F32)
    high = through.astype(BF16).astype(F32)
    row = lax.broadcasted_iota(jnp.int32, (16, 1024), 0)
    tail = jnp.where(row == 0, high, jnp.where(row == 1, through - high, 0.0))
    end_ref[...] = jnp.concatenate([state, tail], axis=0).astype(BF16)


def local_ends(states, own):
    return pl.pallas_call(
        ends_kernel,
        out_shape=jax.ShapeDtypeStruct((32, 1024), BF16),
        in_specs=[VMEM] * 2,
        out_specs=VMEM,
        scratch_shapes=[pltpu.VMEM((16, 1024), F32)],
        compiler_params=params(8),
    )(states, own)


def enter_kernel(place_ref, s_ref, own_ref, ends_ref, e_ref, d_ref):
    chunk_decays(own_ref, d_ref)
    place = place_ref[0]
    state = jnp.zeros((NS, 1024), F32)
    for c in range(7):
        through = (ends_ref[c, 16:17].astype(F32) + ends_ref[c, 17:18].astype(F32))
        later = state * through + ends_ref[c, :16].astype(F32)
        state = jnp.where(c < place, later, state)
    for k in range(16):
        e_ref[k] = state.astype(BF16)
        state = state * d_ref[k : k + 1] + s_ref[k].astype(F32)


def entering_states(place, states, own, ends):
    return pl.pallas_call(
        enter_kernel,
        out_shape=jax.ShapeDtypeStruct((16, NS, 1024), BF16),
        in_specs=[SMEM, VMEM, VMEM, VMEM],
        out_specs=VMEM,
        scratch_shapes=[pltpu.VMEM((16, 1024), F32)],
        compiler_params=params(8),
    )(place, states, own, ends)


def per_device(
    mamba_in, state_in_b, state_out_c, step_decay, skip_gain, queries, keys, values, doc_ids
):
    core, y, zl = lax.axis_index("core"), lax.axis_index("y"), lax.axis_index("zl")
    ctx, tp = lax.axis_index(CTX), lax.axis_index(TP)

    kv = jnp.concatenate([keys.reshape(CHUNK, KVH, HD), values.reshape(CHUNK, KVH, HD)], axis=2)
    kv = lax.all_to_all(kv.transpose(1, 0, 2), HEADS, 0, 0, tiled=True)
    kv = lax.all_gather(kv, SHARE).reshape(2, 4, 2, 4, 2, CHUNK, 2 * HD)

    own = step_decay.T
    dec = own.reshape(16, 16, CHUNK).transpose(1, 0, 2)
    gain = jnp.broadcast_to(skip_gain[None, :, None], (16, 16, CHUNK))
    dec = lax.all_to_all(jnp.concatenate([dec, gain], axis=2), TP, 0, 0, tiled=True)
    dec = dec.reshape(HM, 2 * CHUNK)
    b = lax.dynamic_slice_in_dim(state_in_b, tp * CHUNK, CHUNK, 0)
    c = lax.dynamic_slice_in_dim(state_out_c, tp * CHUNK, CHUNK, 0)

    states = chunk_states(mamba_in, dec, b)
    states = lax.all_to_all(states, TP, 0, 0, tiled=True)
    ends = lax.all_gather(local_ends(states, own), CTX)
    entering = entering_states(ctx.reshape(1).astype(jnp.int32), states, own, ends)
    entering = lax.all_to_all(entering, TP, 0, 0, tiled=True)
    mamba_out = chunk_outputs(mamba_in, dec, b, c, entering)

    q = queries.reshape(CHUNK, KVH, 8, HD).transpose(1, 2, 0, 3)
    q = lax.all_to_all(q, HEADS, 0, 0, tiled=True).reshape(8, 512, HD)
    source = jnp.arange(8, dtype=jnp.int32)
    place = (2 * (source // 2) + core) * 1024 + (4 * y + 2 * (source % 2) + zl) * CHUNK
    block = jnp.arange(64, dtype=jnp.int32)
    doc = jnp.sum(jnp.where(block[None] == place[:, None] // 128, doc_ids[None], 0), axis=1)
    first = jnp.sum((doc_ids[None] < doc[:, None]).astype(jnp.int32), axis=1) * 128
    attn = attend(jnp.stack([place, first]).astype(jnp.int32), q, kv)
    attn = lax.all_to_all(attn.reshape(8, 8, CHUNK, HD), HEADS, 0, 0, tiled=True)
    attn_out = attn.transpose(2, 0, 1, 3).reshape(CHUNK, -1)
    return (mamba_out, attn_out)


def solution(mesh):
    inner = Mesh(mesh.devices.reshape(4, 2, 4, 2, 2), ALL)
    in_specs = (
        P(ALL, None),
        P(CTX, None),
        P(CTX, None),
        P(CTX, TP),
        P(TP),
        P(ALL, None),
        P(ALL, None),
        P(ALL, None),
        P(),
    )
    out_specs = (P(ALL, None), P(ALL, None))
    return jax.shard_map(
        per_device, mesh=inner, in_specs=in_specs, out_specs=out_specs, check_vma=False
    )
```

time: 1380 us -> 158 us (0.11)
  the two profiles are of different devices: /device:TPU:4 before, /device:TPU:1 now
where the time goes in v1:
time: 158 us
  Pallas kernels  47.3 us (30%)
  blocking collectives  39.2 us (25%)
  starting transfers between devices  23.7 us (15%)
  waiting for transfers between devices  18.9 us (12%)
  between operations  14.2 us (9%)
  local copies, waits for them, and re-layouts  13.2 us (8%)
    pallas_call x1, Pallas kernels, attend(): pl.pallas_call(attn_kernel, out_shape=jax.ShapeDtypeStruct((8, 512, HD),...  29.1 us
    all_gather x1, blocking collectives, per_device(): ends = lax.all_gather(local_ends(states, own), CTX)  23.7 us
    all_to_all x1, blocking collectives, per_device(): kv = lax.all_to_all(kv.transpose(1, 0, 2), HEADS, 0, 0, tiled=True)  15.5 us
    all_to_all x1, waiting for transfers between devices, per_device(): states = lax.all_to_all(states, TP, 0, 0, tiled=True)  9.96 us
    pallas_call x1, Pallas kernels, chunk_outputs(): pl.pallas_call(output_kernel, out_shape=jax.ShapeDtypeStruct((CHUNK, 1638...  8.93 us
    unnamed x20, local copies, waits for them, and re-layouts  8.55 us
    pallas_call x1, Pallas kernels, chunk_states(): pl.pallas_call(state_kernel, out_shape=jax.ShapeDtypeStruct((16, NS, 1024...  7.37 us
    all_to_all x1, waiting for transfers between devices, per_device(): lax.all_to_all(jnp.concatenate([dec, gain], axis=2), TP, 0, 0, tiled=True)  6.58 us
  transfers between devices with their start and end apart: 6, of which 3 were waited for; matrix products, arithmetic and copies ran while one was open for 4% of the time, Pallas kernels for 30%

profile of v1, /device:TPU:1, one launch (start us, length us, event | category | flops | bytes accessed | tf_op | source)
XLA Modules:
  0.0 157.6 jit_solution(9052843720968721097)
XLA Ops:
  7.2 0.0 copy-start
  7.2 0.0 copy-start.3
  7.2 0.0 copy-start.5
  7.2 0.0 copy-start.1
  7.2 0.0 all-gather.4.cloned.1.call-start
  7.3 1.1 copy.44
  8.3 0.9 copy.45
  9.4 15.5 %all_to_all.30 = bf16[8,64,256]{2,1,0:T(8,128)(2,1)} all-to-all(bf16[8,64,256]{2,1,0:T(8,128)(2,1)S(1)} %copy.39), channel_id=1, replica_groups=mesh['x'=4,'core'=2,'y'=4,'zh'=2,'zl'=2] {'x','zh'}, dimensions={0} | all-to-all | bytes 524288 | tf_op jit(solution)/shard_map/all_to_all | solution.py:305
  24.9 0.0 all-gather.4.cloned.1.call-update
  24.9 0.0 copy-done.3
  24.9 0.1 reshape.180
  25.0 0.0 copy-done.5
  25.0 0.1 broadcast_in_dim.8
  25.1 0.8 pad_maximum_fusion
  25.9 5.2 %all-to-all-start = ((f32[16,16,128]{2,1,0:T(8,128)}), f32[16,16,128]{2,1,0:T(8,128)S(1)}, u32[]{:S(2)}, u32[]{:S(2)}) async-start(f32[16,16,128]{2,1,0:T(8,128)} %pad_maximum_fusion), calls=%async_computation | async-start | bytes 262144 | tf_op jit(solution)/shard_map/all_to_all | solution.py:311
  31.1 0.0 copy-done
  31.2 0.1 constant_dynamic-slice_fusion.1
  31.2 0.1 copy.41.b_ref
  31.3 6.6 %all-to-all-done = f32[16,16,128]{2,1,0:T(8,128)S(1)} async-done(((f32[16,16,128]{2,1,0:T(8,128)}), f32[16,16,128]{2,1,0:T(8,128)S(1)}, u32[]{:S(2)}, u32[]{:S(2)}) %all-to-all-start) | async-done | bytes 131104 | tf_op jit(solution)/shard_map/all_to_all | solution.py:311
  37.9 0.0 copy-done.1
  37.9 7.4 %shard_map.104 = bf16[16,16,1024]{2,1,0:T(8,128)(2,1)} custom-call(bf16[64,16384]{1,0:T(8,128)(2,1)S(1)} %copy-done.1, f32[256,128]{1,0:T(8,128)S(1)} %bitcast.31, f32[64,16]{1,0:T(8,128)S(1)} %copy.41.b_ref), custom_call_target="tpu_custom_call" | custom-call | flops 67108864 | bytes 3145728 | tf_op jit(solution)/shard_map/pallas_call | solution.py:186
  45.3 3.6 %all-to-all-start.1 = ((bf16[16,16,1024]{2,1,0:T(8,128)(2,1)}), bf16[16,16,1024]{2,1,0:T(8,128)(2,1)S(1)}, u32[]{:S(2)}, u32[]{:S(2)}) async-start(bf16[16,16,1024]{2,1,0:T(8,128)(2,1)} %shard_map.104), calls=%async_computation.1 | async-start | bytes 1048576 | tf_op jit(solution)/shard_map/all_to_all | solution.py:317
  48.9 1.5 copy.43
  50.4 0.0 copy-start.6
  50.4 1.6 %copy.51 = bf16[64,8,8,128]{3,0,2,1:T(8,128)(2,1)} copy(bf16[64,8,8,128]{3,2,1,0:T(8,128)(2,1)S(1)} %bitcast.40) | data formatting | bytes 2097152 | tf_op jit(solution)/shard_map/reshape | solution.py:323
  52.0 10.0 %all-to-all-done.1.s_ref = bf16[16,16,1024]{2,1,0:T(8,128)(2,1)S(1)} async-done(((bf16[16,16,1024]{2,1,0:T(8,128)(2,1)}), bf16[16,16,1024]{2,1,0:T(8,128)(2,1)S(1)}, u32[]{:S(2)}, u32[]{:S(2)}) %all-to-all-start.1) | async-done | bytes 524320 | tf_op jit(solution)/shard_map/all_to_all | solution.py:317
  62.0 5.1 %all-to-all-start.3 = ((bf16[8,8,64,128]{3,2,1,0:T(8,128)(2,1)}), bf16[8,8,64,128]{3,2,1,0:T(8,128)(2,1)}, u32[]{:S(2)}, u32[]{:S(2)}) async-start(bf16[8,8,64,128]{3,2,1,0:T(8,128)(2,1)} %bitcast.38), calls=%async_computation.3 | async-start | bytes 2097152 | tf_op jit(solution)/shard_map/all_to_all | solution.py:324
  67.1 0.0 copy-done.6
  67.1 0.2 select_reduce_fusion
  67.3 0.2 convert_reduce_fusion
  67.5 0.5 shard_map.105
  68.0 23.7 %all-gather = bf16[256,1024]{1,0:T(8,128)(2,1)S(1)} all-gather(bf16[32,1024]{1,0:T(8,128)(2,1)S(1)} %shard_map.105), channel_id=2, replica_groups=mesh['x'=4,'core'=2,'y'=4,'zh'=2,'zl'=2] {'x','core'}, dimensions={0}, use_global_device_ids=true | all-gather | bytes 589824 | tf_op jit(solution)/shard_map/all_gather | solution.py:318
  91.7 1.4 shard_map.106
  93.1 0.0 all-to-all-done.3
  93.1 4.2 %all-to-all-start.2 = ((bf16[16,16,1024]{2,1,0:T(8,128)(2,1)}), bf16[16,16,1024]{2,1,0:T(8,128)(2,1)S(1)}, u32[]{:S(2)}, u32[]{:S(2)}) async-start(bf16[16,16,1024]{2,1,0:T(8,128)(2,1)} %shard_map.106), calls=%async_computation.2 | async-start | bytes 1048576 | tf_op jit(solution)/shard_map/all_to_all | solution.py:320
  97.3 0.0 all-gather.4.cloned.1.call-done
  97.3 0.0 copy-start.4
  97.3 2.2 %copy-done.4 = bf16[128,64,256]{2,1,0:T(8,128)(2,1)S(1)} copy-done((bf16[128,64,256]{2,1,0:T(8,128)(2,1)S(1)}, bf16[128,64,256]{2,1,0:T(8,128)(2,1)}, u32[]{:S(2)}) %copy-start.4) | copy-done | bytes 4194328
  99.5 29.1 %shard_map.108 = bf16[8,512,128]{2,1,0:T(8,128)(2,1)S(1)} custom-call(s32[2,8]{1,0:T(2,128)S(1)} %pad_add_fusion.meta_ref, bf16[8,512,128]{2,1,0:T(8,128)(2,1)} %bitcast.7.q_ref, bf16[2,4,2,4,2,64,256]{6,5,4,3,2,1,0:T(8,128)(2,1)S(1)} %bitcast.37), custom_call_target="tpu_custom_call" | custom-call | flops 5242880000 | bytes 6291456 | tf_op jit(solution)/shard_map/pallas_call | solution.py:120
  128.6 0.0 copy-start.2
  128.6 1.0 copy-done.2
  129.6 0.0 all-to-all-done.2.e_ref
  129.6 5.5 %all-to-all-start.5 = ((bf16[8,8,64,128]{3,2,1,0:T(8,128)(2,1)}), bf16[8,8,64,128]{3,2,1,0:T(8,128)(2,1)}, u32[]{:S(2)}, u32[]{:S(2)}) async-start(bf16[8,8,64,128]{3,2,1,0:T(8,128)(2,1)} %bitcast.33), calls=%async_computation.5 | async-start | bytes 2097152 | tf_op jit(solution)/shard_map/all_to_all | solution.py:331
  135.1 0.8 constant_dynamic-slice_fusion
  135.9 0.1 copy.42.c_ref
  136.0 8.9 %shard_map.107 = bf16[64,16384]{1,0:T(8,128)(2,1)} custom-call(bf16[64,16384]{1,0:T(8,128)(2,1)S(1)} %copy-done.1, f32[256,128]{1,0:T(8,128)S(1)} %bitcast.32, f32[64,16]{1,0:T(8,128)S(1)} %copy.41.b_ref, f32[64,16]{1,0:T(8,128)S(1)} %copy.42.c_ref, bf16[16,16,1024]{2,1,0:T(8,128)(2,1)S(1)} %all-to-all-done.2.e_ref), custom_call_target="tpu_custom_call" | custom-call | flops 167772160 | bytes 5242880 | tf_op jit(solution)/shard_map/pallas_call | solution.py:226
  144.9 2.3 %all-to-all-done.5 = bf16[8,8,64,128]{3,2,1,0:T(8,128)(2,1)} async-done(((bf16[8,8,64,128]{3,2,1,0:T(8,128)(2,1)}), bf16[8,8,64,128]{3,2,1,0:T(8,128)(2,1)}, u32[]{:S(2)}, u32[]{:S(2)}) %all-to-all-start.5) | async-done | bytes 1048608 | tf_op jit(solution)/shard_map/all_to_all | solution.py:331
  147.2 1.9 %copy.40 = bf16[64,8,8,128]{3,2,1,0:T(8,128)(2,1)S(1)} copy(bf16[64,8,8,128]{3,0,2,1:T(8,128)(2,1)} %bitcast.11) | data formatting | bytes 2097152 | tf_op jit(solution)/shard_map/transpose | solution.py:332
  149.1 1.7 %copy.50 = bf16[8,8,64,128]{3,1,2,0:T(8,128)(2,1)} copy(bf16[8,8,64,128]{3,2,1,0:T(8,128)(2,1)S(1)} %bitcast.39) | data formatting | bytes 2097152
  (7 shorter events, 0.2 us)
Async XLA Ops:
  7.2 24.0 %copy-start = (f32[1024,16]{0,1:T(8,128)S(1)}, f32[1024,16]{0,1:T(8,128)}, u32[]{:S(2)}) copy-start(f32[1024,16]{0,1:T(8,128)} %param.10) | copy-start | bytes 196612
  7.2 17.7 %copy-start.3 = (f32[1024,16]{0,1:T(8,128)S(1)}, f32[1024,16]{0,1:T(8,128)}, u32[]{:S(2)}) copy-start(f32[1024,16]{0,1:T(8,128)} %param.12) | copy-start | bytes 196612
  7.2 17.8 %copy-start.5 = (f32[16]{0:T(128)S(1)}, f32[16]{0:T(128)}, u32[]{:S(2)}) copy-start(f32[16]{0:T(128)} %param.13) | copy-start | bytes 196
  7.2 30.7 %copy-start.1 = (bf16[64,16384]{1,0:T(8,128)(2,1)S(1)}, bf16[64,16384]{1,0:T(8,128)(2,1)}, u32[]{:S(2)}) copy-start(bf16[64,16384]{1,0:T(8,128)(2,1)} %x_ref.3) | copy-start | bytes 6291460
  7.2 90.1 %all-gather.4.cloned.1.call-start = ((), (), s32[]{:S(2)}) async-start(), calls=%async_computation.6 | async-start | bytes 4456448 | tf_op jit(solution)/shard_map/all_gather | solution.py:306
  25.9 12.0 %all-to-all-start = ((f32[16,16,128]{2,1,0:T(8,128)}), f32[16,16,128]{2,1,0:T(8,128)S(1)}, u32[]{:S(2)}, u32[]{:S(2)}) async-start(f32[16,16,128]{2,1,0:T(8,128)} %pad_maximum_fusion), calls=%async_computation | async-start | bytes 262144 | tf_op jit(solution)/shard_map/all_to_all | solution.py:311
  45.3 16.7 %all-to-all-start.1 = ((bf16[16,16,1024]{2,1,0:T(8,128)(2,1)}), bf16[16,16,1024]{2,1,0:T(8,128)(2,1)S(1)}, u32[]{:S(2)}, u32[]{:S(2)}) async-start(bf16[16,16,1024]{2,1,0:T(8,128)(2,1)} %shard_map.104), calls=%async_computation.1 | async-start | bytes 1048576 | tf_op jit(solution)/shard_map/all_to_all | solution.py:317
  50.4 16.7 %copy-start.6 = (s32[64]{0:T(128)S(1)}, s32[64]{0:T(128)}, u32[]{:S(2)}) copy-start(s32[64]{0:T(128)} %param.17) | copy-start | bytes 772
  62.0 31.1 %all-to-all-start.3 = ((bf16[8,8,64,128]{3,2,1,0:T(8,128)(2,1)}), bf16[8,8,64,128]{3,2,1,0:T(8,128)(2,1)}, u32[]{:S(2)}, u32[]{:S(2)}) async-start(bf16[8,8,64,128]{3,2,1,0:T(8,128)(2,1)} %bitcast.38), calls=%async_computation.3 | async-start | bytes 2097152 | tf_op jit(solution)/shard_map/all_to_all | solution.py:324
  93.1 36.5 %all-to-all-start.2 = ((bf16[16,16,1024]{2,1,0:T(8,128)(2,1)}), bf16[16,16,1024]{2,1,0:T(8,128)(2,1)S(1)}, u32[]{:S(2)}, u32[]{:S(2)}) async-start(bf16[16,16,1024]{2,1,0:T(8,128)(2,1)} %shard_map.106), calls=%async_computation.2 | async-start | bytes 1048576 | tf_op jit(solution)/shard_map/all_to_all | solution.py:320
  97.3 2.2 %copy-start.4 = (bf16[128,64,256]{2,1,0:T(8,128)(2,1)S(1)}, bf16[128,64,256]{2,1,0:T(8,128)(2,1)}, u32[]{:S(2)}) copy-start(bf16[128,64,256]{2,1,0:T(8,128)(2,1)} %all-gather.4.cloned.1.call-done) | copy-start | bytes 12582916
  128.6 1.0 copy-start.2
  129.6 17.6 %all-to-all-start.5 = ((bf16[8,8,64,128]{3,2,1,0:T(8,128)(2,1)}), bf16[8,8,64,128]{3,2,1,0:T(8,128)(2,1)}, u32[]{:S(2)}, u32[]{:S(2)}) async-start(bf16[8,8,64,128]{3,2,1,0:T(8,128)(2,1)} %bitcast.33), calls=%async_computation.5 | async-start | bytes 2097152 | tf_op jit(solution)/shard_map/all_to_all | solution.py:331
Sparse Core Ops, SparseCore 0:
  25.0 41.5 all-gather.3

commit v2 on v1

v2 whole, which is shorter than its diff:
```python
import math

import jax
import jax.numpy as jnp
from jax import lax
from jax.experimental import pallas as pl
from jax.experimental.pallas import tpu as pltpu
from jax.sharding import Mesh, PartitionSpec as P

NS = 16
KVH = 8
HD = 128
HM = 256
CHUNK = 64
NEG = -1e30
SCORE_EXP2 = HD**-0.5 * math.log2(math.e)
HIGHEST = lax.Precision.HIGHEST
F32 = jnp.float32
BF16 = jnp.bfloat16
ALL = ("x", "core", "y", "zh", "zl")
CTX = ("x", "core")
TP = ("y", "zh", "zl")
HEADS = ("x", "zh")
VMEM = pl.BlockSpec(memory_space=pltpu.VMEM)
SMEM = pl.BlockSpec(memory_space=pltpu.SMEM)
ANY = pl.BlockSpec(memory_space=pl.ANY)
TK = 1024
NG = 4
RG = 1024 // NG
SMALL = pltpu.CompilerParams(vmem_limit_bytes=16 << 20)


def dot(a, b, dims=((1,), (0,)), precision=None):
    return lax.dot_general(
        a, b, (dims, ((), ())), precision=precision, preferred_element_type=F32
    )


def split_kernel(q_ref, k_ref, v_ref, o_ref):
    for h in range(KVH):
        o_ref[h, :, :1024] = q_ref[:, h * 1024 : (h + 1) * 1024]
        o_ref[h, :, 1024 : 1024 + HD] = k_ref[:, h * HD : (h + 1) * HD]
        o_ref[h, :, 1024 + HD :] = v_ref[:, h * HD : (h + 1) * HD]


def split_heads(queries, keys, values):
    return pl.pallas_call(
        split_kernel,
        out_shape=jax.ShapeDtypeStruct((KVH, CHUNK, 1024 + 2 * HD), BF16),
        in_specs=[VMEM] * 3,
        out_specs=VMEM,
    )(queries, keys, values)


def pick_kernel(i_ref, *refs):
    copies = [
        pltpu.make_async_copy(
            i_ref.at[pl.ds(4 * n, 4), :, pl.ds(1024, 2 * HD)], refs[n], refs[2].at[n]
        )
        for n in range(2)
    ]
    for copy in copies:
        copy.start()
    for copy in copies:
        copy.wait()


def pick_kv(arrived):
    return pl.pallas_call(
        pick_kernel,
        out_shape=[jax.ShapeDtypeStruct((4, CHUNK, 2 * HD), BF16)] * 2,
        in_specs=[ANY],
        out_specs=[VMEM] * 2,
        scratch_shapes=[pltpu.SemaphoreType.DMA((2,))],
    )(arrived)


def stack_kernel(*refs):
    for n, ref in enumerate(refs[:-1]):
        refs[-1][n] = ref[...]


def stack(blocks):
    return pl.pallas_call(
        stack_kernel,
        out_shape=jax.ShapeDtypeStruct((len(blocks),) + blocks[0].shape, blocks[0].dtype),
        in_specs=[VMEM] * len(blocks),
        out_specs=VMEM,
    )(*blocks)


def join_kernel(i_ref, o_ref):
    for h in range(KVH):
        o_ref[:, h * 1024 : (h + 1) * 1024] = i_ref[h]


def join_heads(pieces):
    return pl.pallas_call(
        join_kernel,
        out_shape=jax.ShapeDtypeStruct((CHUNK, 64 * HD), BF16),
        in_specs=[VMEM],
        out_specs=VMEM,
        compiler_params=SMALL,
    )(pieces)


def split_decay_kernel(own_ref, gain_ref, o_ref):
    row = lax.broadcasted_iota(jnp.int32, (16, 16), 0)
    col = lax.broadcasted_iota(jnp.int32, (16, 16), 1)
    gain = jnp.where(row == col, jnp.broadcast_to(gain_ref[...], (16, 16)), 0.0)
    gain = jnp.broadcast_to(jnp.sum(gain, axis=1, keepdims=True), (16, CHUNK))
    for t in range(16):
        o_ref[t, :, :CHUNK] = own_ref[:, t * CHUNK : (t + 1) * CHUNK]
        o_ref[t, :, CHUNK:] = gain


def split_decay(own, gain):
    return pl.pallas_call(
        split_decay_kernel,
        out_shape=jax.ShapeDtypeStruct((16, 16, 2 * CHUNK), F32),
        in_specs=[VMEM] * 2,
        out_specs=VMEM,
        compiler_params=SMALL,
    )(own, gain)


def attn_kernel(meta_ref, rows_ref, all_ref, *refs):
    own_refs, other_refs, refs = refs[:6], refs[6:12], refs[12:]
    out_ref, m_ref, acc_ref, s_ref, q_ref, kv_ref, vt_ref, o_ref, q_sem, sems, o_sem = refs
    core, y, zl = meta_ref[2, 0], meta_ref[3, 0], meta_ref[3, 1]
    pltpu.make_async_copy(all_ref.at[:, :, pl.ds(0, 1024)], q_ref, q_sem).start()
    for x in range(4):
        for group, of in ((own_refs, core), (other_refs, 1 - core)):
            for dy in range(4):
                for dz in range(2):
                    piece = group[dy].at[dz] if x < 2 else group[4 + dz].at[dy]
                    pltpu.make_async_copy(
                        piece.at[pl.ds(2 * (x % 2), 2)],
                        kv_ref.at[2 * x + of, lax.rem(y + 4 - dy, 4), :, lax.rem(zl + dz, 2)],
                        sems.at[2 * x + of],
                    ).start()

    def arrive(w):
        pltpu.make_async_copy(kv_ref.at[w], kv_ref.at[w], sems.at[w]).wait()

    def prepare(w):
        arrive(w)
        vt_ref[w, :HD, :] = kv_ref[w].reshape(TK, 2 * HD)[:, HD:].T
        vt_ref[w, HD:, :] = jnp.ones((16, TK), BF16)

    def scores(i, j, slot):
        k = kv_ref[j].reshape(TK, 2 * HD)[:, :HD]
        for g in range(NG):
            heads = range(4 * (g % 2), 4 * (g % 2) + 4)
            q = [q_ref[2 * i + g // 2, :, a * HD : (a + 1) * HD] for a in heads]
            s_ref[slot, g] = dot(k, jnp.concatenate(q, axis=0), ((1,), (1,)))

    def absorb(i, j, slot, masked):
        v = vt_ref[j]
        for g in range(NG):
            s = s_ref[slot, g]
            if masked:
                kpos = j * TK + lax.broadcasted_iota(jnp.int32, (TK, RG), 0)
                seen = (kpos <= rows_ref[i, g, 0:1]) & (kpos >= rows_ref[i, g, 1:2])
                s = jnp.where(seen, s, NEG)
            before = m_ref[g]
            top = jnp.maximum(before, jnp.max(s, axis=0, keepdims=True))
            p = jnp.exp2((s - top) * SCORE_EXP2)
            fade = jnp.exp2((before - top) * SCORE_EXP2)
            m_ref[g] = top
            acc_ref[g] = acc_ref[g] * fade + dot(v, p.astype(BF16))

    def reset():
        m_ref[...] = jnp.full_like(m_ref, NEG)
        acc_ref[...] = jnp.zeros_like(acc_ref)

    def window(i):
        return 2 * i + core

    def body(carry):
        i, j, slot = carry
        last = j == window(i)
        i_next = jnp.where(last, i + 1, i)
        i_read = jnp.minimum(i_next, 3)
        j_next = jnp.where(last, meta_ref[0, i_read] // TK, j + 1)
        edge = last | (j * TK < meta_ref[1, i])

        @pl.when(last & (i < 3))
        def _():
            for n in range(2):
                prepare(window(i) + 1 + n)

        @pl.when(edge)
        def _():
            scores(i_read, j_next, 1 - slot)
            absorb(i, j, slot, True)

        @pl.when(jnp.logical_not(edge))
        def _():
            scores(i_read, j_next, 1 - slot)
            absorb(i, j, slot, False)

        @pl.when(last)
        def _():
            for g in range(NG):
                out = (acc_ref[g, :HD] * (1.0 / acc_ref[g, HD : HD + 1])).T.astype(BF16)
                for a in range(4):
                    low = (4 * (g % 2) + a) * HD
                    o_ref[i, g // 2, :, low : low + HD] = out[a * CHUNK : (a + 1) * CHUNK]
            pltpu.make_async_copy(o_ref.at[i], out_ref.at[pl.ds(2 * i, 2)], o_sem.at[i]).start()
            reset()

        return (i_next, j_next, 1 - slot)

    reset()
    prepare(0)

    @pl.when(core == 1)
    def _():
        prepare(1)

    pltpu.make_async_copy(q_ref, q_ref, q_sem).wait()
    start = meta_ref[0, 0] // TK
    scores(0, start, 0)
    lax.while_loop(lambda carry: carry[0] < 4, body, (jnp.int32(0), start, jnp.int32(0)))

    @pl.when(core == 0)
    def _():
        arrive(7)

    for n in range(4):
        pltpu.make_async_copy(o_ref.at[n], out_ref.at[pl.ds(0, 2)], o_sem.at[n]).wait()


def attend(meta, rows, heads, own, other):
    return pl.pallas_call(
        attn_kernel,
        out_shape=jax.ShapeDtypeStruct((8, CHUNK, 1024), BF16),
        in_specs=[SMEM, VMEM] + [ANY] * 13,
        out_specs=ANY,
        scratch_shapes=[
            pltpu.VMEM((NG, 1, RG), F32),
            pltpu.VMEM((NG, HD + 16, RG), F32),
            pltpu.VMEM((2, NG, TK, RG), F32),
            pltpu.VMEM((8, CHUNK, 1024), BF16),
            pltpu.VMEM((8, 4, 2, 2, CHUNK, 2 * HD), BF16),
            pltpu.VMEM((8, HD + 16, TK), BF16),
            pltpu.VMEM((4, 2, CHUNK, 1024), BF16),
            pltpu.SemaphoreType.DMA,
            pltpu.SemaphoreType.DMA((8,)),
            pltpu.SemaphoreType.DMA((4,)),
        ],
        compiler_params=pltpu.CompilerParams(vmem_limit_bytes=60 << 20),
        cost_estimate=pl.CostEstimate(
            flops=12_000_000_000, bytes_accessed=6 << 20, transcendentals=5_000_000
        ),
    )(meta, rows, heads, *own, *other)


def one_minus_exp(u):
    small = -u * (
        1
        + u / 2 * (1 + u / 3 * (1 + u / 4 * (1 + u / 5 * (1 + u / 6 * (1 + u / 7 * (1 + u / 8))))))
    )
    return jnp.where(u > -0.5, small, 1 - jnp.exp(u))


def spread(columns, heads):
    rows = columns.shape[0]
    half = lax.broadcasted_iota(jnp.int32, (rows, 128), 1) // CHUNK
    parts = [
        jnp.take_along_axis(columns, half + h, axis=1, mode="promise_in_bounds")
        for h in range(0, heads, 2)
    ]
    return jnp.concatenate(parts, axis=1)


def running_decay(decay):
    row = lax.broadcasted_iota(jnp.int32, (CHUNK, CHUNK), 0)
    col = lax.broadcasted_iota(jnp.int32, (CHUNK, CHUNK), 1)
    tri = jnp.where(row >= col, 1.0, 0.0).astype(F32)
    return dot(tri, decay, precision=HIGHEST)


def own_columns(ref, place):
    block = ref[:, pl.ds(pl.multiple_of(place // 2 * 128, 128), 128)]
    return jnp.where(place % 2 == 1, block[:, CHUNK:], block[:, :CHUNK])


def state_kernel(place_ref, x_ref, dec_ref, b_ref, s_ref, f_ref, d_ref):
    decay = dec_ref[...].T[:CHUNK]
    run = running_decay(decay)
    drive = jnp.exp(run[CHUNK - 1 :] - run) * jnp.sqrt(one_minus_exp(2.0 * decay))
    end = jnp.exp(run[CHUNK - 1 :])
    high = end.astype(BF16).astype(F32)
    row = lax.broadcasted_iota(jnp.int32, (8, HM), 0)
    parts = jnp.where(row == 0, high, jnp.where(row == 1, end - high, 0.0))
    for k in range(16):
        f_ref[k, :, :16] = drive[:, 16 * k : 16 * k + 16]
        d_ref[k, :, :16] = parts[:, 16 * k : 16 * k + 16]
    b = own_columns(b_ref, place_ref[2])
    b_high = b.astype(BF16)
    b_low = (b - b_high.astype(F32)).astype(BF16)
    b_two = jnp.concatenate([b_high, b_low], axis=0)

    def block(k, carry):
        cols = pl.ds(pl.multiple_of(k * 1024, 1024), 1024)
        z = (x_ref[:, cols].astype(F32) * spread(f_ref[k], 16)).astype(BF16)
        two = dot(b_two, z)
        full = jnp.concatenate([two[:NS] + two[NS:], spread(d_ref[k], 16)], axis=0).astype(BF16)
        for m in range(8):
            s_ref[8 * k + m] = full[:, 128 * m : 128 * (m + 1)]
        return carry

    lax.fori_loop(0, 16, block, 0, unroll=4)


def chunk_states(place, x, dec, b):
    return pl.pallas_call(
        state_kernel,
        out_shape=jax.ShapeDtypeStruct((128, NS + 8, 128), BF16),
        in_specs=[SMEM] + [VMEM] * 3,
        out_specs=VMEM,
        scratch_shapes=[pltpu.VMEM((16, CHUNK, 128), F32), pltpu.VMEM((16, 8, 128), F32)],
        compiler_params=SMALL,
        cost_estimate=pl.CostEstimate(
            flops=2 * 32 * CHUNK * 16384, bytes_accessed=3 << 20, transcendentals=50_000
        ),
    )(place, x, dec, b)


def output_kernel(place_ref, x_ref, dec_ref, b_ref, c_ref, e_ref, y_ref, f_ref, r_ref, g_ref):
    both = dec_ref[...].T
    decay = both[:CHUNK]
    run = running_decay(decay)
    drive = jnp.exp(-run) * jnp.sqrt(one_minus_exp(2.0 * decay))
    reach = jnp.exp(run)
    gain = jnp.broadcast_to(both[CHUNK : CHUNK + 1], (8, HM))
    for k in range(16):
        f_ref[k, :, :16] = drive[:, 16 * k : 16 * k + 16]
        r_ref[k, :, :16] = reach[:, 16 * k : 16 * k + 16]
        g_ref[k, :, :16] = gain[:, 16 * k : 16 * k + 16]
    row = lax.broadcasted_iota(jnp.int32, (CHUNK, CHUNK), 0)
    col = lax.broadcasted_iota(jnp.int32, (CHUNK, CHUNK), 1)
    b = own_columns(b_ref, place_ref[2])
    c = own_columns(c_ref, place_ref[2])
    inner = jnp.where(row >= col, dot(c, b, ((0,), (0,)), HIGHEST), 0.0)
    weights = jnp.concatenate([inner, c.T], axis=1).astype(BF16)

    def block(k, carry):
        cols = pl.ds(pl.multiple_of(k * 1024, 1024), 1024)
        x = x_ref[:, cols].astype(F32)
        z = (x * spread(f_ref[k], 16)).astype(BF16)
        entering = jnp.concatenate([e_ref[8 * k + m] for m in range(8)], axis=1)
        y = dot(weights, jnp.concatenate([z, entering], axis=0))
        y = y * spread(r_ref[k], 16) + spread(g_ref[k], 16)[:1] * x
        y_ref[:, cols] = y.astype(BF16)
        return carry

    lax.fori_loop(0, 16, block, 0, unroll=4)


def chunk_outputs(place, x, dec, b, c, entering):
    return pl.pallas_call(
        output_kernel,
        out_shape=jax.ShapeDtypeStruct((CHUNK, 16384), BF16),
        in_specs=[SMEM] + [VMEM] * 5,
        out_specs=VMEM,
        scratch_shapes=[
            pltpu.VMEM((16, CHUNK, 128), F32),
            pltpu.VMEM((16, CHUNK, 128), F32),
            pltpu.VMEM((16, 8, 128), F32),
        ],
        compiler_params=SMALL,
        cost_estimate=pl.CostEstimate(
            flops=2 * 80 * CHUNK * 16384, bytes_accessed=5 << 20, transcendentals=50_000
        ),
    )(place, x, dec, b, c, entering)


def enter_kernel(s_ref, e_ref):
    def chunk(k, state):
        e_ref[k] = state.astype(BF16)
        arrived = s_ref[k].astype(F32)
        return state * (arrived[NS : NS + 1] + arrived[NS + 1 : NS + 2]) + arrived[:NS]

    lax.fori_loop(0, 128, chunk, jnp.zeros((NS, 128), F32), unroll=8)


def entering_states(states):
    return pl.pallas_call(
        enter_kernel,
        out_shape=jax.ShapeDtypeStruct((128, NS, 128), BF16),
        in_specs=[VMEM],
        out_specs=VMEM,
        compiler_params=SMALL,
        cost_estimate=pl.CostEstimate(
            flops=60_000_000_000, bytes_accessed=2 << 20, transcendentals=0
        ),
    )(states)


def per_device(
    mamba_in, state_in_b, state_out_c, step_decay, skip_gain, queries, keys, values, doc_ids
):
    core, y, zl = lax.axis_index("core"), lax.axis_index("y"), lax.axis_index("zl")
    z = 2 * lax.axis_index("zh") + zl
    spot = jnp.stack([y, z, 4 * y + z]).astype(jnp.int32)
    b, c = state_in_b.T, state_out_c.T

    heads = lax.all_to_all(split_heads(queries, keys, values), HEADS, 0, 0, tiled=True)

    dec, heads = lax.optimization_barrier((split_decay(step_decay.T, skip_gain[None]), heads))
    dec = lax.all_to_all(dec, TP, 0, 0, tiled=True).reshape(HM, 2 * CHUNK)
    def along_z(block):
        return [block, lax.ppermute(block, "zl", [(0, 1), (1, 0)])]

    def along_y(block):
        steps = [[(n, (n + k) % 4) for n in range(4)] for k in range(1, 4)]
        return [block] + [lax.ppermute(block, "y", step) for step in steps]

    lead, tail = pick_kv(heads)
    lead, tail = stack(along_z(lead)), stack(along_y(tail))
    dec, lead, tail = lax.optimization_barrier((dec, lead, tail))
    states = chunk_states(spot, mamba_in, dec, b)
    own = along_y(lead) + along_z(tail)
    other = [lax.ppermute(block, "core", [(0, 1), (1, 0)]) for block in own]
    states = lax.all_to_all(states, ALL, 0, 0, tiled=True)

    blocks = jnp.arange(64, dtype=jnp.int32)
    starts = jnp.sum(doc_ids[None] < doc_ids[:, None], axis=1).astype(jnp.int32) * 128
    row = jnp.arange(1024, dtype=jnp.int32)
    place = (2 * jnp.arange(4)[:, None] + core) * 1024 + row % 64
    place = place + (4 * y + 2 * (row // 512) + zl) * CHUNK
    first = jnp.sum(
        jnp.where(place[:, :, None] // 128 == blocks, starts[None, None], 0), axis=2
    )
    rows = jnp.stack([place, first], axis=1).astype(jnp.int32)
    low, high = jnp.min(first, axis=1), jnp.max(first, axis=1)
    rows = rows.reshape(4, 2, NG, RG).transpose(0, 2, 1, 3)
    ids = jnp.stack([y, zl, y, zl])
    meta = jnp.stack([low, high, jnp.broadcast_to(core, (4,)), ids]).astype(jnp.int32)
    entering = entering_states(states)
    entering, meta = lax.optimization_barrier((entering, meta))
    entering = lax.all_to_all(entering, ALL, 0, 0, tiled=True)
    attn = attend(meta, rows, heads, own, other)
    attn = lax.all_to_all(attn, HEADS, 0, 0, tiled=True)
    mamba_out = chunk_outputs(spot, mamba_in, dec, b, c, entering)
    return (mamba_out, join_heads(attn))


def solution(mesh):
    inner = Mesh(mesh.devices.reshape(4, 2, 4, 2, 2), ALL)
    in_specs = (
        P(ALL, None),
        P(CTX, None),
        P(CTX, None),
        P(CTX, TP),
        P(TP),
        P(ALL, None),
        P(ALL, None),
        P(ALL, None),
        P(),
    )
    out_specs = (P(ALL, None), P(ALL, None))
    return jax.shard_map(
        per_device, mesh=inner, in_specs=in_specs, out_specs=out_specs, check_vma=False
    )
```

time: 158 us -> 146 us (0.924)
  the two profiles are of different devices: /device:TPU:1 before, /device:TPU:0 now
where the time goes in v2:
time: 146 us; the launch traced here: 145 us
  Pallas kernels  48.5 us (33%)
  starting transfers between devices  46.9 us (32%)
  waiting for transfers between devices  41.3 us (28%)
  local copies, waits for them, and re-layouts  4.85 us (3%)
  other arithmetic  2.22 us (2%)
    pallas_call x1, Pallas kernels, attend(): pl.pallas_call(attn_kernel, out_shape=jax.ShapeDtypeStruct((8, CHUNK, 102...  26.8 us
    all_to_all x1, waiting for transfers between devices, per_device(): lax.all_to_all(split_heads(queries, keys, values), HEADS, 0, 0, tiled=True)  18.7 us
    ppermute x6, waiting for transfers between devices, along_y(): return [block] + [lax.ppermute(block, 'y', step) for step in steps]  14.7 us
    ppermute x6, starting transfers between devices, along_y(): return [block] + [lax.ppermute(block, 'y', step) for step in steps]  11 us
    all_to_all x1, starting transfers between devices, per_device(): entering = lax.all_to_all(entering, ALL, 0, 0, tiled=True)  8.47 us
    all_to_all x1, starting transfers between devices, per_device(): lax.all_to_all(split_heads(queries, keys, values), HEADS, 0, 0, tiled=True)  7.7 us
    all_to_all x1, starting transfers between devices, per_device(): attn = lax.all_to_all(attn, HEADS, 0, 0, tiled=True)  6.57 us
    all_to_all x1, starting transfers between devices, per_device(): states = lax.all_to_all(states, ALL, 0, 0, tiled=True)  6.46 us
  transfers between devices with their start and end apart: 19, of which 7 were waited for; matrix products, arithmetic and copies ran while one was open for 2% of the time, Pallas kernels for 27%

profile of v2, /device:TPU:0, one launch (start us, length us, event | category | flops | bytes accessed | tf_op | source)
XLA Modules:
  0.0 144.6 jit_solution(11700697170700733159)
XLA Ops:
  0.7 2.5 %shard_map.105 = bf16[8,64,1280]{2,1,0:T(8,128)(2,1)} custom-call(bf16[64,8192]{1,0:T(8,128)(2,1)} %q_ref.1, bf16[64,1024]{1,0:T(8,128)(2,1)} %k_ref.1, bf16[64,1024]{1,0:T(8,128)(2,1)} %v_ref.1), custom_call_target="tpu_custom_call" | custom-call | tf_op jit(solution)/shard_map/pallas_call | solution.py:47
  3.2 7.7 %all-to-all-start = ((bf16[8,64,1280]{2,1,0:T(8,128)(2,1)}), bf16[8,64,1280]{2,1,0:T(8,128)(2,1)}, u32[]{:S(2)}, u32[]{:S(2)}) async-start(bf16[8,64,1280]{2,1,0:T(8,128)(2,1)} %shard_map.105), calls=%async_computation | async-start | bytes 2621440 | tf_op jit(solution)/shard_map/all_to_all | solution.py:411
  10.9 0.0 copy-start.3
  10.9 0.8 shard_map.104
  11.7 0.2 convert_reduce_fusion
  11.9 0.1 add_select_fusion
  12.0 0.2 select_reduce_fusion
  12.2 18.7 %all-to-all-done.i_ref.all_ref = bf16[8,64,1280]{2,1,0:T(8,128)(2,1)} async-done(((bf16[8,64,1280]{2,1,0:T(8,128)(2,1)}), bf16[8,64,1280]{2,1,0:T(8,128)(2,1)}, u32[]{:S(2)}, u32[]{:S(2)}) %all-to-all-start) | async-done | bytes 1310752 | tf_op jit(solution)/shard_map/all_to_all | solution.py:411
  30.9 1.7 %shard_map.106 = (bf16[4,64,256]{2,1,0:T(8,128)(2,1)}, bf16[4,64,256]{2,1,0:T(8,128)(2,1)}) custom-call(bf16[8,64,1280]{2,1,0:T(8,128)(2,1)} %all-to-all-done.i_ref.all_ref), custom_call_target="tpu_custom_call" | custom-call | tf_op jit(solution)/shard_map/pallas_call | solution.py:69
  32.6 1.6 %collective-permute-start.1 = (bf16[4,64,256]{2,1,0:T(8,128)(2,1)}, bf16[4,64,256]{2,1,0:T(8,128)(2,1)S(1)}, u32[]{:S(2)}, u32[]{:S(2)}) collective-permute-start(bf16[4,64,256]{2,1,0:T(8,128)(2,1)} %get-tuple-element.14.refs_0_), channel_id=1, source_target_pairs={{0,4},{4,8},{8,12},{12,0},{1,5},{5,9},{9,13},{13,1},{2,6},{6,10},{... | collective-permute-start | bytes 393224 | tf_op jit(solution)/shard_map/ppermute | solution.py:420
  34.2 2.9 %collective-permute-start.2 = (bf16[4,64,256]{2,1,0:T(8,128)(2,1)}, bf16[4,64,256]{2,1,0:T(8,128)(2,1)S(1)}, u32[]{:S(2)}, u32[]{:S(2)}) collective-permute-start(bf16[4,64,256]{2,1,0:T(8,128)(2,1)} %get-tuple-element.14.refs_0_), channel_id=1, source_target_pairs={{0,8},{4,12},{8,0},{12,4},{1,9},{5,13},{9,1},{13,5},{2,10},{6,14},... | collective-permute-start | bytes 393224 | tf_op jit(solution)/shard_map/ppermute | solution.py:420
  37.1 1.3 collective-permute-start.3
  38.5 1.0 collective-permute-start
  39.5 3.5 %all-to-all-start.1 = ((f32[16,16,128]{2,1,0:T(8,128)}), f32[16,16,128]{2,1,0:T(8,128)S(1)}, u32[]{:S(2)}, u32[]{:S(2)}) async-start(f32[16,16,128]{2,1,0:T(8,128)} %shard_map.104), calls=%async_computation.1 | async-start | bytes 262144 | tf_op jit(solution)/shard_map/all_to_all | solution.py:414
  43.0 0.1 pad_add_fusion.1.place_ref
  43.1 0.7 collective-permute-done.refs_1_
  43.8 0.6 copy-done.8
  44.4 1.7 %shard_map.107.refs_0_ = bf16[2,4,64,256]{3,2,1,0:T(8,128)(2,1)} custom-call(bf16[4,64,256]{2,1,0:T(8,128)(2,1)} %get-tuple-element.13.refs_0_, bf16[4,64,256]{2,1,0:T(8,128)(2,1)} %copy-done.8), custom_call_target="tpu_custom_call" | custom-call | tf_op jit(solution)/shard_map/pallas_call | solution.py:84
  46.1 0.0 collective-permute-done.1.refs_1_
  46.1 0.0 collective-permute-done.2.refs_2_
  46.2 0.0 collective-permute-done.3.refs_3_
  46.2 0.6 copy-done.9
  46.8 0.0 copy-done.10
  46.8 0.6 copy-done.11
  47.5 1.9 %shard_map.108.refs_4_ = bf16[4,4,64,256]{3,2,1,0:T(8,128)(2,1)} custom-call(bf16[4,64,256]{2,1,0:T(8,128)(2,1)} %get-tuple-element.14.refs_0_, bf16[4,64,256]{2,1,0:T(8,128)(2,1)} %copy-done.9, bf16[4,64,256]{2,1,0:T(8,128)(2,1)} %copy-done.10, bf16[4,64,256]{2,1,0:T(8,128)(2,1)} %copy-done.11), custom_call_target="tpu_custom_call" | custom-call | tf_op jit(solution)/shard_map/pallas_call | solution.py:84
  49.4 1.4 all-to-all-done.1
  50.8 4.6 %shard_map.109 = bf16[128,24,128]{2,1,0:T(8,128)(2,1)} custom-call(s32[3]{0:T(128)S(1)} %pad_add_fusion.1.place_ref, bf16[64,16384]{1,0:T(8,128)(2,1)S(1)} %copy-done, f32[256,128]{1,0:T(8,128)S(1)} %bitcast.16, f32[16,1024]{1,0:T(8,128)S(1)} %bitcast.18), custom_call_target="tpu_custom_call" | custom-call | flops 67108864 | bytes 3145728 | tf_op jit(solution)/shard_map/pallas_call | solution.py:319
  55.4 6.5 %all-to-all-start.2 = ((bf16[128,24,128]{2,1,0:T(8,128)(2,1)}), bf16[128,24,128]{2,1,0:T(8,128)(2,1)S(1)}, u32[]{:S(2)}, u32[]{:S(2)}) async-start(bf16[128,24,128]{2,1,0:T(8,128)(2,1)} %shard_map.109), calls=%async_computation.2 | async-start | bytes 1572864 | tf_op jit(solution)/shard_map/all_to_all | solution.py:428
  61.8 0.1 add_add_fusion
  61.9 1.2 collective-permute-start.7
  63.1 0.2 fusion.22
  63.2 0.6 add_bitcast_fusion.rows_ref
  63.9 3.1 %collective-permute-start.5 = (bf16[2,4,64,256]{3,2,1,0:T(8,128)(2,1)S(1)}, bf16[2,4,64,256]{3,2,1,0:T(8,128)(2,1)}, u32[]{:S(2)}, u32[]{:S(2)}) collective-permute-start(bf16[2,4,64,256]{3,2,1,0:T(8,128)(2,1)S(1)} %copy-done.7), channel_id=1, source_target_pairs={{0,8},{4,12},{8,0},{12,4},{1,9},{5,13},{9,1},{13,5},{2,10},{6,14},... | collective-permute-start | bytes 786440 | tf_op jit(solution)/shard_map/ppermute | solution.py:420
  67.0 1.1 collective-permute-start.6
  68.1 0.9 collective-permute-start.4
  69.0 0.0 collective-permute-start.8
  69.0 0.1 add_bitcast_fusion.1
  69.1 0.1 pad.4.clone
  69.1 0.7 pad_add_fusion.meta_ref
  69.8 9.5 %collective-permute-done.5.refs_2_ = bf16[2,4,64,256]{3,2,1,0:T(8,128)(2,1)} collective-permute-done((bf16[2,4,64,256]{3,2,1,0:T(8,128)(2,1)S(1)}, bf16[2,4,64,256]{3,2,1,0:T(8,128)(2,1)}, u32[]{:S(2)}, u32[]{:S(2)}) %collective-permute-start.5) | collective-permute-done | bytes 262176 | tf_op jit(solution)/shard_map/ppermute | solution.py:420
  79.3 0.0 collective-permute-start.12
  79.3 4.1 %collective-permute-done.6.refs_3_ = bf16[2,4,64,256]{3,2,1,0:T(8,128)(2,1)} collective-permute-done((bf16[2,4,64,256]{3,2,1,0:T(8,128)(2,1)S(1)}, bf16[2,4,64,256]{3,2,1,0:T(8,128)(2,1)}, u32[]{:S(2)}, u32[]{:S(2)}) %collective-permute-start.6) | collective-permute-done | bytes 262176 | tf_op jit(solution)/shard_map/ppermute | solution.py:420
  83.4 0.0 collective-permute-start.10
  83.4 1.1 collective-permute-done.4.refs_1_
  84.5 0.1 collective-permute-start.11
  84.6 0.5 collective-permute-start.9
  85.0 0.3 copy-done.12
  85.3 0.5 collective-permute-start.13
  85.8 1.2 shard_map.110
  86.9 8.5 %all-to-all-start.3 = ((bf16[128,16,128]{2,1,0:T(8,128)(2,1)}), bf16[128,16,128]{2,1,0:T(8,128)(2,1)S(1)}, u32[]{:S(2)}, u32[]{:S(2)}) async-start(bf16[128,16,128]{2,1,0:T(8,128)(2,1)} %shard_map.110), calls=%async_computation.3 | async-start | bytes 1048576 | tf_op jit(solution)/shard_map/all_to_all | solution.py:445
  95.4 0.0 collective-permute-done.11.refs_9_
  95.4 0.0 collective-permute-done.9.refs_7_
  95.5 0.0 collective-permute-done.13.refs_11_
  95.5 0.7 copy-done.13
  96.2 26.8 %shard_map.112 = bf16[8,64,1024]{2,1,0:T(8,128)(2,1)} custom-call(s32[4,4]{1,0:T(4,128)} %pad_add_fusion.meta_ref, s32[4,4,2,256]{3,2,1,0:T(2,128)} %add_bitcast_fusion.rows_ref, bf16[8,64,1280]{2,1,0:T(8,128)(2,1)} %all-to-all-done.i_ref.all_ref, bf16[2,4,64,256]{3,2,1,0:T(8,128)(2,1)} %shard_map.107.refs_0_, ...), custom_call_target="tpu_custom_call" | custom-call | flops 12000000000 | bytes 6291456 | tf_op jit(solution)/shard_map/pallas_call | solution.py:236
  123.0 0.0 copy-start.4
  123.0 0.0 copy-start.1
  123.0 0.8 copy-done.1
  123.8 6.6 %all-to-all-start.4 = ((bf16[8,64,1024]{2,1,0:T(8,128)(2,1)}), bf16[8,64,1024]{2,1,0:T(8,128)(2,1)S(1)}, u32[]{:S(2)}, u32[]{:S(2)}) async-start(bf16[8,64,1024]{2,1,0:T(8,128)(2,1)} %shard_map.112), calls=%async_computation.4 | async-start | bytes 2097152 | tf_op jit(solution)/shard_map/all_to_all | solution.py:447
  130.4 0.0 copy-start.2
  130.4 1.0 copy-done.2
  131.4 6.3 %shard_map.111 = bf16[64,16384]{1,0:T(8,128)(2,1)} custom-call(s32[3]{0:T(128)S(1)} %pad_add_fusion.1.place_ref, bf16[64,16384]{1,0:T(8,128)(2,1)S(1)} %copy-done, f32[256,128]{1,0:T(8,128)S(1)} %bitcast.17, f32[16,1024]{1,0:T(8,128)S(1)} %bitcast.19, f32[16,1024]{1,0:T(8,128)S(1)} %bitcast.20, bf16[128,16,128]{2,1,0:T(8,128)(2,1)S(1)} %copy-done.2), custom_call_target="tpu_custom_call" | custom-call | flops 167772160 | bytes 5242880 | tf_op jit(solution)/shard_map/pallas_call | solution.py:364
  137.7 5.8 %all-to-all-done.4.i_ref = bf16[8,64,1024]{2,1,0:T(8,128)(2,1)S(1)} async-done(((bf16[8,64,1024]{2,1,0:T(8,128)(2,1)}), bf16[8,64,1024]{2,1,0:T(8,128)(2,1)S(1)}, u32[]{:S(2)}, u32[]{:S(2)}) %all-to-all-start.4) | async-done | bytes 1048608 | tf_op jit(solution)/shard_map/all_to_all | solution.py:447
  143.5 1.0 shard_map.113
  (29 shorter events, 0.1 us)
Async XLA Ops:
  0.6 10.2 %copy-start.5 = (f32[1024,16]{0,1:T(8,128)S(1)}, f32[1024,16]{0,1:T(8,128)}, u32[]{:S(2)}) copy-start(f32[1024,16]{0,1:T(8,128)} %param.12) | copy-start | bytes 196612
  0.6 10.2 %copy-start.6 = (f32[16]{0:T(128)S(1)}, f32[16]{0:T(128)}, u32[]{:S(2)}) copy-start(f32[16]{0:T(128)} %param.13) | copy-start | bytes 196
  0.7 11.0 %copy-start.14 = (s32[64]{0:T(128)S(1)}, s32[64]{0:T(128)}, u32[]{:S(2)}) copy-start(s32[64]{0:T(128)} %param.17) | copy-start | bytes 772
  3.2 27.7 %all-to-all-start = ((bf16[8,64,1280]{2,1,0:T(8,128)(2,1)}), bf16[8,64,1280]{2,1,0:T(8,128)(2,1)}, u32[]{:S(2)}, u32[]{:S(2)}) async-start(bf16[8,64,1280]{2,1,0:T(8,128)(2,1)} %shard_map.105), calls=%async_computation | async-start | bytes 2621440 | tf_op jit(solution)/shard_map/all_to_all | solution.py:411
  10.9 39.9 %copy-start = (bf16[64,16384]{1,0:T(8,128)(2,1)S(1)}, bf16[64,16384]{1,0:T(8,128)(2,1)}, u32[]{:S(2)}) copy-start(bf16[64,16384]{1,0:T(8,128)(2,1)} %x_ref.3) | copy-start | bytes 6291460
  10.9 39.9 %copy-start.3 = (f32[1024,16]{0,1:T(8,128)S(1)}, f32[1024,16]{0,1:T(8,128)}, u32[]{:S(2)}) copy-start(f32[1024,16]{0,1:T(8,128)} %param.10) | copy-start | bytes 196612
  32.6 13.6 %collective-permute-start.1 = (bf16[4,64,256]{2,1,0:T(8,128)(2,1)}, bf16[4,64,256]{2,1,0:T(8,128)(2,1)S(1)}, u32[]{:S(2)}, u32[]{:S(2)}) collective-permute-start(bf16[4,64,256]{2,1,0:T(8,128)(2,1)} %get-tuple-element.14.refs_0_), channel_id=1, source_target_pairs={{0,4},{4,8},{8,12},{12,0},{1,5},{5,9},{9,13},{13,1},{2,6},{6,10},{... | collective-permute-start | bytes 393224 | tf_op jit(solution)/shard_map/ppermute | solution.py:420
  34.2 11.9 %collective-permute-start.2 = (bf16[4,64,256]{2,1,0:T(8,128)(2,1)}, bf16[4,64,256]{2,1,0:T(8,128)(2,1)S(1)}, u32[]{:S(2)}, u32[]{:S(2)}) collective-permute-start(bf16[4,64,256]{2,1,0:T(8,128)(2,1)} %get-tuple-element.14.refs_0_), channel_id=1, source_target_pairs={{0,8},{4,12},{8,0},{12,4},{1,9},{5,13},{9,1},{13,5},{2,10},{6,14},... | collective-permute-start | bytes 393224 | tf_op jit(solution)/shard_map/ppermute | solution.py:420
  37.1 9.1 %collective-permute-start.3 = (bf16[4,64,256]{2,1,0:T(8,128)(2,1)}, bf16[4,64,256]{2,1,0:T(8,128)(2,1)S(1)}, u32[]{:S(2)}, u32[]{:S(2)}) collective-permute-start(bf16[4,64,256]{2,1,0:T(8,128)(2,1)} %get-tuple-element.14.refs_0_), channel_id=1, source_target_pairs={{0,12},{4,0},{8,4},{12,8},{1,13},{5,1},{9,5},{13,9},{2,14},{6,2},{... | collective-permute-start | bytes 393224 | tf_op jit(solution)/shard_map/ppermute | solution.py:420
  38.5 5.4 %collective-permute-start = (bf16[4,64,256]{2,1,0:T(8,128)(2,1)}, bf16[4,64,256]{2,1,0:T(8,128)(2,1)S(1)}, u32[]{:S(2)}, u32[]{:S(2)}) collective-permute-start(bf16[4,64,256]{2,1,0:T(8,128)(2,1)} %get-tuple-element.13.refs_0_), channel_id=1, source_target_pairs={{0,1},{1,0},{2,3},{3,2},{4,5},{5,4},{6,7},{7,6},{8,9},{9,8},{10,11... | collective-permute-start | bytes 393224 | tf_op jit(solution)/shard_map/ppermute | solution.py:416
  39.5 11.3 %all-to-all-start.1 = ((f32[16,16,128]{2,1,0:T(8,128)}), f32[16,16,128]{2,1,0:T(8,128)S(1)}, u32[]{:S(2)}, u32[]{:S(2)}) async-start(f32[16,16,128]{2,1,0:T(8,128)} %shard_map.104), calls=%async_computation.1 | async-start | bytes 262144 | tf_op jit(solution)/shard_map/all_to_all | solution.py:414
  43.8 0.6 copy-start.8
  46.1 0.7 copy-start.9
  46.2 0.7 copy-start.10
  46.8 0.6 copy-start.11
  50.8 13.1 %copy-start.7 = (bf16[2,4,64,256]{3,2,1,0:T(8,128)(2,1)S(1)}, bf16[2,4,64,256]{3,2,1,0:T(8,128)(2,1)}, u32[]{:S(2)}) copy-start(bf16[2,4,64,256]{3,2,1,0:T(8,128)(2,1)} %shard_map.107.refs_0_) | copy-start | bytes 786436
  55.4 30.4 %all-to-all-start.2 = ((bf16[128,24,128]{2,1,0:T(8,128)(2,1)}), bf16[128,24,128]{2,1,0:T(8,128)(2,1)S(1)}, u32[]{:S(2)}, u32[]{:S(2)}) async-start(bf16[128,24,128]{2,1,0:T(8,128)(2,1)} %shard_map.109), calls=%async_computation.2 | async-start | bytes 1572864 | tf_op jit(solution)/shard_map/all_to_all | solution.py:428
  61.9 23.1 %collective-permute-start.7 = (bf16[4,4,64,256]{3,2,1,0:T(8,128)(2,1)}, bf16[4,4,64,256]{3,2,1,0:T(8,128)(2,1)}, u32[]{:S(2)}, u32[]{:S(2)}) collective-permute-start(bf16[4,4,64,256]{3,2,1,0:T(8,128)(2,1)} %shard_map.108.refs_4_), channel_id=1, source_target_pairs={{0,1},{1,0},{2,3},{3,2},{4,5},{5,4},{6,7},{7,6},{8,9},{9,8},{10,11... | collective-permute-start | bytes 1572872 | tf_op jit(solution)/shard_map/ppermute | solution.py:416
  63.9 15.5 %collective-permute-start.5 = (bf16[2,4,64,256]{3,2,1,0:T(8,128)(2,1)S(1)}, bf16[2,4,64,256]{3,2,1,0:T(8,128)(2,1)}, u32[]{:S(2)}, u32[]{:S(2)}) collective-permute-start(bf16[2,4,64,256]{3,2,1,0:T(8,128)(2,1)S(1)} %copy-done.7), channel_id=1, source_target_pairs={{0,8},{4,12},{8,0},{12,4},{1,9},{5,13},{9,1},{13,5},{2,10},{6,14},... | collective-permute-start | bytes 786440 | tf_op jit(solution)/shard_map/ppermute | solution.py:420
  67.0 16.4 %collective-permute-start.6 = (bf16[2,4,64,256]{3,2,1,0:T(8,128)(2,1)S(1)}, bf16[2,4,64,256]{3,2,1,0:T(8,128)(2,1)}, u32[]{:S(2)}, u32[]{:S(2)}) collective-permute-start(bf16[2,4,64,256]{3,2,1,0:T(8,128)(2,1)S(1)} %copy-done.7), channel_id=1, source_target_pairs={{0,12},{4,0},{8,4},{12,8},{1,13},{5,1},{9,5},{13,9},{2,14},{6,2},{... | collective-permute-start | bytes 786440 | tf_op jit(solution)/shard_map/ppermute | solution.py:420
  68.1 16.5 %collective-permute-start.4 = (bf16[2,4,64,256]{3,2,1,0:T(8,128)(2,1)S(1)}, bf16[2,4,64,256]{3,2,1,0:T(8,128)(2,1)}, u32[]{:S(2)}, u32[]{:S(2)}) collective-permute-start(bf16[2,4,64,256]{3,2,1,0:T(8,128)(2,1)S(1)} %copy-done.7), channel_id=1, source_target_pairs={{0,4},{4,8},{8,12},{12,0},{1,5},{5,9},{9,13},{13,1},{2,6},{6,10},{... | collective-permute-start | bytes 786440 | tf_op jit(solution)/shard_map/ppermute | solution.py:420
  69.0 15.6 %collective-permute-start.8 = (bf16[2,4,64,256]{3,2,1,0:T(8,128)(2,1)S(1)}, bf16[2,4,64,256]{3,2,1,0:T(8,128)(2,1)S(1)}, u32[]{:S(2)}, u32[]{:S(2)}) collective-permute-start(bf16[2,4,64,256]{3,2,1,0:T(8,128)(2,1)S(1)} %copy-done.7), channel_id=1, source_target_pairs={{0,16},{16,0},{1,17},{17,1},{2,18},{18,2},{3,19},{19,3},{4,20},{20... | collective-permute-start | bytes 786440 | tf_op jit(solution)/shard_map/ppermute | solution.py:427
  79.3 16.1 %collective-permute-start.12 = (bf16[4,4,64,256]{3,2,1,0:T(8,128)(2,1)}, bf16[4,4,64,256]{3,2,1,0:T(8,128)(2,1)}, u32[]{:S(2)}, u32[]{:S(2)}) collective-permute-start(bf16[4,4,64,256]{3,2,1,0:T(8,128)(2,1)} %shard_map.108.refs_4_), channel_id=1, source_target_pairs={{0,16},{16,0},{1,17},{17,1},{2,18},{18,2},{3,19},{19,3},{4,20},{20... | collective-permute-start | bytes 1572872 | tf_op jit(solution)/shard_map/ppermute | solution.py:427
  83.4 12.0 %collective-permute-start.10 = (bf16[2,4,64,256]{3,2,1,0:T(8,128)(2,1)}, bf16[2,4,64,256]{3,2,1,0:T(8,128)(2,1)}, u32[]{:S(2)}, u32[]{:S(2)}) collective-permute-start(bf16[2,4,64,256]{3,2,1,0:T(8,128)(2,1)} %collective-permute-done.5.refs_2_), channel_id=1, source_target_pairs={{0,16},{16,0},{1,17},{17,1},{2,18},{18,2},{3,19},{19,3},{4,20},{20... | collective-permute-start | bytes 786440 | tf_op jit(solution)/shard_map/ppermute | solution.py:427
  84.5 10.9 %collective-permute-start.11 = (bf16[2,4,64,256]{3,2,1,0:T(8,128)(2,1)}, bf16[2,4,64,256]{3,2,1,0:T(8,128)(2,1)}, u32[]{:S(2)}, u32[]{:S(2)}) collective-permute-start(bf16[2,4,64,256]{3,2,1,0:T(8,128)(2,1)} %collective-permute-done.6.refs_3_), channel_id=1, source_target_pairs={{0,16},{16,0},{1,17},{17,1},{2,18},{18,2},{3,19},{19,3},{4,20},{20... | collective-permute-start | bytes 786440 | tf_op jit(solution)/shard_map/ppermute | solution.py:427
  84.6 0.7 copy-start.12
  84.6 10.9 %collective-permute-start.9 = (bf16[2,4,64,256]{3,2,1,0:T(8,128)(2,1)}, bf16[2,4,64,256]{3,2,1,0:T(8,128)(2,1)S(1)}, u32[]{:S(2)}, u32[]{:S(2)}) collective-permute-start(bf16[2,4,64,256]{3,2,1,0:T(8,128)(2,1)} %collective-permute-done.4.refs_1_), channel_id=1, source_target_pairs={{0,16},{16,0},{1,17},{17,1},{2,18},{18,2},{3,19},{19,3},{4,20},{20... | collective-permute-start | bytes 786440 | tf_op jit(solution)/shard_map/ppermute | solution.py:427
  85.3 10.2 %collective-permute-start.13 = (bf16[4,4,64,256]{3,2,1,0:T(8,128)(2,1)}, bf16[4,4,64,256]{3,2,1,0:T(8,128)(2,1)}, u32[]{:S(2)}, u32[]{:S(2)}) collective-permute-start(bf16[4,4,64,256]{3,2,1,0:T(8,128)(2,1)} %collective-permute-done.7.refs_5_), channel_id=1, source_target_pairs={{0,16},{16,0},{1,17},{17,1},{2,18},{18,2},{3,19},{19,3},{4,20},{20... | collective-permute-start | bytes 1572872 | tf_op jit(solution)/shard_map/ppermute | solution.py:427
  86.9 36.1 %all-to-all-start.3 = ((bf16[128,16,128]{2,1,0:T(8,128)(2,1)}), bf16[128,16,128]{2,1,0:T(8,128)(2,1)S(1)}, u32[]{:S(2)}, u32[]{:S(2)}) async-start(bf16[128,16,128]{2,1,0:T(8,128)(2,1)} %shard_map.110), calls=%async_computation.3 | async-start | bytes 1048576 | tf_op jit(solution)/shard_map/all_to_all | solution.py:445
  95.5 0.7 copy-start.13
  123.0 7.4 %copy-start.4 = (f32[1024,16]{0,1:T(8,128)S(1)}, f32[1024,16]{0,1:T(8,128)}, u32[]{:S(2)}) copy-start(f32[1024,16]{0,1:T(8,128)} %param.11) | copy-start | bytes 196612
  123.0 0.8 copy-start.1
  123.8 19.7 %all-to-all-start.4 = ((bf16[8,64,1024]{2,1,0:T(8,128)(2,1)}), bf16[8,64,1024]{2,1,0:T(8,128)(2,1)S(1)}, u32[]{:S(2)}, u32[]{:S(2)}) async-start(bf16[8,64,1024]{2,1,0:T(8,128)(2,1)} %shard_map.112), calls=%async_computation.4 | async-start | bytes 2097152 | tf_op jit(solution)/shard_map/all_to_all | solution.py:447
  130.4 1.0 copy-start.2

commit v3 on v2

--- a/solution.py
+++ b/solution.py
@@ -20,7 +20,7 @@
 ALL = ("x", "core", "y", "zh", "zl")
 CTX = ("x", "core")
 TP = ("y", "zh", "zl")
-HEADS = ("x", "zh")
+HEADS = ("zl", "x")
 VMEM = pl.BlockSpec(memory_space=pltpu.VMEM)
 SMEM = pl.BlockSpec(memory_space=pltpu.SMEM)
 ANY = pl.BlockSpec(memory_space=pl.ANY)
@@ -124,45 +124,44 @@
     )(own, gain)
 
 
-def attn_kernel(meta_ref, rows_ref, all_ref, *refs):
+def attn_kernel(meta_ref, all_ref, *refs):
     own_refs, other_refs, refs = refs[:6], refs[6:12], refs[12:]
-    out_ref, m_ref, acc_ref, s_ref, q_ref, kv_ref, vt_ref, o_ref, q_sem, sems, o_sem = refs
-    core, y, zl = meta_ref[2, 0], meta_ref[3, 0], meta_ref[3, 1]
+    out_ref, m_ref, acc_ref, s_ref, q_ref, kv_ref, vt_ref, o_ref, q_sem, sem, o_sem = refs
+    core, y, zh = meta_ref[1, 0], meta_ref[1, 1], meta_ref[1, 2]
+    for group, of in ((own_refs, core), (other_refs, 1 - core)):
+        for dy in range(4):
+            for dz in range(2):
+                for zl in range(2):
+                    piece = group[4 + dz].at[dy] if zl else group[dy].at[dz]
+                    place = kv_ref.at[:, of, lax.rem(y + 4 - dy, 4), lax.rem(zh + dz, 2), zl]
+                    pltpu.make_async_copy(piece, place, sem).start()
     pltpu.make_async_copy(all_ref.at[:, :, pl.ds(0, 1024)], q_ref, q_sem).start()
-    for x in range(4):
-        for group, of in ((own_refs, core), (other_refs, 1 - core)):
-            for dy in range(4):
-                for dz in range(2):
-                    piece = group[dy].at[dz] if x < 2 else group[4 + dz].at[dy]
-                    pltpu.make_async_copy(
-                        piece.at[pl.ds(2 * (x % 2), 2)],
-                        kv_ref.at[2 * x + of, lax.rem(y + 4 - dy, 4), :, lax.rem(zl + dz, 2)],
-                        sems.at[2 * x + of],
-                    ).start()
-
-    def arrive(w):
-        pltpu.make_async_copy(kv_ref.at[w], kv_ref.at[w], sems.at[w]).wait()
+
+    def tile(j):
+        return kv_ref[j // 2, j % 2].reshape(TK, 2 * HD)
 
     def prepare(w):
-        arrive(w)
-        vt_ref[w, :HD, :] = kv_ref[w].reshape(TK, 2 * HD)[:, HD:].T
+        vt_ref[w, :HD, :] = tile(w)[:, HD:].T
         vt_ref[w, HD:, :] = jnp.ones((16, TK), BF16)
 
     def scores(i, j, slot):
-        k = kv_ref[j].reshape(TK, 2 * HD)[:, :HD]
+        k = tile(j)[:, :HD]
         for g in range(NG):
             heads = range(4 * (g % 2), 4 * (g % 2) + 4)
-            q = [q_ref[2 * i + g // 2, :, a * HD : (a + 1) * HD] for a in heads]
+            q = [q_ref[4 * (g // 2) + i, :, a * HD : (a + 1) * HD] for a in heads]
             s_ref[slot, g] = dot(k, jnp.concatenate(q, axis=0), ((1,), (1,)))
 
-    def absorb(i, j, slot, masked):
+    def absorb(i, j, slot, causal, begins):
         v = vt_ref[j]
+        key = lax.broadcasted_iota(jnp.int32, (TK, RG), 0)
+        token = lax.broadcasted_iota(jnp.int32, (1, RG), 1) % CHUNK
+        at = (2 * i + core - j) * TK + y * 256 + zh * 128 + token
         for g in range(NG):
             s = s_ref[slot, g]
-            if masked:
-                kpos = j * TK + lax.broadcasted_iota(jnp.int32, (TK, RG), 0)
-                seen = (kpos <= rows_ref[i, g, 0:1]) & (kpos >= rows_ref[i, g, 1:2])
-                s = jnp.where(seen, s, NEG)
+            if causal:
+                s = jnp.where(key <= at + CHUNK * (g // 2), s, NEG)
+            if begins:
+                s = jnp.where(key >= meta_ref[0, i] - j * TK, s, NEG)
             before = m_ref[g]
             top = jnp.maximum(before, jnp.max(s, axis=0, keepdims=True))
             p = jnp.exp2((s - top) * SCORE_EXP2)
@@ -174,31 +173,34 @@
         m_ref[...] = jnp.full_like(m_ref, NEG)
         acc_ref[...] = jnp.zeros_like(acc_ref)
 
-    def window(i):
-        return 2 * i + core
-
     def body(carry):
         i, j, slot = carry
-        last = j == window(i)
+        last = j == 2 * i + core
         i_next = jnp.where(last, i + 1, i)
         i_read = jnp.minimum(i_next, 3)
         j_next = jnp.where(last, meta_ref[0, i_read] // TK, j + 1)
-        edge = last | (j * TK < meta_ref[1, i])
+        begins = j * TK < meta_ref[0, i]
+        causal = last & jnp.logical_not(begins)
 
         @pl.when(last & (i < 3))
         def _():
             for n in range(2):
-                prepare(window(i) + 1 + n)
-
-        @pl.when(edge)
+                prepare(2 * i + core + 1 + n)
+
+        @pl.when(begins)
         def _():
             scores(i_read, j_next, 1 - slot)
-            absorb(i, j, slot, True)
-
-        @pl.when(jnp.logical_not(edge))
+            absorb(i, j, slot, True, True)
+
+        @pl.when(causal)
         def _():
             scores(i_read, j_next, 1 - slot)
-            absorb(i, j, slot, False)
+            absorb(i, j, slot, True, False)
+
+        @pl.when(jnp.logical_not(begins | causal))
+        def _():
+            scores(i_read, j_next, 1 - slot)
+            absorb(i, j, slot, False, False)
 
         @pl.when(last)
         def _():
@@ -206,13 +208,14 @@
                 out = (acc_ref[g, :HD] * (1.0 / acc_ref[g, HD : HD + 1])).T.astype(BF16)
                 for a in range(4):
                     low = (4 * (g % 2) + a) * HD
-                    o_ref[i, g // 2, :, low : low + HD] = out[a * CHUNK : (a + 1) * CHUNK]
-            pltpu.make_async_copy(o_ref.at[i], out_ref.at[pl.ds(2 * i, 2)], o_sem.at[i]).start()
+                    o_ref[g // 2, i, :, low : low + HD] = out[a * CHUNK : (a + 1) * CHUNK]
+            pltpu.make_async_copy(o_ref.at[:, i], out_ref.at[:, i], o_sem.at[i]).start()
             reset()
 
         return (i_next, j_next, 1 - slot)
 
     reset()
+    pltpu.make_async_copy(kv_ref, kv_ref, sem).wait()
     prepare(0)
 
     @pl.when(core == 1)
@@ -223,38 +226,33 @@
     start = meta_ref[0, 0] // TK
     scores(0, start, 0)
     lax.while_loop(lambda carry: carry[0] < 4, body, (jnp.int32(0), start, jnp.int32(0)))
-
-    @pl.when(core == 0)
-    def _():
-        arrive(7)
-
     for n in range(4):
-        pltpu.make_async_copy(o_ref.at[n], out_ref.at[pl.ds(0, 2)], o_sem.at[n]).wait()
-
-
-def attend(meta, rows, heads, own, other):
+        pltpu.make_async_copy(o_ref.at[:, n], out_ref.at[:, n], o_sem.at[n]).wait()
+
+
+def attend(meta, heads, own, other):
     return pl.pallas_call(
         attn_kernel,
-        out_shape=jax.ShapeDtypeStruct((8, CHUNK, 1024), BF16),
-        in_specs=[SMEM, VMEM] + [ANY] * 13,
+        out_shape=jax.ShapeDtypeStruct((2, 4, CHUNK, 1024), BF16),
+        in_specs=[SMEM] + [ANY] * 13,
         out_specs=ANY,
         scratch_shapes=[
             pltpu.VMEM((NG, 1, RG), F32),
             pltpu.VMEM((NG, HD + 16, RG), F32),
             pltpu.VMEM((2, NG, TK, RG), F32),
             pltpu.VMEM((8, CHUNK, 1024), BF16),
-            pltpu.VMEM((8, 4, 2, 2, CHUNK, 2 * HD), BF16),
+            pltpu.VMEM((4, 2, 4, 2, 2, CHUNK, 2 * HD), BF16),
             pltpu.VMEM((8, HD + 16, TK), BF16),
-            pltpu.VMEM((4, 2, CHUNK, 1024), BF16),
+            pltpu.VMEM((2, 4, CHUNK, 1024), BF16),
             pltpu.SemaphoreType.DMA,
-            pltpu.SemaphoreType.DMA((8,)),
+            pltpu.SemaphoreType.DMA,
             pltpu.SemaphoreType.DMA((4,)),
         ],
         compiler_params=pltpu.CompilerParams(vmem_limit_bytes=60 << 20),
         cost_estimate=pl.CostEstimate(
             flops=12_000_000_000, bytes_accessed=6 << 20, transcendentals=5_000_000
         ),
-    )(meta, rows, heads, *own, *other)
+    )(meta, heads, *own, *other)
 
 
 def one_minus_exp(u):
@@ -324,7 +322,7 @@
         scratch_shapes=[pltpu.VMEM((16, CHUNK, 128), F32), pltpu.VMEM((16, 8, 128), F32)],
         compiler_params=SMALL,
         cost_estimate=pl.CostEstimate(
-            flops=2 * 32 * CHUNK * 16384, bytes_accessed=3 << 20, transcendentals=50_000
+            flops=30_000_000_000, bytes_accessed=3 << 20, transcendentals=50_000
         ),
     )(place, x, dec, b)
 
@@ -403,8 +401,8 @@
 def per_device(
     mamba_in, state_in_b, state_out_c, step_decay, skip_gain, queries, keys, values, doc_ids
 ):
-    core, y, zl = lax.axis_index("core"), lax.axis_index("y"), lax.axis_index("zl")
-    z = 2 * lax.axis_index("zh") + zl
+    core, y, zh = lax.axis_index("core"), lax.axis_index("y"), lax.axis_index("zh")
+    z = 2 * zh + lax.axis_index("zl")
     spot = jnp.stack([y, z, 4 * y + z]).astype(jnp.int32)
     b, c = state_in_b.T, state_out_c.T
 
@@ -413,7 +411,7 @@
     dec, heads = lax.optimization_barrier((split_decay(step_decay.T, skip_gain[None]), heads))
     dec = lax.all_to_all(dec, TP, 0, 0, tiled=True).reshape(HM, 2 * CHUNK)
     def along_z(block):
-        return [block, lax.ppermute(block, "zl", [(0, 1), (1, 0)])]
+        return [block, lax.ppermute(block, "zh", [(0, 1), (1, 0)])]
 
     def along_y(block):
         steps = [[(n, (n + k) % 4) for n in range(4)] for k in range(1, 4)]
@@ -421,29 +419,21 @@
 
     lead, tail = pick_kv(heads)
     lead, tail = stack(along_z(lead)), stack(along_y(tail))
-    dec, lead, tail = lax.optimization_barrier((dec, lead, tail))
     states = chunk_states(spot, mamba_in, dec, b)
+    states, lead, tail = lax.optimization_barrier((states, lead, tail))
     own = along_y(lead) + along_z(tail)
     other = [lax.ppermute(block, "core", [(0, 1), (1, 0)]) for block in own]
     states = lax.all_to_all(states, ALL, 0, 0, tiled=True)
 
-    blocks = jnp.arange(64, dtype=jnp.int32)
-    starts = jnp.sum(doc_ids[None] < doc_ids[:, None], axis=1).astype(jnp.int32) * 128
-    row = jnp.arange(1024, dtype=jnp.int32)
-    place = (2 * jnp.arange(4)[:, None] + core) * 1024 + row % 64
-    place = place + (4 * y + 2 * (row // 512) + zl) * CHUNK
-    first = jnp.sum(
-        jnp.where(place[:, :, None] // 128 == blocks, starts[None, None], 0), axis=2
-    )
-    rows = jnp.stack([place, first], axis=1).astype(jnp.int32)
-    low, high = jnp.min(first, axis=1), jnp.max(first, axis=1)
-    rows = rows.reshape(4, 2, NG, RG).transpose(0, 2, 1, 3)
-    ids = jnp.stack([y, zl, y, zl])
-    meta = jnp.stack([low, high, jnp.broadcast_to(core, (4,)), ids]).astype(jnp.int32)
+    blocks = jnp.arange(64)
+    mine = (2 * jnp.arange(4)[:, None] + core) * 8 + 2 * y + zh
+    doc = jnp.sum(jnp.where(blocks[None] == mine, doc_ids[None], 0), axis=1)
+    first = jnp.sum(doc_ids[None] < doc[:, None], axis=1) * 128
+    meta = jnp.stack([first, jnp.stack([core, y, zh, zh])]).astype(jnp.int32)
     entering = entering_states(states)
     entering, meta = lax.optimization_barrier((entering, meta))
     entering = lax.all_to_all(entering, ALL, 0, 0, tiled=True)
-    attn = attend(meta, rows, heads, own, other)
+    attn = attend(meta, heads, own, other).reshape(8, CHUNK, 1024)
     attn = lax.all_to_all(attn, HEADS, 0, 0, tiled=True)
     mamba_out = chunk_outputs(spot, mamba_in, dec, b, c, entering)
     return (mamba_out, join_heads(attn))

time: 146 us -> 151 us (1.034)
  the two profiles are of different devices: /device:TPU:0 before, /device:TPU:1 now
where the time goes in v3:
time: 151 us; the launch traced here: 150 us
  Pallas kernels  55.9 us (37%)
  starting transfers between devices  50.3 us (33%)
  waiting for transfers between devices  36.6 us (24%)
  local copies, waits for them, and re-layouts  5.28 us (3%)
    pallas_call x1, Pallas kernels, attend(): pl.pallas_call(attn_kernel, out_shape=jax.ShapeDtypeStruct((2, 4, CHUNK,...  34.1 us
    all_to_all x1, waiting for transfers between devices, per_device(): lax.all_to_all(split_heads(queries, keys, values), HEADS, 0, 0, tiled=True)  18 us
    ppermute x6, waiting for transfers between devices, along_y(): return [block] + [lax.ppermute(block, 'y', step) for step in steps]  13.2 us
    all_to_all x1, starting transfers between devices, per_device(): states = lax.all_to_all(states, ALL, 0, 0, tiled=True)  7.56 us
    ppermute x6, starting transfers between devices, along_y(): return [block] + [lax.ppermute(block, 'y', step) for step in steps]  7.49 us
    all_to_all x1, starting transfers between devices, per_device(): dec = lax.all_to_all(dec, TP, 0, 0, tiled=True).reshape(HM, 2 * CHUNK)  7.31 us
    all_to_all x1, starting transfers between devices, per_device(): entering = lax.all_to_all(entering, ALL, 0, 0, tiled=True)  6.79 us
    pallas_call x1, Pallas kernels, chunk_outputs(): pl.pallas_call(output_kernel, out_shape=jax.ShapeDtypeStruct((CHUNK, 1638...  6.39 us
  transfers between devices with their start and end apart: 19, of which 5 were waited for; matrix products, arithmetic and copies ran while one was open for 1% of the time, Pallas kernels for 34%

profile of v3, /device:TPU:1, one launch (start us, length us, event | category | flops | bytes accessed | tf_op | source)
XLA Modules:
  0.0 150.0 jit_solution(5979056456276673223)
XLA Ops:
  0.7 2.5 %shard_map.105 = bf16[8,64,1280]{2,1,0:T(8,128)(2,1)} custom-call(bf16[64,8192]{1,0:T(8,128)(2,1)} %q_ref.1, bf16[64,1024]{1,0:T(8,128)(2,1)} %k_ref.1, bf16[64,1024]{1,0:T(8,128)(2,1)} %v_ref.1), custom_call_target="tpu_custom_call" | custom-call | tf_op jit(solution)/shard_map/pallas_call | solution.py:47
  3.1 6.3 %all-to-all-start = ((bf16[8,64,1280]{2,1,0:T(8,128)(2,1)}), bf16[8,64,1280]{2,1,0:T(8,128)(2,1)}, u32[]{:S(2)}, u32[]{:S(2)}) async-start(bf16[8,64,1280]{2,1,0:T(8,128)(2,1)} %shard_map.105), calls=%async_computation | async-start | bytes 2621440 | tf_op jit(solution)/shard_map/all_to_all | solution.py:409
  9.5 0.8 shard_map.104
  10.3 18.0 %all-to-all-done.i_ref.all_ref = bf16[8,64,1280]{2,1,0:T(8,128)(2,1)} async-done(((bf16[8,64,1280]{2,1,0:T(8,128)(2,1)}), bf16[8,64,1280]{2,1,0:T(8,128)(2,1)}, u32[]{:S(2)}, u32[]{:S(2)}) %all-to-all-start) | async-done | bytes 1310752 | tf_op jit(solution)/shard_map/all_to_all | solution.py:409
  28.2 7.3 %all-to-all-start.1 = ((f32[16,16,128]{2,1,0:T(8,128)}), f32[16,16,128]{2,1,0:T(8,128)S(1)}, u32[]{:S(2)}, u32[]{:S(2)}) async-start(f32[16,16,128]{2,1,0:T(8,128)} %shard_map.104), calls=%async_computation.1 | async-start | bytes 262144 | tf_op jit(solution)/shard_map/all_to_all | solution.py:412
  35.5 0.1 pad_add_fusion.1.place_ref
  35.6 1.7 %shard_map.107 = (bf16[4,64,256]{2,1,0:T(8,128)(2,1)}, bf16[4,64,256]{2,1,0:T(8,128)(2,1)}) custom-call(bf16[8,64,1280]{2,1,0:T(8,128)(2,1)} %all-to-all-done.i_ref.all_ref), custom_call_target="tpu_custom_call" | custom-call | tf_op jit(solution)/shard_map/pallas_call | solution.py:69
  37.3 2.6 %collective-permute-start.3 = (bf16[4,64,256]{2,1,0:T(8,128)(2,1)}, bf16[4,64,256]{2,1,0:T(8,128)(2,1)S(1)}, u32[]{:S(2)}, u32[]{:S(2)}) collective-permute-start(bf16[4,64,256]{2,1,0:T(8,128)(2,1)} %get-tuple-element.14.refs_0_), channel_id=1, source_target_pairs={{0,12},{4,0},{8,4},{12,8},{1,13},{5,1},{9,5},{13,9},{2,14},{6,2},{... | collective-permute-start | bytes 393224 | tf_op jit(solution)/shard_map/ppermute | solution.py:418
  40.0 0.6 collective-permute-start.2
  40.5 0.6 collective-permute-start.1
  41.1 2.7 %collective-permute-start = (bf16[4,64,256]{2,1,0:T(8,128)(2,1)}, bf16[4,64,256]{2,1,0:T(8,128)(2,1)S(1)}, u32[]{:S(2)}, u32[]{:S(2)}) collective-permute-start(bf16[4,64,256]{2,1,0:T(8,128)(2,1)} %get-tuple-element.13.refs_0_), channel_id=1, source_target_pairs={{0,2},{2,0},{1,3},{3,1},{4,6},{6,4},{5,7},{7,5},{8,10},{10,8},{9,1... | collective-permute-start | bytes 393224 | tf_op jit(solution)/shard_map/ppermute | solution.py:414
  43.8 0.0 all-to-all-done.1
  43.8 4.6 %shard_map.106 = bf16[128,24,128]{2,1,0:T(8,128)(2,1)} custom-call(s32[3]{0:T(128)S(1)} %pad_add_fusion.1.place_ref, bf16[64,16384]{1,0:T(8,128)(2,1)S(1)} %copy-done, f32[256,128]{1,0:T(8,128)S(1)} %bitcast.15, f32[16,1024]{1,0:T(8,128)S(1)} %bitcast.17), custom_call_target="tpu_custom_call" | custom-call | flops 30000001024 | bytes 3145728 | tf_op jit(solution)/shard_map/pallas_call | solution.py:317
  48.4 0.0 collective-permute-done.refs_1_
  48.4 0.7 copy-done.7
  49.1 1.7 %shard_map.108.refs_0_ = bf16[2,4,64,256]{3,2,1,0:T(8,128)(2,1)} custom-call(bf16[4,64,256]{2,1,0:T(8,128)(2,1)} %get-tuple-element.13.refs_0_, bf16[4,64,256]{2,1,0:T(8,128)(2,1)} %copy-done.7), custom_call_target="tpu_custom_call" | custom-call | tf_op jit(solution)/shard_map/pallas_call | solution.py:84
  50.8 0.0 collective-permute-done.3.refs_3_
  50.8 0.0 collective-permute-done.2.refs_2_
  50.8 0.0 collective-permute-done.1.refs_1_
  50.8 0.6 copy-done.8
  51.4 0.0 copy-done.9
  51.5 0.7 copy-done.10
  52.1 1.9 %shard_map.109.refs_4_ = bf16[4,4,64,256]{3,2,1,0:T(8,128)(2,1)} custom-call(bf16[4,64,256]{2,1,0:T(8,128)(2,1)} %get-tuple-element.14.refs_0_, bf16[4,64,256]{2,1,0:T(8,128)(2,1)} %copy-done.10, bf16[4,64,256]{2,1,0:T(8,128)(2,1)} %copy-done.9, bf16[4,64,256]{2,1,0:T(8,128)(2,1)} %copy-done.8), custom_call_target="tpu_custom_call" | custom-call | tf_op jit(solution)/shard_map/pallas_call | solution.py:84
  54.1 7.6 %all-to-all-start.2 = ((bf16[128,24,128]{2,1,0:T(8,128)(2,1)}), bf16[128,24,128]{2,1,0:T(8,128)(2,1)S(1)}, u32[]{:S(2)}, u32[]{:S(2)}) async-start(bf16[128,24,128]{2,1,0:T(8,128)(2,1)} %shard_map.106), calls=%async_computation.2 | async-start | bytes 1572864 | tf_op jit(solution)/shard_map/all_to_all | solution.py:426
  61.6 3.4 %collective-permute-start.7 = (bf16[4,4,64,256]{3,2,1,0:T(8,128)(2,1)}, bf16[4,4,64,256]{3,2,1,0:T(8,128)(2,1)S(1)}, u32[]{:S(2)}, u32[]{:S(2)}) collective-permute-start(bf16[4,4,64,256]{3,2,1,0:T(8,128)(2,1)} %shard_map.109.refs_4_), channel_id=1, source_target_pairs={{0,2},{2,0},{1,3},{3,1},{4,6},{6,4},{5,7},{7,5},{8,10},{10,8},{9,1... | collective-permute-start | bytes 1572872 | tf_op jit(solution)/shard_map/ppermute | solution.py:414
  65.0 0.2 select_reduce_fusion
  65.2 0.2 convert_reduce_fusion
  65.4 0.7 collective-permute-start.8
  66.1 2.6 %collective-permute-start.6 = (bf16[2,4,64,256]{3,2,1,0:T(8,128)(2,1)S(1)}, bf16[2,4,64,256]{3,2,1,0:T(8,128)(2,1)S(1)}, u32[]{:S(2)}, u32[]{:S(2)}) collective-permute-start(bf16[2,4,64,256]{3,2,1,0:T(8,128)(2,1)S(1)} %copy-done.6), channel_id=1, source_target_pairs={{0,12},{4,0},{8,4},{12,8},{1,13},{5,1},{9,5},{13,9},{2,14},{6,2},{... | collective-permute-start | bytes 786440 | tf_op jit(solution)/shard_map/ppermute | solution.py:418
  68.7 0.4 collective-permute-start.5
  69.2 0.6 collective-permute-start.4
  69.8 0.1 add_bitcast_fusion
  69.9 0.6 pad_add_fusion.meta_ref
  70.5 0.0 collective-permute-done.8.refs_6_
  70.5 0.9 collective-permute-start.12
  71.4 6.8 %collective-permute-done.6.refs_3_ = bf16[2,4,64,256]{3,2,1,0:T(8,128)(2,1)S(1)} collective-permute-done((bf16[2,4,64,256]{3,2,1,0:T(8,128)(2,1)S(1)}, bf16[2,4,64,256]{3,2,1,0:T(8,128)(2,1)S(1)}, u32[]{:S(2)}, u32[]{:S(2)}) %collective-permute-start.6) | collective-permute-done | bytes 262176 | tf_op jit(solution)/shard_map/ppermute | solution.py:418
  78.2 0.6 collective-permute-start.11
  78.8 1.6 %collective-permute-done.5.refs_2_ = bf16[2,4,64,256]{3,2,1,0:T(8,128)(2,1)} collective-permute-done((bf16[2,4,64,256]{3,2,1,0:T(8,128)(2,1)S(1)}, bf16[2,4,64,256]{3,2,1,0:T(8,128)(2,1)}, u32[]{:S(2)}, u32[]{:S(2)}) %collective-permute-start.5) | collective-permute-done | bytes 262176 | tf_op jit(solution)/shard_map/ppermute | solution.py:418
  80.4 0.6 collective-permute-start.10
  81.0 4.8 %collective-permute-done.4.refs_1_ = bf16[2,4,64,256]{3,2,1,0:T(8,128)(2,1)} collective-permute-done((bf16[2,4,64,256]{3,2,1,0:T(8,128)(2,1)S(1)}, bf16[2,4,64,256]{3,2,1,0:T(8,128)(2,1)}, u32[]{:S(2)}, u32[]{:S(2)}) %collective-permute-start.4) | collective-permute-done | bytes 262176 | tf_op jit(solution)/shard_map/ppermute | solution.py:418
  85.8 0.5 collective-permute-start.9
  86.3 0.0 collective-permute-done.7.refs_5_
  86.3 0.1 collective-permute-start.13
  86.4 0.0 all-to-all-done.2.s_ref
  86.4 1.2 shard_map.110
  87.6 0.0 copy-done.14
  87.6 6.8 %all-to-all-start.3 = ((bf16[128,16,128]{2,1,0:T(8,128)(2,1)}), bf16[128,16,128]{2,1,0:T(8,128)(2,1)S(1)}, u32[]{:S(2)}, u32[]{:S(2)}) async-start(bf16[128,16,128]{2,1,0:T(8,128)(2,1)} %shard_map.110), calls=%async_computation.3 | async-start | bytes 1048576 | tf_op jit(solution)/shard_map/all_to_all | solution.py:435
  94.4 0.0 collective-permute-done.11.refs_9_
  94.4 0.0 collective-permute-done.10.refs_8_
  94.4 0.0 collective-permute-done.9.refs_7_
  94.4 0.0 collective-permute-done.12.refs_10_
  94.5 0.0 collective-permute-done.13.refs_11_
  94.5 0.7 copy-done.16
  95.1 0.2 copy-done.12
  95.3 0.8 copy-done.13
  96.1 34.1 %shard_map.112 = bf16[2,4,64,1024]{3,2,1,0:T(8,128)(2,1)} custom-call(s32[2,4]{1,0:T(2,128)} %pad_add_fusion.meta_ref, bf16[8,64,1280]{2,1,0:T(8,128)(2,1)} %all-to-all-done.i_ref.all_ref, bf16[2,4,64,256]{3,2,1,0:T(8,128)(2,1)} %shard_map.108.refs_0_, bf16[2,4,64,256]{3,2,1,0:T(8,128)(2,1)} %collective-permute-done.4.refs_1_, ...), custom_call_target="tpu_custom_call" | custom-call | flops 12000000000 | bytes 6291456 | tf_op jit(solution)/shard_map/pallas_call | solution.py:234
  130.3 0.0 copy-start.3
  130.3 0.0 all-to-all-done.3.e_ref
  130.3 5.2 %all-to-all-start.4 = ((bf16[8,64,1024]{2,1,0:T(8,128)(2,1)}), bf16[8,64,1024]{2,1,0:T(8,128)(2,1)S(1)}, u32[]{:S(2)}, u32[]{:S(2)}) async-start(bf16[8,64,1024]{2,1,0:T(8,128)(2,1)} %bitcast.22), calls=%async_computation.4 | async-start | bytes 2097152 | tf_op jit(solution)/shard_map/all_to_all | solution.py:437
  135.5 0.0 copy-start.1
  135.5 1.6 %copy-done.1 = bf16[64,16384]{1,0:T(8,128)(2,1)S(1)} copy-done((bf16[64,16384]{1,0:T(8,128)(2,1)S(1)}, bf16[64,16384]{1,0:T(8,128)(2,1)}, u32[]{:S(2)}) %copy-start.1) | copy-done | bytes 2097176
  137.1 6.4 %shard_map.111 = bf16[64,16384]{1,0:T(8,128)(2,1)} custom-call(s32[3]{0:T(128)S(1)} %pad_add_fusion.1.place_ref, bf16[64,16384]{1,0:T(8,128)(2,1)S(1)} %copy-done.1, f32[256,128]{1,0:T(8,128)S(1)} %bitcast.16, f32[16,1024]{1,0:T(8,128)S(1)} %bitcast.18, f32[16,1024]{1,0:T(8,128)S(1)} %bitcast.19, bf16[128,16,128]{2,1,0:T(8,128)(2,1)S(1)} %all-to-all-done.3.e_ref), custom_call_target="tpu_custom_call" | custom-call | flops 167772160 | bytes 5242880 | tf_op jit(solution)/shard_map/pallas_call | solution.py:362
  143.5 5.4 %all-to-all-done.4.i_ref = bf16[8,64,1024]{2,1,0:T(8,128)(2,1)S(1)} async-done(((bf16[8,64,1024]{2,1,0:T(8,128)(2,1)}), bf16[8,64,1024]{2,1,0:T(8,128)(2,1)S(1)}, u32[]{:S(2)}, u32[]{:S(2)}) %all-to-all-start.4) | async-done | bytes 1048608 | tf_op jit(solution)/shard_map/all_to_all | solution.py:437
  149.0 1.0 shard_map.113
  (26 shorter events, 0.1 us)
Async XLA Ops:
  0.6 8.9 %copy-start.5 = (f32[16]{0:T(128)S(1)}, f32[16]{0:T(128)}, u32[]{:S(2)}) copy-start(f32[16]{0:T(128)} %param.13) | copy-start | bytes 196
  0.6 8.9 %copy-start.4 = (f32[1024,16]{0,1:T(8,128)S(1)}, f32[1024,16]{0,1:T(8,128)}, u32[]{:S(2)}) copy-start(f32[1024,16]{0,1:T(8,128)} %param.12) | copy-start | bytes 196612
  3.1 40.7 %copy-start = (bf16[64,16384]{1,0:T(8,128)(2,1)S(1)}, bf16[64,16384]{1,0:T(8,128)(2,1)}, u32[]{:S(2)}) copy-start(bf16[64,16384]{1,0:T(8,128)(2,1)} %x_ref.3) | copy-start | bytes 6291460
  3.1 40.7 %copy-start.2 = (f32[1024,16]{0,1:T(8,128)S(1)}, f32[1024,16]{0,1:T(8,128)}, u32[]{:S(2)}) copy-start(f32[1024,16]{0,1:T(8,128)} %param.10) | copy-start | bytes 196612
  3.1 25.1 %all-to-all-start = ((bf16[8,64,1280]{2,1,0:T(8,128)(2,1)}), bf16[8,64,1280]{2,1,0:T(8,128)(2,1)}, u32[]{:S(2)}, u32[]{:S(2)}) async-start(bf16[8,64,1280]{2,1,0:T(8,128)(2,1)} %shard_map.105), calls=%async_computation | async-start | bytes 2621440 | tf_op jit(solution)/shard_map/all_to_all | solution.py:409
  28.2 15.6 %all-to-all-start.1 = ((f32[16,16,128]{2,1,0:T(8,128)}), f32[16,16,128]{2,1,0:T(8,128)S(1)}, u32[]{:S(2)}, u32[]{:S(2)}) async-start(f32[16,16,128]{2,1,0:T(8,128)} %shard_map.104), calls=%async_computation.1 | async-start | bytes 262144 | tf_op jit(solution)/shard_map/all_to_all | solution.py:412
  37.3 13.4 %collective-permute-start.3 = (bf16[4,64,256]{2,1,0:T(8,128)(2,1)}, bf16[4,64,256]{2,1,0:T(8,128)(2,1)S(1)}, u32[]{:S(2)}, u32[]{:S(2)}) collective-permute-start(bf16[4,64,256]{2,1,0:T(8,128)(2,1)} %get-tuple-element.14.refs_0_), channel_id=1, source_target_pairs={{0,12},{4,0},{8,4},{12,8},{1,13},{5,1},{9,5},{13,9},{2,14},{6,2},{... | collective-permute-start | bytes 393224 | tf_op jit(solution)/shard_map/ppermute | solution.py:418
  40.0 10.8 %collective-permute-start.2 = (bf16[4,64,256]{2,1,0:T(8,128)(2,1)}, bf16[4,64,256]{2,1,0:T(8,128)(2,1)S(1)}, u32[]{:S(2)}, u32[]{:S(2)}) collective-permute-start(bf16[4,64,256]{2,1,0:T(8,128)(2,1)} %get-tuple-element.14.refs_0_), channel_id=1, source_target_pairs={{0,8},{4,12},{8,0},{12,4},{1,9},{5,13},{9,1},{13,5},{2,10},{6,14},... | collective-permute-start | bytes 393224 | tf_op jit(solution)/shard_map/ppermute | solution.py:418
  40.5 10.3 %collective-permute-start.1 = (bf16[4,64,256]{2,1,0:T(8,128)(2,1)}, bf16[4,64,256]{2,1,0:T(8,128)(2,1)S(1)}, u32[]{:S(2)}, u32[]{:S(2)}) collective-permute-start(bf16[4,64,256]{2,1,0:T(8,128)(2,1)} %get-tuple-element.14.refs_0_), channel_id=1, source_target_pairs={{0,4},{4,8},{8,12},{12,0},{1,5},{5,9},{9,13},{13,1},{2,6},{6,10},{... | collective-permute-start | bytes 393224 | tf_op jit(solution)/shard_map/ppermute | solution.py:418
  41.1 7.3 %collective-permute-start = (bf16[4,64,256]{2,1,0:T(8,128)(2,1)}, bf16[4,64,256]{2,1,0:T(8,128)(2,1)S(1)}, u32[]{:S(2)}, u32[]{:S(2)}) collective-permute-start(bf16[4,64,256]{2,1,0:T(8,128)(2,1)} %get-tuple-element.13.refs_0_), channel_id=1, source_target_pairs={{0,2},{2,0},{1,3},{3,1},{4,6},{6,4},{5,7},{7,5},{8,10},{10,8},{9,1... | collective-permute-start | bytes 393224 | tf_op jit(solution)/shard_map/ppermute | solution.py:414
  48.4 16.6 %copy-start.17 = (s32[64]{0:T(128)S(1)}, s32[64]{0:T(128)}, u32[]{:S(2)}) copy-start(s32[64]{0:T(128)} %param.17) | copy-start | bytes 772
  48.4 0.7 copy-start.7
  50.8 14.6 %copy-start.6 = (bf16[2,4,64,256]{3,2,1,0:T(8,128)(2,1)S(1)}, bf16[2,4,64,256]{3,2,1,0:T(8,128)(2,1)}, u32[]{:S(2)}) copy-start(bf16[2,4,64,256]{3,2,1,0:T(8,128)(2,1)} %shard_map.108.refs_0_) | copy-start | bytes 786436
  50.8 0.7 copy-start.8
  50.8 0.7 copy-start.9
  51.5 0.7 copy-start.10
  54.1 32.4 %all-to-all-start.2 = ((bf16[128,24,128]{2,1,0:T(8,128)(2,1)}), bf16[128,24,128]{2,1,0:T(8,128)(2,1)S(1)}, u32[]{:S(2)}, u32[]{:S(2)}) async-start(bf16[128,24,128]{2,1,0:T(8,128)(2,1)} %shard_map.106), calls=%async_computation.2 | async-start | bytes 1572864 | tf_op jit(solution)/shard_map/all_to_all | solution.py:426
  61.6 24.7 %collective-permute-start.7 = (bf16[4,4,64,256]{3,2,1,0:T(8,128)(2,1)}, bf16[4,4,64,256]{3,2,1,0:T(8,128)(2,1)S(1)}, u32[]{:S(2)}, u32[]{:S(2)}) collective-permute-start(bf16[4,4,64,256]{3,2,1,0:T(8,128)(2,1)} %shard_map.109.refs_4_), channel_id=1, source_target_pairs={{0,2},{2,0},{1,3},{3,1},{4,6},{6,4},{5,7},{7,5},{8,10},{10,8},{9,1... | collective-permute-start | bytes 1572872 | tf_op jit(solution)/shard_map/ppermute | solution.py:414
  65.4 5.1 %collective-permute-start.8 = (bf16[2,4,64,256]{3,2,1,0:T(8,128)(2,1)S(1)}, bf16[2,4,64,256]{3,2,1,0:T(8,128)(2,1)S(1)}, u32[]{:S(2)}, u32[]{:S(2)}) collective-permute-start(bf16[2,4,64,256]{3,2,1,0:T(8,128)(2,1)S(1)} %copy-done.6), channel_id=1, source_target_pairs={{0,16},{16,0},{1,17},{17,1},{2,18},{18,2},{3,19},{19,3},{4,20},{20... | collective-permute-start | bytes 786440 | tf_op jit(solution)/shard_map/ppermute | solution.py:425
  66.1 12.0 %collective-permute-start.6 = (bf16[2,4,64,256]{3,2,1,0:T(8,128)(2,1)S(1)}, bf16[2,4,64,256]{3,2,1,0:T(8,128)(2,1)S(1)}, u32[]{:S(2)}, u32[]{:S(2)}) collective-permute-start(bf16[2,4,64,256]{3,2,1,0:T(8,128)(2,1)S(1)} %copy-done.6), channel_id=1, source_target_pairs={{0,12},{4,0},{8,4},{12,8},{1,13},{5,1},{9,5},{13,9},{2,14},{6,2},{... | collective-permute-start | bytes 786440 | tf_op jit(solution)/shard_map/ppermute | solution.py:418
  68.7 11.6 %collective-permute-start.5 = (bf16[2,4,64,256]{3,2,1,0:T(8,128)(2,1)S(1)}, bf16[2,4,64,256]{3,2,1,0:T(8,128)(2,1)}, u32[]{:S(2)}, u32[]{:S(2)}) collective-permute-start(bf16[2,4,64,256]{3,2,1,0:T(8,128)(2,1)S(1)} %copy-done.6), channel_id=1, source_target_pairs={{0,8},{4,12},{8,0},{12,4},{1,9},{5,13},{9,1},{13,5},{2,10},{6,14},... | collective-permute-start | bytes 786440 | tf_op jit(solution)/shard_map/ppermute | solution.py:418
  69.2 16.6 %collective-permute-start.4 = (bf16[2,4,64,256]{3,2,1,0:T(8,128)(2,1)S(1)}, bf16[2,4,64,256]{3,2,1,0:T(8,128)(2,1)}, u32[]{:S(2)}, u32[]{:S(2)}) collective-permute-start(bf16[2,4,64,256]{3,2,1,0:T(8,128)(2,1)S(1)} %copy-done.6), channel_id=1, source_target_pairs={{0,4},{4,8},{8,12},{12,0},{1,5},{5,9},{9,13},{13,1},{2,6},{6,10},{... | collective-permute-start | bytes 786440 | tf_op jit(solution)/shard_map/ppermute | solution.py:418
  70.5 17.1 %copy-start.14 = (bf16[2,4,64,256]{3,2,1,0:T(8,128)(2,1)}, bf16[2,4,64,256]{3,2,1,0:T(8,128)(2,1)S(1)}, u32[]{:S(2)}) copy-start(bf16[2,4,64,256]{3,2,1,0:T(8,128)(2,1)S(1)} %collective-permute-done.8.refs_6_) | copy-start | bytes 786436
  70.5 24.0 %collective-permute-start.12 = (bf16[4,4,64,256]{3,2,1,0:T(8,128)(2,1)}, bf16[4,4,64,256]{3,2,1,0:T(8,128)(2,1)S(1)}, u32[]{:S(2)}, u32[]{:S(2)}) collective-permute-start(bf16[4,4,64,256]{3,2,1,0:T(8,128)(2,1)} %shard_map.109.refs_4_), channel_id=1, source_target_pairs={{0,16},{16,0},{1,17},{17,1},{2,18},{18,2},{3,19},{19,3},{4,20},{20... | collective-permute-start | bytes 1572872 | tf_op jit(solution)/shard_map/ppermute | solution.py:425
  78.2 9.4 %copy-start.15 = (bf16[2,4,64,256]{3,2,1,0:T(8,128)(2,1)}, bf16[2,4,64,256]{3,2,1,0:T(8,128)(2,1)S(1)}, u32[]{:S(2)}) copy-start(bf16[2,4,64,256]{3,2,1,0:T(8,128)(2,1)S(1)} %collective-permute-done.6.refs_3_) | copy-start | bytes 786436
  78.2 16.2 %collective-permute-start.11 = (bf16[2,4,64,256]{3,2,1,0:T(8,128)(2,1)S(1)}, bf16[2,4,64,256]{3,2,1,0:T(8,128)(2,1)}, u32[]{:S(2)}, u32[]{:S(2)}) collective-permute-start(bf16[2,4,64,256]{3,2,1,0:T(8,128)(2,1)S(1)} %collective-permute-done.6.refs_3_), channel_id=1, source_target_pairs={{0,16},{16,0},{1,17},{17,1},{2,18},{18,2},{3,19},{19,3},{4,20},{20... | collective-permute-start | bytes 786440 | tf_op jit(solution)/shard_map/ppermute | solution.py:425
  80.4 14.0 %collective-permute-start.10 = (bf16[2,4,64,256]{3,2,1,0:T(8,128)(2,1)}, bf16[2,4,64,256]{3,2,1,0:T(8,128)(2,1)}, u32[]{:S(2)}, u32[]{:S(2)}) collective-permute-start(bf16[2,4,64,256]{3,2,1,0:T(8,128)(2,1)} %collective-permute-done.5.refs_2_), channel_id=1, source_target_pairs={{0,16},{16,0},{1,17},{17,1},{2,18},{18,2},{3,19},{19,3},{4,20},{20... | collective-permute-start | bytes 786440 | tf_op jit(solution)/shard_map/ppermute | solution.py:425
  85.8 8.6 %collective-permute-start.9 = (bf16[2,4,64,256]{3,2,1,0:T(8,128)(2,1)}, bf16[2,4,64,256]{3,2,1,0:T(8,128)(2,1)S(1)}, u32[]{:S(2)}, u32[]{:S(2)}) collective-permute-start(bf16[2,4,64,256]{3,2,1,0:T(8,128)(2,1)} %collective-permute-done.4.refs_1_), channel_id=1, source_target_pairs={{0,16},{16,0},{1,17},{17,1},{2,18},{18,2},{3,19},{19,3},{4,20},{20... | collective-permute-start | bytes 786440 | tf_op jit(solution)/shard_map/ppermute | solution.py:425
  86.3 1.3 copy-start.11
  86.3 8.1 %collective-permute-start.13 = (bf16[4,4,64,256]{3,2,1,0:T(8,128)(2,1)S(1)}, bf16[4,4,64,256]{3,2,1,0:T(8,128)(2,1)S(1)}, u32[]{:S(2)}, u32[]{:S(2)}) collective-permute-start(bf16[4,4,64,256]{3,2,1,0:T(8,128)(2,1)S(1)} %collective-permute-done.7.refs_5_), channel_id=1, source_target_pairs={{0,16},{16,0},{1,17},{17,1},{2,18},{18,2},{3,19},{19,3},{4,20},{20... | collective-permute-start | bytes 1572872 | tf_op jit(solution)/shard_map/ppermute | solution.py:425
  87.6 42.7 %all-to-all-start.3 = ((bf16[128,16,128]{2,1,0:T(8,128)(2,1)}), bf16[128,16,128]{2,1,0:T(8,128)(2,1)S(1)}, u32[]{:S(2)}, u32[]{:S(2)}) async-start(bf16[128,16,128]{2,1,0:T(8,128)(2,1)} %shard_map.110), calls=%async_computation.3 | async-start | bytes 1048576 | tf_op jit(solution)/shard_map/all_to_all | solution.py:435
  94.4 0.7 copy-start.16
  94.4 0.9 copy-start.12
  95.3 0.8 copy-start.13
  130.3 5.3 %copy-start.3 = (f32[1024,16]{0,1:T(8,128)S(1)}, f32[1024,16]{0,1:T(8,128)}, u32[]{:S(2)}) copy-start(f32[1024,16]{0,1:T(8,128)} %param.11) | copy-start | bytes 196612
  130.3 18.7 %all-to-all-start.4 = ((bf16[8,64,1024]{2,1,0:T(8,128)(2,1)}), bf16[8,64,1024]{2,1,0:T(8,128)(2,1)S(1)}, u32[]{:S(2)}, u32[]{:S(2)}) async-start(bf16[8,64,1024]{2,1,0:T(8,128)(2,1)} %bitcast.22), calls=%async_computation.4 | async-start | bytes 2097152 | tf_op jit(solution)/shard_map/all_to_all | solution.py:437
  135.5 1.6 %copy-start.1 = (bf16[64,16384]{1,0:T(8,128)(2,1)S(1)}, bf16[64,16384]{1,0:T(8,128)(2,1)}, u32[]{:S(2)}) copy-start(bf16[64,16384]{1,0:T(8,128)(2,1)} %x_ref.3) | copy-start | bytes 6291460

commit v4 on v3

--- a/solution.py
+++ b/solution.py
@@ -126,7 +126,7 @@
 
 def attn_kernel(meta_ref, all_ref, *refs):
     own_refs, other_refs, refs = refs[:6], refs[6:12], refs[12:]
-    out_ref, m_ref, acc_ref, s_ref, q_ref, kv_ref, vt_ref, o_ref, q_sem, sem, o_sem = refs
+    out_ref, m_ref, acc_ref, *s_refs, q_ref, kv_ref, vt_ref, o_ref, q_sem, sem, o_sem = refs
     core, y, zh = meta_ref[1, 0], meta_ref[1, 1], meta_ref[1, 2]
     for group, of in ((own_refs, core), (other_refs, 1 - core)):
         for dy in range(4):
@@ -144,20 +144,20 @@
         vt_ref[w, :HD, :] = tile(w)[:, HD:].T
         vt_ref[w, HD:, :] = jnp.ones((16, TK), BF16)
 
-    def scores(i, j, slot):
+    def scores(i, j, slot, groups):
         k = tile(j)[:, :HD]
-        for g in range(NG):
+        for g in groups:
             heads = range(4 * (g % 2), 4 * (g % 2) + 4)
             q = [q_ref[4 * (g // 2) + i, :, a * HD : (a + 1) * HD] for a in heads]
-            s_ref[slot, g] = dot(k, jnp.concatenate(q, axis=0), ((1,), (1,)))
-
-    def absorb(i, j, slot, causal, begins):
+            s_refs[slot][g] = dot(k, jnp.concatenate(q, axis=0), ((1,), (1,)))
+
+    def absorb(i, j, slot, causal, begins, groups):
         v = vt_ref[j]
         key = lax.broadcasted_iota(jnp.int32, (TK, RG), 0)
         token = lax.broadcasted_iota(jnp.int32, (1, RG), 1) % CHUNK
         at = (2 * i + core - j) * TK + y * 256 + zh * 128 + token
-        for g in range(NG):
-            s = s_ref[slot, g]
+        for g in groups:
+            s = s_refs[slot][g]
             if causal:
                 s = jnp.where(key <= at + CHUNK * (g // 2), s, NEG)
             if begins:
@@ -169,6 +169,11 @@
             m_ref[g] = top
             acc_ref[g] = acc_ref[g] * fade + dot(v, p.astype(BF16))
 
+    def step(i_read, j_next, i, j, now, causal, begins):
+        for g in range(NG):
+            scores(i_read, j_next, 1 - now, [g])
+            absorb(i, j, now, causal, begins, [g])
+
     def reset():
         m_ref[...] = jnp.full_like(m_ref, NEG)
         acc_ref[...] = jnp.zeros_like(acc_ref)
@@ -187,20 +192,20 @@
             for n in range(2):
                 prepare(2 * i + core + 1 + n)
 
-        @pl.when(begins)
-        def _():
-            scores(i_read, j_next, 1 - slot)
-            absorb(i, j, slot, True, True)
-
-        @pl.when(causal)
-        def _():
-            scores(i_read, j_next, 1 - slot)
-            absorb(i, j, slot, True, False)
-
-        @pl.when(jnp.logical_not(begins | causal))
-        def _():
-            scores(i_read, j_next, 1 - slot)
-            absorb(i, j, slot, False, False)
+        for now in range(2):
+            turn = slot == now
+
+            @pl.when(turn & begins)
+            def _(now=now):
+                step(i_read, j_next, i, j, now, True, True)
+
+            @pl.when(turn & causal)
+            def _(now=now):
+                step(i_read, j_next, i, j, now, True, False)
+
+            @pl.when(turn & jnp.logical_not(begins | causal))
+            def _(now=now):
+                step(i_read, j_next, i, j, now, False, False)
 
         @pl.when(last)
         def _():
@@ -224,7 +229,7 @@
 
     pltpu.make_async_copy(q_ref, q_ref, q_sem).wait()
     start = meta_ref[0, 0] // TK
-    scores(0, start, 0)
+    scores(0, start, 0, range(NG))
     lax.while_loop(lambda carry: carry[0] < 4, body, (jnp.int32(0), start, jnp.int32(0)))
     for n in range(4):
         pltpu.make_async_copy(o_ref.at[:, n], out_ref.at[:, n], o_sem.at[n]).wait()
@@ -239,7 +244,8 @@
         scratch_shapes=[
             pltpu.VMEM((NG, 1, RG), F32),
             pltpu.VMEM((NG, HD + 16, RG), F32),
-            pltpu.VMEM((2, NG, TK, RG), F32),
+            pltpu.VMEM((NG, TK, RG), F32),
+            pltpu.VMEM((NG, TK, RG), F32),
             pltpu.VMEM((8, CHUNK, 1024), BF16),
             pltpu.VMEM((4, 2, 4, 2, 2, CHUNK, 2 * HD), BF16),
             pltpu.VMEM((8, HD + 16, TK), BF16),

time: 151 us -> 139 us (0.921)
  Pallas kernels: 55.9 us -> 42.8 us
  waiting for transfers between devices: 36.6 us -> 39 us
    pallas_call x1, Pallas kernels: 34.1 us -> 21 us  [attend(): pl.pallas_call(attn_kernel, out_shape=jax.ShapeDtypeStruct((2, 4, CHUNK,...]
    all_to_all x1, waiting for transfers between devices: 5.44 us -> 7.82 us  [per_device(): attn = lax.all_to_all(attn, HEADS, 0, 0, tiled=True)]
  transfers between devices with their start and end apart: 19 -> 19, of which waited for: 5 -> 5; matrix products, arithmetic and copies ran while one was open for 1% -> 1% of each run, Pallas kernels for 34% -> 27%
where the time goes in v4:
time: 139 us
  starting transfers between devices  50.3 us (36%)
  Pallas kernels  42.8 us (31%)
  waiting for transfers between devices  39 us (28%)
  local copies, waits for them, and re-layouts  5.28 us (4%)
    pallas_call x1, Pallas kernels, attend(): pl.pallas_call(attn_kernel, out_shape=jax.ShapeDtypeStruct((2, 4, CHUNK,...  21 us
    all_to_all x1, waiting for transfers between devices, per_device(): lax.all_to_all(split_heads(queries, keys, values), HEADS, 0, 0, tiled=True)  18 us
    ppermute x6, waiting for transfers between devices, along_y(): return [block] + [lax.ppermute(block, 'y', step) for step in steps]  13.2 us
    all_to_all x1, waiting for transfers between devices, per_device(): attn = lax.all_to_all(attn, HEADS, 0, 0, tiled=True)  7.82 us
    all_to_all x1, starting transfers between devices, per_device(): states = lax.all_to_all(states, ALL, 0, 0, tiled=True)  7.56 us
    ppermute x6, starting transfers between devices, along_y(): return [block] + [lax.ppermute(block, 'y', step) for step in steps]  7.49 us
    all_to_all x1, starting transfers between devices, per_device(): dec = lax.all_to_all(dec, TP, 0, 0, tiled=True).reshape(HM, 2 * CHUNK)  7.31 us
    all_to_all x1, starting transfers between devices, per_device(): entering = lax.all_to_all(entering, ALL, 0, 0, tiled=True)  6.79 us
  transfers between devices with their start and end apart: 19, of which 5 were waited for; matrix products, arithmetic and copies ran while one was open for 1% of the time, Pallas kernels for 27%

profile of v4, /device:TPU:1, one launch (start us, length us, event | category | flops | bytes accessed | tf_op | source)
XLA Modules:
  0.0 139.3 jit_solution(8358651205223815163)
XLA Ops:
  0.7 2.5 %shard_map.105 = bf16[8,64,1280]{2,1,0:T(8,128)(2,1)} custom-call(bf16[64,8192]{1,0:T(8,128)(2,1)} %q_ref.1, bf16[64,1024]{1,0:T(8,128)(2,1)} %k_ref.1, bf16[64,1024]{1,0:T(8,128)(2,1)} %v_ref.1), custom_call_target="tpu_custom_call" | custom-call | tf_op jit(solution)/shard_map/pallas_call | solution.py:47
  3.1 6.3 %all-to-all-start = ((bf16[8,64,1280]{2,1,0:T(8,128)(2,1)}), bf16[8,64,1280]{2,1,0:T(8,128)(2,1)}, u32[]{:S(2)}, u32[]{:S(2)}) async-start(bf16[8,64,1280]{2,1,0:T(8,128)(2,1)} %shard_map.105), calls=%async_computation | async-start | bytes 2621440 | tf_op jit(solution)/shard_map/all_to_all | solution.py:415
  9.5 0.0 copy-done.5
  9.5 0.8 shard_map.104
  10.3 18.0 %all-to-all-done.i_ref.all_ref = bf16[8,64,1280]{2,1,0:T(8,128)(2,1)} async-done(((bf16[8,64,1280]{2,1,0:T(8,128)(2,1)}), bf16[8,64,1280]{2,1,0:T(8,128)(2,1)}, u32[]{:S(2)}, u32[]{:S(2)}) %all-to-all-start) | async-done | bytes 1310752 | tf_op jit(solution)/shard_map/all_to_all | solution.py:415
  28.2 7.3 %all-to-all-start.1 = ((f32[16,16,128]{2,1,0:T(8,128)}), f32[16,16,128]{2,1,0:T(8,128)S(1)}, u32[]{:S(2)}, u32[]{:S(2)}) async-start(f32[16,16,128]{2,1,0:T(8,128)} %shard_map.104), calls=%async_computation.1 | async-start | bytes 262144 | tf_op jit(solution)/shard_map/all_to_all | solution.py:418
  35.5 0.1 pad_add_fusion.1.place_ref
  35.6 1.7 %shard_map.107 = (bf16[4,64,256]{2,1,0:T(8,128)(2,1)}, bf16[4,64,256]{2,1,0:T(8,128)(2,1)}) custom-call(bf16[8,64,1280]{2,1,0:T(8,128)(2,1)} %all-to-all-done.i_ref.all_ref), custom_call_target="tpu_custom_call" | custom-call | tf_op jit(solution)/shard_map/pallas_call | solution.py:69
  37.3 2.6 %collective-permute-start.3 = (bf16[4,64,256]{2,1,0:T(8,128)(2,1)}, bf16[4,64,256]{2,1,0:T(8,128)(2,1)S(1)}, u32[]{:S(2)}, u32[]{:S(2)}) collective-permute-start(bf16[4,64,256]{2,1,0:T(8,128)(2,1)} %get-tuple-element.14.refs_0_), channel_id=1, source_target_pairs={{0,12},{4,0},{8,4},{12,8},{1,13},{5,1},{9,5},{13,9},{2,14},{6,2},{... | collective-permute-start | bytes 393224 | tf_op jit(solution)/shard_map/ppermute | solution.py:424
  40.0 0.6 collective-permute-start.2
  40.5 0.6 collective-permute-start.1
  41.1 2.7 %collective-permute-start = (bf16[4,64,256]{2,1,0:T(8,128)(2,1)}, bf16[4,64,256]{2,1,0:T(8,128)(2,1)S(1)}, u32[]{:S(2)}, u32[]{:S(2)}) collective-permute-start(bf16[4,64,256]{2,1,0:T(8,128)(2,1)} %get-tuple-element.13.refs_0_), channel_id=1, source_target_pairs={{0,2},{2,0},{1,3},{3,1},{4,6},{6,4},{5,7},{7,5},{8,10},{10,8},{9,1... | collective-permute-start | bytes 393224 | tf_op jit(solution)/shard_map/ppermute | solution.py:420
  43.8 0.0 all-to-all-done.1
  43.8 4.6 %shard_map.106 = bf16[128,24,128]{2,1,0:T(8,128)(2,1)} custom-call(s32[3]{0:T(128)S(1)} %pad_add_fusion.1.place_ref, bf16[64,16384]{1,0:T(8,128)(2,1)S(1)} %copy-done, f32[256,128]{1,0:T(8,128)S(1)} %bitcast.15, f32[16,1024]{1,0:T(8,128)S(1)} %bitcast.17), custom_call_target="tpu_custom_call" | custom-call | flops 30000001024 | bytes 3145728 | tf_op jit(solution)/shard_map/pallas_call | solution.py:323
  48.4 0.0 collective-permute-done.refs_1_
  48.4 0.7 copy-done.7
  49.1 1.7 %shard_map.108.refs_0_ = bf16[2,4,64,256]{3,2,1,0:T(8,128)(2,1)} custom-call(bf16[4,64,256]{2,1,0:T(8,128)(2,1)} %get-tuple-element.13.refs_0_, bf16[4,64,256]{2,1,0:T(8,128)(2,1)} %copy-done.7), custom_call_target="tpu_custom_call" | custom-call | tf_op jit(solution)/shard_map/pallas_call | solution.py:84
  50.8 0.0 collective-permute-done.3.refs_3_
  50.8 0.0 collective-permute-done.2.refs_2_
  50.8 0.0 collective-permute-done.1.refs_1_
  50.8 0.6 copy-done.8
  51.4 0.0 copy-done.9
  51.5 0.7 copy-done.10
  52.1 1.9 %shard_map.109.refs_4_ = bf16[4,4,64,256]{3,2,1,0:T(8,128)(2,1)} custom-call(bf16[4,64,256]{2,1,0:T(8,128)(2,1)} %get-tuple-element.14.refs_0_, bf16[4,64,256]{2,1,0:T(8,128)(2,1)} %copy-done.10, bf16[4,64,256]{2,1,0:T(8,128)(2,1)} %copy-done.9, bf16[4,64,256]{2,1,0:T(8,128)(2,1)} %copy-done.8), custom_call_target="tpu_custom_call" | custom-call | tf_op jit(solution)/shard_map/pallas_call | solution.py:84
  54.1 7.6 %all-to-all-start.2 = ((bf16[128,24,128]{2,1,0:T(8,128)(2,1)}), bf16[128,24,128]{2,1,0:T(8,128)(2,1)S(1)}, u32[]{:S(2)}, u32[]{:S(2)}) async-start(bf16[128,24,128]{2,1,0:T(8,128)(2,1)} %shard_map.106), calls=%async_computation.2 | async-start | bytes 1572864 | tf_op jit(solution)/shard_map/all_to_all | solution.py:432
  61.6 3.4 %collective-permute-start.7 = (bf16[4,4,64,256]{3,2,1,0:T(8,128)(2,1)}, bf16[4,4,64,256]{3,2,1,0:T(8,128)(2,1)S(1)}, u32[]{:S(2)}, u32[]{:S(2)}) collective-permute-start(bf16[4,4,64,256]{3,2,1,0:T(8,128)(2,1)} %shard_map.109.refs_4_), channel_id=1, source_target_pairs={{0,2},{2,0},{1,3},{3,1},{4,6},{6,4},{5,7},{7,5},{8,10},{10,8},{9,1... | collective-permute-start | bytes 1572872 | tf_op jit(solution)/shard_map/ppermute | solution.py:420
  65.0 0.2 select_reduce_fusion
  65.2 0.2 convert_reduce_fusion
  65.4 0.7 collective-permute-start.8
  66.1 2.6 %collective-permute-start.6 = (bf16[2,4,64,256]{3,2,1,0:T(8,128)(2,1)S(1)}, bf16[2,4,64,256]{3,2,1,0:T(8,128)(2,1)S(1)}, u32[]{:S(2)}, u32[]{:S(2)}) collective-permute-start(bf16[2,4,64,256]{3,2,1,0:T(8,128)(2,1)S(1)} %copy-done.6), channel_id=1, source_target_pairs={{0,12},{4,0},{8,4},{12,8},{1,13},{5,1},{9,5},{13,9},{2,14},{6,2},{... | collective-permute-start | bytes 786440 | tf_op jit(solution)/shard_map/ppermute | solution.py:424
  68.7 0.4 collective-permute-start.5
  69.2 0.6 collective-permute-start.4
  69.8 0.1 add_bitcast_fusion
  69.9 0.6 pad_add_fusion.meta_ref
  70.5 0.0 collective-permute-done.8.refs_6_
  70.5 0.9 collective-permute-start.12
  71.4 6.8 %collective-permute-done.6.refs_3_ = bf16[2,4,64,256]{3,2,1,0:T(8,128)(2,1)S(1)} collective-permute-done((bf16[2,4,64,256]{3,2,1,0:T(8,128)(2,1)S(1)}, bf16[2,4,64,256]{3,2,1,0:T(8,128)(2,1)S(1)}, u32[]{:S(2)}, u32[]{:S(2)}) %collective-permute-start.6) | collective-permute-done | bytes 262176 | tf_op jit(solution)/shard_map/ppermute | solution.py:424
  78.2 0.6 collective-permute-start.11
  78.8 1.6 %collective-permute-done.5.refs_2_ = bf16[2,4,64,256]{3,2,1,0:T(8,128)(2,1)} collective-permute-done((bf16[2,4,64,256]{3,2,1,0:T(8,128)(2,1)S(1)}, bf16[2,4,64,256]{3,2,1,0:T(8,128)(2,1)}, u32[]{:S(2)}, u32[]{:S(2)}) %collective-permute-start.5) | collective-permute-done | bytes 262176 | tf_op jit(solution)/shard_map/ppermute | solution.py:424
  80.4 0.6 collective-permute-start.10
  81.0 4.8 %collective-permute-done.4.refs_1_ = bf16[2,4,64,256]{3,2,1,0:T(8,128)(2,1)} collective-permute-done((bf16[2,4,64,256]{3,2,1,0:T(8,128)(2,1)S(1)}, bf16[2,4,64,256]{3,2,1,0:T(8,128)(2,1)}, u32[]{:S(2)}, u32[]{:S(2)}) %collective-permute-start.4) | collective-permute-done | bytes 262176 | tf_op jit(solution)/shard_map/ppermute | solution.py:424
  85.8 0.5 collective-permute-start.9
  86.3 0.0 collective-permute-done.7.refs_5_
  86.3 0.1 collective-permute-start.13
  86.4 0.0 all-to-all-done.2.s_ref
  86.4 1.2 shard_map.110
  87.6 6.8 %all-to-all-start.3 = ((bf16[128,16,128]{2,1,0:T(8,128)(2,1)}), bf16[128,16,128]{2,1,0:T(8,128)(2,1)S(1)}, u32[]{:S(2)}, u32[]{:S(2)}) async-start(bf16[128,16,128]{2,1,0:T(8,128)(2,1)} %shard_map.110), calls=%async_computation.3 | async-start | bytes 1048576 | tf_op jit(solution)/shard_map/all_to_all | solution.py:441
  94.4 0.0 collective-permute-done.11.refs_9_
  94.4 0.0 collective-permute-done.10.refs_8_
  94.4 0.0 collective-permute-done.9.refs_7_
  94.4 0.0 collective-permute-done.12.refs_10_
  94.5 0.0 collective-permute-done.13.refs_11_
  94.5 0.7 copy-done.16
  95.1 0.2 copy-done.12
  95.3 0.8 copy-done.13
  96.1 21.0 %shard_map.112 = bf16[2,4,64,1024]{3,2,1,0:T(8,128)(2,1)} custom-call(s32[2,4]{1,0:T(2,128)} %pad_add_fusion.meta_ref, bf16[8,64,1280]{2,1,0:T(8,128)(2,1)} %all-to-all-done.i_ref.all_ref, bf16[2,4,64,256]{3,2,1,0:T(8,128)(2,1)} %shard_map.108.refs_0_, bf16[2,4,64,256]{3,2,1,0:T(8,128)(2,1)} %collective-permute-done.4.refs_1_, ...), custom_call_target="tpu_custom_call" | custom-call | flops 12000000000 | bytes 6291456 | tf_op jit(solution)/shard_map/pallas_call | solution.py:239
  117.1 0.0 copy-start.3
  117.2 0.0 all-to-all-done.3.e_ref
  117.2 5.2 %all-to-all-start.4 = ((bf16[8,64,1024]{2,1,0:T(8,128)(2,1)}), bf16[8,64,1024]{2,1,0:T(8,128)(2,1)S(1)}, u32[]{:S(2)}, u32[]{:S(2)}) async-start(bf16[8,64,1024]{2,1,0:T(8,128)(2,1)} %bitcast.22), calls=%async_computation.4 | async-start | bytes 2097152 | tf_op jit(solution)/shard_map/all_to_all | solution.py:443
  122.4 0.0 copy-start.1
  122.4 1.6 %copy-done.1 = bf16[64,16384]{1,0:T(8,128)(2,1)S(1)} copy-done((bf16[64,16384]{1,0:T(8,128)(2,1)S(1)}, bf16[64,16384]{1,0:T(8,128)(2,1)}, u32[]{:S(2)}) %copy-start.1) | copy-done | bytes 2097176
  124.0 6.4 %shard_map.111 = bf16[64,16384]{1,0:T(8,128)(2,1)} custom-call(s32[3]{0:T(128)S(1)} %pad_add_fusion.1.place_ref, bf16[64,16384]{1,0:T(8,128)(2,1)S(1)} %copy-done.1, f32[256,128]{1,0:T(8,128)S(1)} %bitcast.16, f32[16,1024]{1,0:T(8,128)S(1)} %bitcast.18, f32[16,1024]{1,0:T(8,128)S(1)} %bitcast.19, bf16[128,16,128]{2,1,0:T(8,128)(2,1)S(1)} %all-to-all-done.3.e_ref), custom_call_target="tpu_custom_call" | custom-call | flops 167772160 | bytes 5242880 | tf_op jit(solution)/shard_map/pallas_call | solution.py:368
  130.4 7.8 %all-to-all-done.4.i_ref = bf16[8,64,1024]{2,1,0:T(8,128)(2,1)S(1)} async-done(((bf16[8,64,1024]{2,1,0:T(8,128)(2,1)}), bf16[8,64,1024]{2,1,0:T(8,128)(2,1)S(1)}, u32[]{:S(2)}, u32[]{:S(2)}) %all-to-all-start.4) | async-done | bytes 1048608 | tf_op jit(solution)/shard_map/all_to_all | solution.py:443
  138.2 1.0 shard_map.113
  (26 shorter events, 0.1 us)
Async XLA Ops:
  0.6 8.9 %copy-start.5 = (f32[16]{0:T(128)S(1)}, f32[16]{0:T(128)}, u32[]{:S(2)}) copy-start(f32[16]{0:T(128)} %param.13) | copy-start | bytes 196
  0.6 8.9 %copy-start.4 = (f32[1024,16]{0,1:T(8,128)S(1)}, f32[1024,16]{0,1:T(8,128)}, u32[]{:S(2)}) copy-start(f32[1024,16]{0,1:T(8,128)} %param.12) | copy-start | bytes 196612
  3.1 40.7 %copy-start = (bf16[64,16384]{1,0:T(8,128)(2,1)S(1)}, bf16[64,16384]{1,0:T(8,128)(2,1)}, u32[]{:S(2)}) copy-start(bf16[64,16384]{1,0:T(8,128)(2,1)} %x_ref.3) | copy-start | bytes 6291460
  3.1 40.7 %copy-start.2 = (f32[1024,16]{0,1:T(8,128)S(1)}, f32[1024,16]{0,1:T(8,128)}, u32[]{:S(2)}) copy-start(f32[1024,16]{0,1:T(8,128)} %param.10) | copy-start | bytes 196612
  3.1 25.1 %all-to-all-start = ((bf16[8,64,1280]{2,1,0:T(8,128)(2,1)}), bf16[8,64,1280]{2,1,0:T(8,128)(2,1)}, u32[]{:S(2)}, u32[]{:S(2)}) async-start(bf16[8,64,1280]{2,1,0:T(8,128)(2,1)} %shard_map.105), calls=%async_computation | async-start | bytes 2621440 | tf_op jit(solution)/shard_map/all_to_all | solution.py:415
  28.2 15.6 %all-to-all-start.1 = ((f32[16,16,128]{2,1,0:T(8,128)}), f32[16,16,128]{2,1,0:T(8,128)S(1)}, u32[]{:S(2)}, u32[]{:S(2)}) async-start(f32[16,16,128]{2,1,0:T(8,128)} %shard_map.104), calls=%async_computation.1 | async-start | bytes 262144 | tf_op jit(solution)/shard_map/all_to_all | solution.py:418
  37.3 13.4 %collective-permute-start.3 = (bf16[4,64,256]{2,1,0:T(8,128)(2,1)}, bf16[4,64,256]{2,1,0:T(8,128)(2,1)S(1)}, u32[]{:S(2)}, u32[]{:S(2)}) collective-permute-start(bf16[4,64,256]{2,1,0:T(8,128)(2,1)} %get-tuple-element.14.refs_0_), channel_id=1, source_target_pairs={{0,12},{4,0},{8,4},{12,8},{1,13},{5,1},{9,5},{13,9},{2,14},{6,2},{... | collective-permute-start | bytes 393224 | tf_op jit(solution)/shard_map/ppermute | solution.py:424
  40.0 10.8 %collective-permute-start.2 = (bf16[4,64,256]{2,1,0:T(8,128)(2,1)}, bf16[4,64,256]{2,1,0:T(8,128)(2,1)S(1)}, u32[]{:S(2)}, u32[]{:S(2)}) collective-permute-start(bf16[4,64,256]{2,1,0:T(8,128)(2,1)} %get-tuple-element.14.refs_0_), channel_id=1, source_target_pairs={{0,8},{4,12},{8,0},{12,4},{1,9},{5,13},{9,1},{13,5},{2,10},{6,14},... | collective-permute-start | bytes 393224 | tf_op jit(solution)/shard_map/ppermute | solution.py:424
  40.5 10.3 %collective-permute-start.1 = (bf16[4,64,256]{2,1,0:T(8,128)(2,1)}, bf16[4,64,256]{2,1,0:T(8,128)(2,1)S(1)}, u32[]{:S(2)}, u32[]{:S(2)}) collective-permute-start(bf16[4,64,256]{2,1,0:T(8,128)(2,1)} %get-tuple-element.14.refs_0_), channel_id=1, source_target_pairs={{0,4},{4,8},{8,12},{12,0},{1,5},{5,9},{9,13},{13,1},{2,6},{6,10},{... | collective-permute-start | bytes 393224 | tf_op jit(solution)/shard_map/ppermute | solution.py:424
  41.1 7.3 %collective-permute-start = (bf16[4,64,256]{2,1,0:T(8,128)(2,1)}, bf16[4,64,256]{2,1,0:T(8,128)(2,1)S(1)}, u32[]{:S(2)}, u32[]{:S(2)}) collective-permute-start(bf16[4,64,256]{2,1,0:T(8,128)(2,1)} %get-tuple-element.13.refs_0_), channel_id=1, source_target_pairs={{0,2},{2,0},{1,3},{3,1},{4,6},{6,4},{5,7},{7,5},{8,10},{10,8},{9,1... | collective-permute-start | bytes 393224 | tf_op jit(solution)/shard_map/ppermute | solution.py:420
  48.4 16.6 %copy-start.17 = (s32[64]{0:T(128)S(1)}, s32[64]{0:T(128)}, u32[]{:S(2)}) copy-start(s32[64]{0:T(128)} %param.17) | copy-start | bytes 772
  48.4 0.7 copy-start.7
  50.8 14.6 %copy-start.6 = (bf16[2,4,64,256]{3,2,1,0:T(8,128)(2,1)S(1)}, bf16[2,4,64,256]{3,2,1,0:T(8,128)(2,1)}, u32[]{:S(2)}) copy-start(bf16[2,4,64,256]{3,2,1,0:T(8,128)(2,1)} %shard_map.108.refs_0_) | copy-start | bytes 786436
  50.8 0.7 copy-start.8
  50.8 0.7 copy-start.9
  51.5 0.7 copy-start.10
  54.1 32.4 %all-to-all-start.2 = ((bf16[128,24,128]{2,1,0:T(8,128)(2,1)}), bf16[128,24,128]{2,1,0:T(8,128)(2,1)S(1)}, u32[]{:S(2)}, u32[]{:S(2)}) async-start(bf16[128,24,128]{2,1,0:T(8,128)(2,1)} %shard_map.106), calls=%async_computation.2 | async-start | bytes 1572864 | tf_op jit(solution)/shard_map/all_to_all | solution.py:432
  61.6 24.7 %collective-permute-start.7 = (bf16[4,4,64,256]{3,2,1,0:T(8,128)(2,1)}, bf16[4,4,64,256]{3,2,1,0:T(8,128)(2,1)S(1)}, u32[]{:S(2)}, u32[]{:S(2)}) collective-permute-start(bf16[4,4,64,256]{3,2,1,0:T(8,128)(2,1)} %shard_map.109.refs_4_), channel_id=1, source_target_pairs={{0,2},{2,0},{1,3},{3,1},{4,6},{6,4},{5,7},{7,5},{8,10},{10,8},{9,1... | collective-permute-start | bytes 1572872 | tf_op jit(solution)/shard_map/ppermute | solution.py:420
  65.4 5.1 %collective-permute-start.8 = (bf16[2,4,64,256]{3,2,1,0:T(8,128)(2,1)S(1)}, bf16[2,4,64,256]{3,2,1,0:T(8,128)(2,1)S(1)}, u32[]{:S(2)}, u32[]{:S(2)}) collective-permute-start(bf16[2,4,64,256]{3,2,1,0:T(8,128)(2,1)S(1)} %copy-done.6), channel_id=1, source_target_pairs={{0,16},{16,0},{1,17},{17,1},{2,18},{18,2},{3,19},{19,3},{4,20},{20... | collective-permute-start | bytes 786440 | tf_op jit(solution)/shard_map/ppermute | solution.py:431
  66.1 12.0 %collective-permute-start.6 = (bf16[2,4,64,256]{3,2,1,0:T(8,128)(2,1)S(1)}, bf16[2,4,64,256]{3,2,1,0:T(8,128)(2,1)S(1)}, u32[]{:S(2)}, u32[]{:S(2)}) collective-permute-start(bf16[2,4,64,256]{3,2,1,0:T(8,128)(2,1)S(1)} %copy-done.6), channel_id=1, source_target_pairs={{0,12},{4,0},{8,4},{12,8},{1,13},{5,1},{9,5},{13,9},{2,14},{6,2},{... | collective-permute-start | bytes 786440 | tf_op jit(solution)/shard_map/ppermute | solution.py:424
  68.7 11.6 %collective-permute-start.5 = (bf16[2,4,64,256]{3,2,1,0:T(8,128)(2,1)S(1)}, bf16[2,4,64,256]{3,2,1,0:T(8,128)(2,1)}, u32[]{:S(2)}, u32[]{:S(2)}) collective-permute-start(bf16[2,4,64,256]{3,2,1,0:T(8,128)(2,1)S(1)} %copy-done.6), channel_id=1, source_target_pairs={{0,8},{4,12},{8,0},{12,4},{1,9},{5,13},{9,1},{13,5},{2,10},{6,14},... | collective-permute-start | bytes 786440 | tf_op jit(solution)/shard_map/ppermute | solution.py:424
  69.2 16.6 %collective-permute-start.4 = (bf16[2,4,64,256]{3,2,1,0:T(8,128)(2,1)S(1)}, bf16[2,4,64,256]{3,2,1,0:T(8,128)(2,1)}, u32[]{:S(2)}, u32[]{:S(2)}) collective-permute-start(bf16[2,4,64,256]{3,2,1,0:T(8,128)(2,1)S(1)} %copy-done.6), channel_id=1, source_target_pairs={{0,4},{4,8},{8,12},{12,0},{1,5},{5,9},{9,13},{13,1},{2,6},{6,10},{... | collective-permute-start | bytes 786440 | tf_op jit(solution)/shard_map/ppermute | solution.py:424
  70.5 17.1 %copy-start.14 = (bf16[2,4,64,256]{3,2,1,0:T(8,128)(2,1)}, bf16[2,4,64,256]{3,2,1,0:T(8,128)(2,1)S(1)}, u32[]{:S(2)}) copy-start(bf16[2,4,64,256]{3,2,1,0:T(8,128)(2,1)S(1)} %collective-permute-done.8.refs_6_) | copy-start | bytes 786436
  70.5 24.0 %collective-permute-start.12 = (bf16[4,4,64,256]{3,2,1,0:T(8,128)(2,1)}, bf16[4,4,64,256]{3,2,1,0:T(8,128)(2,1)S(1)}, u32[]{:S(2)}, u32[]{:S(2)}) collective-permute-start(bf16[4,4,64,256]{3,2,1,0:T(8,128)(2,1)} %shard_map.109.refs_4_), channel_id=1, source_target_pairs={{0,16},{16,0},{1,17},{17,1},{2,18},{18,2},{3,19},{19,3},{4,20},{20... | collective-permute-start | bytes 1572872 | tf_op jit(solution)/shard_map/ppermute | solution.py:431
  78.2 9.4 %copy-start.15 = (bf16[2,4,64,256]{3,2,1,0:T(8,128)(2,1)}, bf16[2,4,64,256]{3,2,1,0:T(8,128)(2,1)S(1)}, u32[]{:S(2)}) copy-start(bf16[2,4,64,256]{3,2,1,0:T(8,128)(2,1)S(1)} %collective-permute-done.6.refs_3_) | copy-start | bytes 786436
  78.2 16.2 %collective-permute-start.11 = (bf16[2,4,64,256]{3,2,1,0:T(8,128)(2,1)S(1)}, bf16[2,4,64,256]{3,2,1,0:T(8,128)(2,1)}, u32[]{:S(2)}, u32[]{:S(2)}) collective-permute-start(bf16[2,4,64,256]{3,2,1,0:T(8,128)(2,1)S(1)} %collective-permute-done.6.refs_3_), channel_id=1, source_target_pairs={{0,16},{16,0},{1,17},{17,1},{2,18},{18,2},{3,19},{19,3},{4,20},{20... | collective-permute-start | bytes 786440 | tf_op jit(solution)/shard_map/ppermute | solution.py:431
  80.4 14.0 %collective-permute-start.10 = (bf16[2,4,64,256]{3,2,1,0:T(8,128)(2,1)}, bf16[2,4,64,256]{3,2,1,0:T(8,128)(2,1)}, u32[]{:S(2)}, u32[]{:S(2)}) collective-permute-start(bf16[2,4,64,256]{3,2,1,0:T(8,128)(2,1)} %collective-permute-done.5.refs_2_), channel_id=1, source_target_pairs={{0,16},{16,0},{1,17},{17,1},{2,18},{18,2},{3,19},{19,3},{4,20},{20... | collective-permute-start | bytes 786440 | tf_op jit(solution)/shard_map/ppermute | solution.py:431
  85.8 8.6 %collective-permute-start.9 = (bf16[2,4,64,256]{3,2,1,0:T(8,128)(2,1)}, bf16[2,4,64,256]{3,2,1,0:T(8,128)(2,1)S(1)}, u32[]{:S(2)}, u32[]{:S(2)}) collective-permute-start(bf16[2,4,64,256]{3,2,1,0:T(8,128)(2,1)} %collective-permute-done.4.refs_1_), channel_id=1, source_target_pairs={{0,16},{16,0},{1,17},{17,1},{2,18},{18,2},{3,19},{19,3},{4,20},{20... | collective-permute-start | bytes 786440 | tf_op jit(solution)/shard_map/ppermute | solution.py:431
  86.3 1.3 copy-start.11
  86.3 8.1 %collective-permute-start.13 = (bf16[4,4,64,256]{3,2,1,0:T(8,128)(2,1)S(1)}, bf16[4,4,64,256]{3,2,1,0:T(8,128)(2,1)S(1)}, u32[]{:S(2)}, u32[]{:S(2)}) collective-permute-start(bf16[4,4,64,256]{3,2,1,0:T(8,128)(2,1)S(1)} %collective-permute-done.7.refs_5_), channel_id=1, source_target_pairs={{0,16},{16,0},{1,17},{17,1},{2,18},{18,2},{3,19},{19,3},{4,20},{20... | collective-permute-start | bytes 1572872 | tf_op jit(solution)/shard_map/ppermute | solution.py:431
  87.6 29.6 %all-to-all-start.3 = ((bf16[128,16,128]{2,1,0:T(8,128)(2,1)}), bf16[128,16,128]{2,1,0:T(8,128)(2,1)S(1)}, u32[]{:S(2)}, u32[]{:S(2)}) async-start(bf16[128,16,128]{2,1,0:T(8,128)(2,1)} %shard_map.110), calls=%async_computation.3 | async-start | bytes 1048576 | tf_op jit(solution)/shard_map/all_to_all | solution.py:441
  94.4 0.7 copy-start.16
  94.4 0.9 copy-start.12
  95.3 0.8 copy-start.13
  117.1 5.3 %copy-start.3 = (f32[1024,16]{0,1:T(8,128)S(1)}, f32[1024,16]{0,1:T(8,128)}, u32[]{:S(2)}) copy-start(f32[1024,16]{0,1:T(8,128)} %param.11) | copy-start | bytes 196612
  117.2 21.0 %all-to-all-start.4 = ((bf16[8,64,1024]{2,1,0:T(8,128)(2,1)}), bf16[8,64,1024]{2,1,0:T(8,128)(2,1)S(1)}, u32[]{:S(2)}, u32[]{:S(2)}) async-start(bf16[8,64,1024]{2,1,0:T(8,128)(2,1)} %bitcast.22), calls=%async_computation.4 | async-start | bytes 2097152 | tf_op jit(solution)/shard_map/all_to_all | solution.py:443
  122.4 1.6 %copy-start.1 = (bf16[64,16384]{1,0:T(8,128)(2,1)S(1)}, bf16[64,16384]{1,0:T(8,128)(2,1)}, u32[]{:S(2)}) copy-start(bf16[64,16384]{1,0:T(8,128)(2,1)} %x_ref.3) | copy-start | bytes 6291460

commit v5 on v4

--- a/solution.py
+++ b/solution.py
@@ -86,6 +86,7 @@
         out_shape=jax.ShapeDtypeStruct((len(blocks),) + blocks[0].shape, blocks[0].dtype),
         in_specs=[VMEM] * len(blocks),
         out_specs=VMEM,
+        compiler_params=SMALL,
     )(*blocks)
 
 

time: 139 us -> 132 us (0.950)
  Pallas kernels: 42.8 us -> 38.2 us
  local copies, waits for them, and re-layouts: 5.28 us -> 3.2 us
    pallas_call x2, Pallas kernels: 3.62 us -> 0.05 us  [stack(): pl.pallas_call(stack_kernel, out_shape=jax.ShapeDtypeStruct((len(blocks),...]
    unnamed x36 -> x30, local copies, waits for them, and re-layouts: 5.28 us -> 3.2 us
  transfers between devices with their start and end apart: 19 -> 19, of which waited for: 5 -> 6; matrix products, arithmetic and copies ran while one was open for 1% -> 1% of each run, Pallas kernels for 27% -> 26%
where the time goes in v5:
time: 132 us; the launch traced here: 133 us
  starting transfers between devices  50.1 us (38%)
  waiting for transfers between devices  39.3 us (30%)
  Pallas kernels  38.2 us (29%)
  local copies, waits for them, and re-layouts  3.2 us (2%)
    pallas_call x1, Pallas kernels, attend(): pl.pallas_call(attn_kernel, out_shape=jax.ShapeDtypeStruct((2, 4, CHUNK,...  20 us
    all_to_all x1, waiting for transfers between devices, per_device(): lax.all_to_all(split_heads(queries, keys, values), HEADS, 0, 0, tiled=True)  18 us
    ppermute x6, waiting for transfers between devices, along_y(): return [block] + [lax.ppermute(block, 'y', step) for step in steps]  13.5 us
    all_to_all x1, waiting for transfers between devices, per_device(): attn = lax.all_to_all(attn, HEADS, 0, 0, tiled=True)  7.81 us
    ppermute x6, starting transfers between devices, along_y(): return [block] + [lax.ppermute(block, 'y', step) for step in steps]  7.49 us
    all_to_all x1, starting transfers between devices, per_device(): dec = lax.all_to_all(dec, TP, 0, 0, tiled=True).reshape(HM, 2 * CHUNK)  7.31 us
    all_to_all x1, starting transfers between devices, per_device(): states = lax.all_to_all(states, ALL, 0, 0, tiled=True)  7.18 us
    all_to_all x1, starting transfers between devices, per_device(): entering = lax.all_to_all(entering, ALL, 0, 0, tiled=True)  6.84 us
  transfers between devices with their start and end apart: 19, of which 6 were waited for; matrix products, arithmetic and copies ran while one was open for 1% of the time, Pallas kernels for 26%

profile of v5, /device:TPU:1, one launch (start us, length us, event | category | flops | bytes accessed | tf_op | source)
XLA Modules:
  0.0 132.7 jit_solution(14095275644275618372)
XLA Ops:
  0.6 0.0 copy-start.9
  0.6 0.0 copy-start.8
  0.7 2.5 %shard_map.105 = bf16[8,64,1280]{2,1,0:T(8,128)(2,1)} custom-call(bf16[64,8192]{1,0:T(8,128)(2,1)} %q_ref.1, bf16[64,1024]{1,0:T(8,128)(2,1)} %k_ref.1, bf16[64,1024]{1,0:T(8,128)(2,1)} %v_ref.1), custom_call_target="tpu_custom_call" | custom-call | tf_op jit(solution)/shard_map/pallas_call | solution.py:47
  3.1 6.3 %all-to-all-start = ((bf16[8,64,1280]{2,1,0:T(8,128)(2,1)}), bf16[8,64,1280]{2,1,0:T(8,128)(2,1)}, u32[]{:S(2)}, u32[]{:S(2)}) async-start(bf16[8,64,1280]{2,1,0:T(8,128)(2,1)} %shard_map.105), calls=%async_computation | async-start | bytes 2621440 | tf_op jit(solution)/shard_map/all_to_all | solution.py:416
  9.5 0.0 copy-done.9
  9.5 0.0 copy-done.8
  9.5 0.8 shard_map.104
  10.3 18.0 %all-to-all-done.i_ref.all_ref = bf16[8,64,1280]{2,1,0:T(8,128)(2,1)} async-done(((bf16[8,64,1280]{2,1,0:T(8,128)(2,1)}), bf16[8,64,1280]{2,1,0:T(8,128)(2,1)}, u32[]{:S(2)}, u32[]{:S(2)}) %all-to-all-start) | async-done | bytes 1310752 | tf_op jit(solution)/shard_map/all_to_all | solution.py:416
  28.2 7.3 %all-to-all-start.1 = ((f32[16,16,128]{2,1,0:T(8,128)}), f32[16,16,128]{2,1,0:T(8,128)S(1)}, u32[]{:S(2)}, u32[]{:S(2)}) async-start(f32[16,16,128]{2,1,0:T(8,128)} %shard_map.104), calls=%async_computation.1 | async-start | bytes 262144 | tf_op jit(solution)/shard_map/all_to_all | solution.py:419
  35.5 0.1 pad_add_fusion.1.place_ref
  35.6 1.7 %shard_map.107 = (bf16[4,64,256]{2,1,0:T(8,128)(2,1)}, bf16[4,64,256]{2,1,0:T(8,128)(2,1)}) custom-call(bf16[8,64,1280]{2,1,0:T(8,128)(2,1)} %all-to-all-done.i_ref.all_ref), custom_call_target="tpu_custom_call" | custom-call | tf_op jit(solution)/shard_map/pallas_call | solution.py:69
  37.3 2.6 %collective-permute-start.3 = (bf16[4,64,256]{2,1,0:T(8,128)(2,1)}, bf16[4,64,256]{2,1,0:T(8,128)(2,1)S(1)}, u32[]{:S(2)}, u32[]{:S(2)}) collective-permute-start(bf16[4,64,256]{2,1,0:T(8,128)(2,1)} %get-tuple-element.14.refs_0_), channel_id=1, source_target_pairs={{0,12},{4,0},{8,4},{12,8},{1,13},{5,1},{9,5},{13,9},{2,14},{6,2},{... | collective-permute-start | bytes 393224 | tf_op jit(solution)/shard_map/ppermute | solution.py:425
  39.9 0.6 collective-permute-start.2
  40.5 0.6 collective-permute-start.1
  41.1 2.7 %collective-permute-start = (bf16[4,64,256]{2,1,0:T(8,128)(2,1)}, bf16[4,64,256]{2,1,0:T(8,128)(2,1)S(1)}, u32[]{:S(2)}, u32[]{:S(2)}) collective-permute-start(bf16[4,64,256]{2,1,0:T(8,128)(2,1)} %get-tuple-element.13.refs_0_), channel_id=1, source_target_pairs={{0,2},{2,0},{1,3},{3,1},{4,6},{6,4},{5,7},{7,5},{8,10},{10,8},{9,1... | collective-permute-start | bytes 393224 | tf_op jit(solution)/shard_map/ppermute | solution.py:421
  43.8 0.0 all-to-all-done.1
  43.8 0.0 copy-done
  43.8 0.0 copy-done.6
  43.8 4.6 %shard_map.106 = bf16[128,24,128]{2,1,0:T(8,128)(2,1)} custom-call(s32[3]{0:T(128)S(1)} %pad_add_fusion.1.place_ref, bf16[64,16384]{1,0:T(8,128)(2,1)S(1)} %copy-done, f32[256,128]{1,0:T(8,128)S(1)} %bitcast.15, f32[16,1024]{1,0:T(8,128)S(1)} %bitcast.17), custom_call_target="tpu_custom_call" | custom-call | flops 30000001024 | bytes 3145728 | tf_op jit(solution)/shard_map/pallas_call | solution.py:324
  48.4 0.0 collective-permute-done.refs_1_
  48.5 0.0 copy-start.3
  48.5 0.0 collective-permute-done.3.refs_3_
  48.5 0.0 collective-permute-done.2.refs_2_
  48.5 0.4 collective-permute-done.1.refs_1_
  48.9 7.2 %all-to-all-start.2 = ((bf16[128,24,128]{2,1,0:T(8,128)(2,1)}), bf16[128,24,128]{2,1,0:T(8,128)(2,1)S(1)}, u32[]{:S(2)}, u32[]{:S(2)}) async-start(bf16[128,24,128]{2,1,0:T(8,128)(2,1)} %shard_map.106), calls=%async_computation.2 | async-start | bytes 1572864 | tf_op jit(solution)/shard_map/all_to_all | solution.py:433
  56.1 3.4 %collective-permute-start.7 = (bf16[4,4,64,256]{3,2,1,0:T(8,128)(2,1)S(1)}, bf16[4,4,64,256]{3,2,1,0:T(8,128)(2,1)S(1)}, u32[]{:S(2)}, u32[]{:S(2)}) collective-permute-start(bf16[4,4,64,256]{3,2,1,0:T(8,128)(2,1)S(1)} %shard_map.109.refs_4_), channel_id=1, source_target_pairs={{0,2},{2,0},{1,3},{3,1},{4,6},{6,4},{5,7},{7,5},{8,10},{10,8},{9,1... | collective-permute-start | bytes 1572872 | tf_op jit(solution)/shard_map/ppermute | solution.py:421
  59.5 0.2 select_reduce_fusion
  59.7 0.2 convert_reduce_fusion
  59.9 0.7 collective-permute-start.8
  60.6 2.6 %collective-permute-start.6 = (bf16[2,4,64,256]{3,2,1,0:T(8,128)(2,1)S(1)}, bf16[2,4,64,256]{3,2,1,0:T(8,128)(2,1)}, u32[]{:S(2)}, u32[]{:S(2)}) collective-permute-start(bf16[2,4,64,256]{3,2,1,0:T(8,128)(2,1)S(1)} %shard_map.108.refs_0_), channel_id=1, source_target_pairs={{0,12},{4,0},{8,4},{12,8},{1,13},{5,1},{9,5},{13,9},{2,14},{6,2},{... | collective-permute-start | bytes 786440 | tf_op jit(solution)/shard_map/ppermute | solution.py:425
  63.2 0.4 collective-permute-start.5
  63.6 0.6 collective-permute-start.4
  64.3 0.1 add_bitcast_fusion
  64.4 0.6 pad_add_fusion.meta_ref
  64.9 0.0 collective-permute-done.8.refs_6_
  64.9 0.9 collective-permute-start.12
  65.8 6.8 %collective-permute-done.6.refs_3_ = bf16[2,4,64,256]{3,2,1,0:T(8,128)(2,1)} collective-permute-done((bf16[2,4,64,256]{3,2,1,0:T(8,128)(2,1)S(1)}, bf16[2,4,64,256]{3,2,1,0:T(8,128)(2,1)}, u32[]{:S(2)}, u32[]{:S(2)}) %collective-permute-start.6) | collective-permute-done | bytes 262176 | tf_op jit(solution)/shard_map/ppermute | solution.py:425
  72.6 0.7 collective-permute-start.11
  73.4 1.5 %collective-permute-done.5.refs_2_ = bf16[2,4,64,256]{3,2,1,0:T(8,128)(2,1)} collective-permute-done((bf16[2,4,64,256]{3,2,1,0:T(8,128)(2,1)S(1)}, bf16[2,4,64,256]{3,2,1,0:T(8,128)(2,1)}, u32[]{:S(2)}, u32[]{:S(2)}) %collective-permute-start.5) | collective-permute-done | bytes 262176 | tf_op jit(solution)/shard_map/ppermute | solution.py:425
  74.8 0.6 collective-permute-start.10
  75.5 4.8 %collective-permute-done.4.refs_1_ = bf16[2,4,64,256]{3,2,1,0:T(8,128)(2,1)} collective-permute-done((bf16[2,4,64,256]{3,2,1,0:T(8,128)(2,1)S(1)}, bf16[2,4,64,256]{3,2,1,0:T(8,128)(2,1)}, u32[]{:S(2)}, u32[]{:S(2)}) %collective-permute-start.4) | collective-permute-done | bytes 262176 | tf_op jit(solution)/shard_map/ppermute | solution.py:425
  80.3 0.5 collective-permute-start.9
  80.8 0.0 collective-permute-done.7.refs_5_
  80.8 0.1 collective-permute-start.13
  80.9 0.0 all-to-all-done.2.s_ref
  80.9 1.2 shard_map.110
  82.1 0.0 copy-done.2
  82.1 6.8 %all-to-all-start.3 = ((bf16[128,16,128]{2,1,0:T(8,128)(2,1)}), bf16[128,16,128]{2,1,0:T(8,128)(2,1)S(1)}, u32[]{:S(2)}, u32[]{:S(2)}) async-start(bf16[128,16,128]{2,1,0:T(8,128)(2,1)} %shard_map.110), calls=%async_computation.3 | async-start | bytes 1048576 | tf_op jit(solution)/shard_map/all_to_all | solution.py:442
  88.9 0.0 collective-permute-done.11.refs_9_
  88.9 0.0 collective-permute-done.10.refs_8_
  89.0 0.0 collective-permute-done.9.refs_7_
  89.0 0.0 collective-permute-done.12.refs_10_
  89.0 0.0 collective-permute-done.13.refs_11_
  89.0 0.8 copy-done.11
  89.8 0.8 copy-done.12
  90.6 20.0 %shard_map.112 = bf16[2,4,64,1024]{3,2,1,0:T(8,128)(2,1)} custom-call(s32[2,4]{1,0:T(2,128)} %pad_add_fusion.meta_ref, bf16[8,64,1280]{2,1,0:T(8,128)(2,1)} %all-to-all-done.i_ref.all_ref, bf16[2,4,64,256]{3,2,1,0:T(8,128)(2,1)} %copy-done.3, bf16[2,4,64,256]{3,2,1,0:T(8,128)(2,1)} %collective-permute-done.4.refs_1_, ...), custom_call_target="tpu_custom_call" | custom-call | flops 12000000000 | bytes 6291456 | tf_op jit(solution)/shard_map/pallas_call | solution.py:240
  110.6 0.0 copy-start.7
  110.6 0.0 all-to-all-done.3.e_ref
  110.6 5.2 %all-to-all-start.4 = ((bf16[8,64,1024]{2,1,0:T(8,128)(2,1)}), bf16[8,64,1024]{2,1,0:T(8,128)(2,1)S(1)}, u32[]{:S(2)}, u32[]{:S(2)}) async-start(bf16[8,64,1024]{2,1,0:T(8,128)(2,1)} %bitcast.22), calls=%async_computation.4 | async-start | bytes 2097152 | tf_op jit(solution)/shard_map/all_to_all | solution.py:444
  115.9 0.0 copy-start.1
  115.9 1.6 %copy-done.1 = bf16[64,16384]{1,0:T(8,128)(2,1)S(1)} copy-done((bf16[64,16384]{1,0:T(8,128)(2,1)S(1)}, bf16[64,16384]{1,0:T(8,128)(2,1)}, u32[]{:S(2)}) %copy-start.1) | copy-done | bytes 2097176
  117.4 6.4 %shard_map.111 = bf16[64,16384]{1,0:T(8,128)(2,1)} custom-call(s32[3]{0:T(128)S(1)} %pad_add_fusion.1.place_ref, bf16[64,16384]{1,0:T(8,128)(2,1)S(1)} %copy-done.1, f32[256,128]{1,0:T(8,128)S(1)} %bitcast.16, f32[16,1024]{1,0:T(8,128)S(1)} %bitcast.18, f32[16,1024]{1,0:T(8,128)S(1)} %bitcast.19, bf16[128,16,128]{2,1,0:T(8,128)(2,1)S(1)} %all-to-all-done.3.e_ref), custom_call_target="tpu_custom_call" | custom-call | flops 167772160 | bytes 5242880 | tf_op jit(solution)/shard_map/pallas_call | solution.py:369
  123.8 7.8 %all-to-all-done.4.i_ref = bf16[8,64,1024]{2,1,0:T(8,128)(2,1)S(1)} async-done(((bf16[8,64,1024]{2,1,0:T(8,128)(2,1)}), bf16[8,64,1024]{2,1,0:T(8,128)(2,1)S(1)}, u32[]{:S(2)}, u32[]{:S(2)}) %all-to-all-start.4) | async-done | bytes 1048608 | tf_op jit(solution)/shard_map/all_to_all | solution.py:444
  131.6 1.0 shard_map.113
  (20 shorter events, 0.1 us)
Async XLA Ops:
  0.6 8.9 %copy-start.9 = (f32[16]{0:T(128)S(1)}, f32[16]{0:T(128)}, u32[]{:S(2)}) copy-start(f32[16]{0:T(128)} %param.13) | copy-start | bytes 196
  0.6 8.9 %copy-start.8 = (f32[1024,16]{0,1:T(8,128)S(1)}, f32[1024,16]{0,1:T(8,128)}, u32[]{:S(2)}) copy-start(f32[1024,16]{0,1:T(8,128)} %param.12) | copy-start | bytes 196612
  3.1 40.6 %copy-start = (bf16[64,16384]{1,0:T(8,128)(2,1)S(1)}, bf16[64,16384]{1,0:T(8,128)(2,1)}, u32[]{:S(2)}) copy-start(bf16[64,16384]{1,0:T(8,128)(2,1)} %x_ref.3) | copy-start | bytes 6291460
  3.1 40.6 %copy-start.6 = (f32[1024,16]{0,1:T(8,128)S(1)}, f32[1024,16]{0,1:T(8,128)}, u32[]{:S(2)}) copy-start(f32[1024,16]{0,1:T(8,128)} %param.10) | copy-start | bytes 196612
  3.1 25.1 %all-to-all-start = ((bf16[8,64,1280]{2,1,0:T(8,128)(2,1)}), bf16[8,64,1280]{2,1,0:T(8,128)(2,1)}, u32[]{:S(2)}, u32[]{:S(2)}) async-start(bf16[8,64,1280]{2,1,0:T(8,128)(2,1)} %shard_map.105), calls=%async_computation | async-start | bytes 2621440 | tf_op jit(solution)/shard_map/all_to_all | solution.py:416
  28.2 15.6 %all-to-all-start.1 = ((f32[16,16,128]{2,1,0:T(8,128)}), f32[16,16,128]{2,1,0:T(8,128)S(1)}, u32[]{:S(2)}, u32[]{:S(2)}) async-start(f32[16,16,128]{2,1,0:T(8,128)} %shard_map.104), calls=%async_computation.1 | async-start | bytes 262144 | tf_op jit(solution)/shard_map/all_to_all | solution.py:419
  37.3 11.2 %collective-permute-start.3 = (bf16[4,64,256]{2,1,0:T(8,128)(2,1)}, bf16[4,64,256]{2,1,0:T(8,128)(2,1)S(1)}, u32[]{:S(2)}, u32[]{:S(2)}) collective-permute-start(bf16[4,64,256]{2,1,0:T(8,128)(2,1)} %get-tuple-element.14.refs_0_), channel_id=1, source_target_pairs={{0,12},{4,0},{8,4},{12,8},{1,13},{5,1},{9,5},{13,9},{2,14},{6,2},{... | collective-permute-start | bytes 393224 | tf_op jit(solution)/shard_map/ppermute | solution.py:425
  39.9 8.5 %collective-permute-start.2 = (bf16[4,64,256]{2,1,0:T(8,128)(2,1)}, bf16[4,64,256]{2,1,0:T(8,128)(2,1)S(1)}, u32[]{:S(2)}, u32[]{:S(2)}) collective-permute-start(bf16[4,64,256]{2,1,0:T(8,128)(2,1)} %get-tuple-element.14.refs_0_), channel_id=1, source_target_pairs={{0,8},{4,12},{8,0},{12,4},{1,9},{5,13},{9,1},{13,5},{2,10},{6,14},... | collective-permute-start | bytes 393224 | tf_op jit(solution)/shard_map/ppermute | solution.py:425
  40.5 8.3 %collective-permute-start.1 = (bf16[4,64,256]{2,1,0:T(8,128)(2,1)}, bf16[4,64,256]{2,1,0:T(8,128)(2,1)S(1)}, u32[]{:S(2)}, u32[]{:S(2)}) collective-permute-start(bf16[4,64,256]{2,1,0:T(8,128)(2,1)} %get-tuple-element.14.refs_0_), channel_id=1, source_target_pairs={{0,4},{4,8},{8,12},{12,0},{1,5},{5,9},{9,13},{13,1},{2,6},{6,10},{... | collective-permute-start | bytes 393224 | tf_op jit(solution)/shard_map/ppermute | solution.py:425
  41.1 7.3 %collective-permute-start = (bf16[4,64,256]{2,1,0:T(8,128)(2,1)}, bf16[4,64,256]{2,1,0:T(8,128)(2,1)S(1)}, u32[]{:S(2)}, u32[]{:S(2)}) collective-permute-start(bf16[4,64,256]{2,1,0:T(8,128)(2,1)} %get-tuple-element.13.refs_0_), channel_id=1, source_target_pairs={{0,2},{2,0},{1,3},{3,1},{4,6},{6,4},{5,7},{7,5},{8,10},{10,8},{9,1... | collective-permute-start | bytes 393224 | tf_op jit(solution)/shard_map/ppermute | solution.py:421
  43.8 4.6 %copy-start.4 = (bf16[4,64,256]{2,1,0:T(8,128)(2,1)S(1)}, bf16[4,64,256]{2,1,0:T(8,128)(2,1)}, u32[]{:S(2)}) copy-start(bf16[4,64,256]{2,1,0:T(8,128)(2,1)} %get-tuple-element.13.refs_0_) | copy-start | bytes 393220
  43.8 5.1 %copy-start.5 = (bf16[4,64,256]{2,1,0:T(8,128)(2,1)S(1)}, bf16[4,64,256]{2,1,0:T(8,128)(2,1)}, u32[]{:S(2)}) copy-start(bf16[4,64,256]{2,1,0:T(8,128)(2,1)} %get-tuple-element.14.refs_0_) | copy-start | bytes 393220
  48.4 11.1 %copy-start.14 = (s32[64]{0:T(128)S(1)}, s32[64]{0:T(128)}, u32[]{:S(2)}) copy-start(s32[64]{0:T(128)} %param.17) | copy-start | bytes 772
  48.5 33.6 %copy-start.3 = (bf16[2,4,64,256]{3,2,1,0:T(8,128)(2,1)}, bf16[2,4,64,256]{3,2,1,0:T(8,128)(2,1)S(1)}, u32[]{:S(2)}) copy-start(bf16[2,4,64,256]{3,2,1,0:T(8,128)(2,1)S(1)} %shard_map.108.refs_0_) | copy-start | bytes 786436
  48.9 33.2 %copy-start.2 = (bf16[4,4,64,256]{3,2,1,0:T(8,128)(2,1)}, bf16[4,4,64,256]{3,2,1,0:T(8,128)(2,1)S(1)}, u32[]{:S(2)}) copy-start(bf16[4,4,64,256]{3,2,1,0:T(8,128)(2,1)S(1)} %shard_map.109.refs_4_) | copy-start | bytes 1572868
  48.9 32.0 %all-to-all-start.2 = ((bf16[128,24,128]{2,1,0:T(8,128)(2,1)}), bf16[128,24,128]{2,1,0:T(8,128)(2,1)S(1)}, u32[]{:S(2)}, u32[]{:S(2)}) async-start(bf16[128,24,128]{2,1,0:T(8,128)(2,1)} %shard_map.106), calls=%async_computation.2 | async-start | bytes 1572864 | tf_op jit(solution)/shard_map/all_to_all | solution.py:433
  56.1 24.7 %collective-permute-start.7 = (bf16[4,4,64,256]{3,2,1,0:T(8,128)(2,1)S(1)}, bf16[4,4,64,256]{3,2,1,0:T(8,128)(2,1)S(1)}, u32[]{:S(2)}, u32[]{:S(2)}) collective-permute-start(bf16[4,4,64,256]{3,2,1,0:T(8,128)(2,1)S(1)} %shard_map.109.refs_4_), channel_id=1, source_target_pairs={{0,2},{2,0},{1,3},{3,1},{4,6},{6,4},{5,7},{7,5},{8,10},{10,8},{9,1... | collective-permute-start | bytes 1572872 | tf_op jit(solution)/shard_map/ppermute | solution.py:421
  59.9 5.0 %collective-permute-start.8 = (bf16[2,4,64,256]{3,2,1,0:T(8,128)(2,1)S(1)}, bf16[2,4,64,256]{3,2,1,0:T(8,128)(2,1)S(1)}, u32[]{:S(2)}, u32[]{:S(2)}) collective-permute-start(bf16[2,4,64,256]{3,2,1,0:T(8,128)(2,1)S(1)} %shard_map.108.refs_0_), channel_id=1, source_target_pairs={{0,16},{16,0},{1,17},{17,1},{2,18},{18,2},{3,19},{19,3},{4,20},{20... | collective-permute-start | bytes 786440 | tf_op jit(solution)/shard_map/ppermute | solution.py:432
  60.6 12.0 %collective-permute-start.6 = (bf16[2,4,64,256]{3,2,1,0:T(8,128)(2,1)S(1)}, bf16[2,4,64,256]{3,2,1,0:T(8,128)(2,1)}, u32[]{:S(2)}, u32[]{:S(2)}) collective-permute-start(bf16[2,4,64,256]{3,2,1,0:T(8,128)(2,1)S(1)} %shard_map.108.refs_0_), channel_id=1, source_target_pairs={{0,12},{4,0},{8,4},{12,8},{1,13},{5,1},{9,5},{13,9},{2,14},{6,2},{... | collective-permute-start | bytes 786440 | tf_op jit(solution)/shard_map/ppermute | solution.py:425
  63.2 11.6 %collective-permute-start.5 = (bf16[2,4,64,256]{3,2,1,0:T(8,128)(2,1)S(1)}, bf16[2,4,64,256]{3,2,1,0:T(8,128)(2,1)}, u32[]{:S(2)}, u32[]{:S(2)}) collective-permute-start(bf16[2,4,64,256]{3,2,1,0:T(8,128)(2,1)S(1)} %shard_map.108.refs_0_), channel_id=1, source_target_pairs={{0,8},{4,12},{8,0},{12,4},{1,9},{5,13},{9,1},{13,5},{2,10},{6,14},... | collective-permute-start | bytes 786440 | tf_op jit(solution)/shard_map/ppermute | solution.py:425
  63.6 16.6 %collective-permute-start.4 = (bf16[2,4,64,256]{3,2,1,0:T(8,128)(2,1)S(1)}, bf16[2,4,64,256]{3,2,1,0:T(8,128)(2,1)}, u32[]{:S(2)}, u32[]{:S(2)}) collective-permute-start(bf16[2,4,64,256]{3,2,1,0:T(8,128)(2,1)S(1)} %shard_map.108.refs_0_), channel_id=1, source_target_pairs={{0,4},{4,8},{8,12},{12,0},{1,5},{5,9},{9,13},{13,1},{2,6},{6,10},{... | collective-permute-start | bytes 786440 | tf_op jit(solution)/shard_map/ppermute | solution.py:425
  64.9 15.9 %copy-start.13 = (bf16[2,4,64,256]{3,2,1,0:T(8,128)(2,1)}, bf16[2,4,64,256]{3,2,1,0:T(8,128)(2,1)S(1)}, u32[]{:S(2)}) copy-start(bf16[2,4,64,256]{3,2,1,0:T(8,128)(2,1)S(1)} %collective-permute-done.8.refs_6_) | copy-start | bytes 786436
  64.9 24.1 %collective-permute-start.12 = (bf16[4,4,64,256]{3,2,1,0:T(8,128)(2,1)S(1)}, bf16[4,4,64,256]{3,2,1,0:T(8,128)(2,1)S(1)}, u32[]{:S(2)}, u32[]{:S(2)}) collective-permute-start(bf16[4,4,64,256]{3,2,1,0:T(8,128)(2,1)S(1)} %shard_map.109.refs_4_), channel_id=1, source_target_pairs={{0,16},{16,0},{1,17},{17,1},{2,18},{18,2},{3,19},{19,3},{4,20},{20... | collective-permute-start | bytes 1572872 | tf_op jit(solution)/shard_map/ppermute | solution.py:432
  72.6 16.3 %collective-permute-start.11 = (bf16[2,4,64,256]{3,2,1,0:T(8,128)(2,1)}, bf16[2,4,64,256]{3,2,1,0:T(8,128)(2,1)}, u32[]{:S(2)}, u32[]{:S(2)}) collective-permute-start(bf16[2,4,64,256]{3,2,1,0:T(8,128)(2,1)} %collective-permute-done.6.refs_3_), channel_id=1, source_target_pairs={{0,16},{16,0},{1,17},{17,1},{2,18},{18,2},{3,19},{19,3},{4,20},{20... | collective-permute-start | bytes 786440 | tf_op jit(solution)/shard_map/ppermute | solution.py:432
  74.8 14.1 %collective-permute-start.10 = (bf16[2,4,64,256]{3,2,1,0:T(8,128)(2,1)}, bf16[2,4,64,256]{3,2,1,0:T(8,128)(2,1)}, u32[]{:S(2)}, u32[]{:S(2)}) collective-permute-start(bf16[2,4,64,256]{3,2,1,0:T(8,128)(2,1)} %collective-permute-done.5.refs_2_), channel_id=1, source_target_pairs={{0,16},{16,0},{1,17},{17,1},{2,18},{18,2},{3,19},{19,3},{4,20},{20... | collective-permute-start | bytes 786440 | tf_op jit(solution)/shard_map/ppermute | solution.py:432
  80.3 8.7 %collective-permute-start.9 = (bf16[2,4,64,256]{3,2,1,0:T(8,128)(2,1)}, bf16[2,4,64,256]{3,2,1,0:T(8,128)(2,1)}, u32[]{:S(2)}, u32[]{:S(2)}) collective-permute-start(bf16[2,4,64,256]{3,2,1,0:T(8,128)(2,1)} %collective-permute-done.4.refs_1_), channel_id=1, source_target_pairs={{0,16},{16,0},{1,17},{17,1},{2,18},{18,2},{3,19},{19,3},{4,20},{20... | collective-permute-start | bytes 786440 | tf_op jit(solution)/shard_map/ppermute | solution.py:432
  80.8 1.3 copy-start.10
  80.8 8.2 %collective-permute-start.13 = (bf16[4,4,64,256]{3,2,1,0:T(8,128)(2,1)S(1)}, bf16[4,4,64,256]{3,2,1,0:T(8,128)(2,1)S(1)}, u32[]{:S(2)}, u32[]{:S(2)}) collective-permute-start(bf16[4,4,64,256]{3,2,1,0:T(8,128)(2,1)S(1)} %collective-permute-done.7.refs_5_), channel_id=1, source_target_pairs={{0,16},{16,0},{1,17},{17,1},{2,18},{18,2},{3,19},{19,3},{4,20},{20... | collective-permute-start | bytes 1572872 | tf_op jit(solution)/shard_map/ppermute | solution.py:432
  82.1 28.5 %all-to-all-start.3 = ((bf16[128,16,128]{2,1,0:T(8,128)(2,1)}), bf16[128,16,128]{2,1,0:T(8,128)(2,1)S(1)}, u32[]{:S(2)}, u32[]{:S(2)}) async-start(bf16[128,16,128]{2,1,0:T(8,128)(2,1)} %shard_map.110), calls=%async_computation.3 | async-start | bytes 1048576 | tf_op jit(solution)/shard_map/all_to_all | solution.py:442
  89.0 0.8 copy-start.11
  89.8 0.8 copy-start.12
  110.6 5.3 %copy-start.7 = (f32[1024,16]{0,1:T(8,128)S(1)}, f32[1024,16]{0,1:T(8,128)}, u32[]{:S(2)}) copy-start(f32[1024,16]{0,1:T(8,128)} %param.11) | copy-start | bytes 196612
  110.6 21.0 %all-to-all-start.4 = ((bf16[8,64,1024]{2,1,0:T(8,128)(2,1)}), bf16[8,64,1024]{2,1,0:T(8,128)(2,1)S(1)}, u32[]{:S(2)}, u32[]{:S(2)}) async-start(bf16[8,64,1024]{2,1,0:T(8,128)(2,1)} %bitcast.22), calls=%async_computation.4 | async-start | bytes 2097152 | tf_op jit(solution)/shard_map/all_to_all | solution.py:444
  115.9 1.6 %copy-start.1 = (bf16[64,16384]{1,0:T(8,128)(2,1)S(1)}, bf16[64,16384]{1,0:T(8,128)(2,1)}, u32[]{:S(2)}) copy-start(bf16[64,16384]{1,0:T(8,128)(2,1)} %x_ref.3) | copy-start | bytes 6291460
